TPU v7x, 128 devices: a whole 4x4x4 slice. The times are simulated.
128 devices in a mesh: dp: 4 (over z_lo, core), ctx: 32 (over z_hi, y, x).
Axes of the slice: x: 4, y: 4, z: 4 (z_hi: 2, z_lo: 2; z = z_hi * 2 + z_lo), core: 2. Of those that a mesh axis runs over, the one named last changes fastest.
Arguments:
- quant_input: bfloat16 [4, 4096, 2048], P('dp', 'ctx'), may hold values from -6 to 6
- input_scales: float32 [4, 4096, 16], P('dp', 'ctx'), may hold values from 0.5 to 2
- out_grad: bfloat16 [4, 4096, 2048], P('dp', 'ctx'), may hold values from -6 to 6
- filter_taps: bfloat16 [2048, 4096], P(None, 'ctx'), may hold values from -1 to 1
- skip: float32 [2048], replicated, may hold values from -1 to 1
- proj_weight: bfloat16 [2048, 2048], P(('dp', 'ctx')), may hold values from -0.125 to 0.125
Outputs:
- grad_input: bfloat16 [4, 4096, 2048], P('dp', 'ctx')
- grad_filter: float32 [2048, 4096], P('ctx', 'dp')
- grad_proj: float32 [2048, 2048], P(('dp', 'ctx'))
All inputs are finite; a program needn't handle non-finite values.
Results may differ from a plain program's by a relative error of at most 0.018.
Values may be sent and summed in bfloat16 or wider, within the bound.
No kernel may reach another device: no remote copies, remote signals or barrier semaphores. Data moves between devices by JAX's collectives and lax.ppermute only.
A program may use at most 128 MiB of HBM per device.

v0:
```python
import math

import jax
import jax.numpy as jnp
from jax import lax
from jax.sharding import PartitionSpec as P

RADIX = 256


precise = lax.Precision.HIGH


def phase(rows, cols, modulus):
    left = jnp.arange(rows, dtype=jnp.int32)[:, None]
    right = jnp.arange(cols, dtype=jnp.int32)[None, :]
    angle = (left * right % modulus).astype(jnp.float32) * (2.0 * math.pi / modulus)
    return (jnp.cos(angle), jnp.sin(angle))


def make_tables(half):
    total = 2 * half
    inner = total // RADIX
    return (phase(RADIX, RADIX // 2, RADIX), phase(RADIX, inner, total), phase(inner, inner, inner))


def forward(field, tables):
    (cos_a, sin_a), (cos_t, sin_t), (cos_b, sin_b) = tables
    chans, half = field.shape
    inner = cos_b.shape[0]
    grid = field.reshape(chans, RADIX // 2, inner)
    part_re = jnp.einsum("kn,cnm->ckm", cos_a, grid, precision=precise)
    part_im = -jnp.einsum("kn,cnm->ckm", sin_a, grid, precision=precise)
    turn_re = part_re * cos_t + part_im * sin_t
    turn_im = part_im * cos_t - part_re * sin_t
    spec_re = jnp.einsum("ckn,nm->ckm", turn_re, cos_b, precision=precise) + jnp.einsum(
        "ckn,nm->ckm", turn_im, sin_b, precision=precise
    )
    spec_im = jnp.einsum("ckn,nm->ckm", turn_im, cos_b, precision=precise) - jnp.einsum(
        "ckn,nm->ckm", turn_re, sin_b, precision=precise
    )
    return (spec_re, spec_im)


def inverse(spec, tables):
    (cos_a, sin_a), (cos_t, sin_t), (cos_b, sin_b) = tables
    spec_re, spec_im = spec
    chans = spec_re.shape[0]
    inner = cos_b.shape[0]
    total = RADIX * inner
    mid_re = jnp.einsum("ckm,nm->ckn", spec_re, cos_b, precision=precise) - jnp.einsum(
        "ckm,nm->ckn", spec_im, sin_b, precision=precise
    )
    mid_im = jnp.einsum("ckm,nm->ckn", spec_im, cos_b, precision=precise) + jnp.einsum(
        "ckm,nm->ckn", spec_re, sin_b, precision=precise
    )
    turn_re = mid_re * cos_t - mid_im * sin_t
    turn_im = mid_im * cos_t + mid_re * sin_t
    field = jnp.einsum("kn,ckm->cnm", cos_a, turn_re, precision=precise) - jnp.einsum(
        "kn,ckm->cnm", sin_a, turn_im, precision=precise
    )
    return (field / total).reshape(chans, total // 2)


def product(first, second):
    return (
        first[0] * second[0] - first[1] * second[1],
        first[0] * second[1] + first[1] * second[0],
    )


def conj_product(first, second):
    return (
        first[0] * second[0] + first[1] * second[1],
        first[0] * second[1] - first[1] * second[0],
    )


def on_device(quant_input, input_scales, out_grad, filter_taps, skip, proj_weight):
    tokens = quant_input.shape[1]
    width = quant_input.shape[2]
    ctx_count = lax.axis_size("ctx")
    dp_count = lax.axis_size("dp")
    blocks = input_scales.shape[2]
    values = quant_input[0]
    cotangent = out_grad[0]
    signal = (
        (values.reshape(tokens, blocks, width // blocks) * input_scales[0][:, :, None])
        .reshape(tokens, width)
        .astype(jnp.bfloat16)
    )
    signal_t = signal.T
    dconv_t = lax.dot_general(
        lax.all_gather(proj_weight, ("dp", "ctx"), axis=0, tiled=True),
        cotangent,
        (((1,), (1,)), ((), ())),
        preferred_element_type=jnp.float32,
    ).astype(jnp.bfloat16)
    signal_c, taps_c, dconv_c = (
        lax.all_to_all(signal_t, "ctx", split_axis=0, concat_axis=1, tiled=True),
        lax.all_to_all(filter_taps, "ctx", split_axis=0, concat_axis=1, tiled=True),
        lax.all_to_all(dconv_t, "ctx", split_axis=0, concat_axis=1, tiled=True),
    )
    chans = width // ctx_count
    length = tokens * ctx_count
    own_skip = lax.dynamic_slice_in_dim(skip, lax.axis_index("ctx") * chans, chans)[:, None]
    tables = make_tables(length)
    signal_f = signal_c.astype(jnp.float32)
    dconv_f = dconv_c.astype(jnp.float32)
    signal_spec = forward(signal_f, tables)
    taps_spec = forward(taps_c.astype(jnp.float32), tables)
    dconv_spec = forward(dconv_f, tables)
    conv_c = (inverse(product(taps_spec, signal_spec), tables) + own_skip * signal_f).astype(
        jnp.bfloat16
    )
    grad_c = (inverse(conj_product(taps_spec, dconv_spec), tables) + own_skip * dconv_f).astype(
        jnp.bfloat16
    )
    taps_grad = inverse(conj_product(signal_spec, dconv_spec), tables)
    conv_t, grad_t = (
        lax.all_to_all(conv_c, "ctx", split_axis=1, concat_axis=0, tiled=True),
        lax.all_to_all(grad_c, "ctx", split_axis=1, concat_axis=0, tiled=True),
    )
    factor = 1.0 / math.sqrt(dp_count * length)
    grad_filter = (
        lax.psum_scatter(
            taps_grad.astype(jnp.bfloat16), "dp", scatter_dimension=1, tiled=True
        ).astype(jnp.float32)
        * factor
    )
    grad_proj = (
        lax.psum_scatter(
            jnp.dot(conv_t, cotangent, preferred_element_type=jnp.float32),
            ("dp", "ctx"),
            scatter_dimension=0,
            tiled=True,
        )
        * factor
    )
    return (grad_t.T[None], grad_filter, grad_proj)


def solution(mesh):
    placed = (
        P("dp", "ctx", None),
        P("dp", "ctx", None),
        P("dp", "ctx", None),
        P(None, "ctx"),
        P(),
        P(("dp", "ctx"), None),
    )
    return jax.shard_map(
        on_device,
        mesh=mesh,
        in_specs=placed,
        out_specs=(P("dp", "ctx", None), P("ctx", "dp"), P(("dp", "ctx"), None)),
        check_vma=False,
    )
```

profile of v0, /device:TPU:64, one launch (start us, length us, event | category | flops | bytes accessed | tf_op | source)
XLA Modules:
  0.0 1209.2 jit_solution(4388474278924310157)
XLA Ops:
  7.9 10.1 all-to-all-start
  18.0 1.3 copy.113
  20.2 8.6 all-to-all-done
  28.8 6.6 all-to-all-start.3
  36.8 1.9 copy.94
  38.8 6.6 all-to-all-done.3
  46.9 1.5 copy.115
  48.5 1.2 fusion.107
  50.9 1.2 fusion.112
  52.1 1.3 add_bitcast_fusion
  53.5 2.2 fusion.32
  55.7 4.0 fusion.38
  59.7 1.3 fusion.96
  61.0 2.6 fusion.100
  63.6 2.9 convolution_subtract_fusion.2
  66.5 259.7 %all-gather.2.cloned.1.call-done = bf16[2048,2048]{1,0:T(8,128)(2,1)} async-done(((bf16[16,2048]{1,0:T(8,128)(2,1)}), bf16[2048,2048]{1,0:T(8,128)(2,1)}) %all-gather.2.cloned.1.call-update) | async-done | bytes 8388624 | tf_op jit(solution)/shard_map/all_gather | solution.py:94
  326.2 6.5 convolution_convert_fusion
  332.7 10.2 all-to-all-start.1
  342.9 5.2 fusion.30
  348.2 2.8 convolution_add_fusion.2
  351.0 3.5 all-to-all-done.1
  355.0 1.5 copy.101
  356.5 1.2 fusion.110
  357.8 1.2 fusion.119
  359.0 1.2 fusion.90
  360.2 1.2 fusion.94
  361.5 1.4 convolution_subtract_fusion.4
  362.9 1.6 convolution_add_fusion.4
  366.3 5.4 multiply_add_fusion
  376.0 1.5 fusion.6
  377.5 2.5 fusion.56
  380.0 4.1 copy.122
  388.4 2.7 convolution_add_fusion.1
  395.9 1.6 fusion.22
  397.5 2.6 fusion.65
  400.0 4.1 copy.111
  404.1 5.1 fusion
  409.2 2.3 copy.123
  411.6 6.4 all-to-all-start.4
  418.3 3.3 fusion.14
  421.6 2.4 fusion.71
  424.0 3.7 copy.121
  427.8 1.5 all-to-all-done.4
  429.3 8.1 fusion.87
  437.4 1.2 copy-done.20
  439.0 18.9 %all_to_all.80 = bf16[64,32,128]{2,0,1:T(8,128)(2,1)S(1)} all-to-all(bf16[64,32,128]{2,0,1:T(8,128)(2,1)S(1)} %copy.112), channel_id=1, replica_groups=mesh['dp'=4,'ctx'=32] {'ctx'}, dimensions={1} | all-to-all | bytes 1048576 | tf_op jit(solution)/shard_map/all_to_all | solution.py:122
  460.8 739.9 %reduce-scatter.5.cloned.1.call-done = f32[16,2048]{1,0:T(8,128)} async-done(((f32[2048,2048]{1,0:T(8,128)}), f32[16,2048]{1,0:T(8,128)}) %reduce-scatter.5.cloned.1.call-update) | async-done | bytes 131088 | tf_op jit(solution)/shard_map/reduce_scatter | solution.py:132
  1200.6 1.6 broadcast_multiply_fusion
  (72 shorter events, 24.9 us)
Async XLA Ops:
  7.2 319.0 %copy-start = (bf16[1,128,2048]{2,1,0:T(8,128)(2,1)S(1)}, bf16[1,128,2048]{2,1,0:T(8,128)(2,1)}, u32[]{:S(2)}) copy-start(bf16[1,128,2048]{2,1,0:T(8,128)(2,1)} %param.8) | copy-start | bytes 1572868
  7.2 12.1 %copy-start.21 = (f32[1,128,16]{1,2,0:T(8,128)S(1)}, f32[1,128,16]{1,2,0:T(8,128)}, u32[]{:S(2)}) copy-start(f32[1,128,16]{1,2,0:T(8,128)} %param.7) | copy-start | bytes 24580
  7.2 319.0 %all-gather.2.cloned.1.call-start = ((), (), s32[]{:S(2)}) async-start(), calls=%async_computation.7 | async-start | bytes 8454144 | tf_op jit(solution)/shard_map/all_gather | solution.py:94
  7.9 20.9 %all-to-all-start = ((bf16[32,64,128]{2,1,0:T(8,128)(2,1)}), bf16[32,64,128]{2,1,0:T(8,128)(2,1)S(1)}, u32[]{:S(2)}, u32[]{:S(2)}) async-start(bf16[32,64,128]{2,1,0:T(8,128)(2,1)} %bitcast.221), calls=%async_computation | async-start | bytes 1048576 | tf_op jit(solution)/shard_map/all_to_all | solution.py:101
  28.8 16.6 %all-to-all-start.3 = ((bf16[32,64,128]{2,1,0:T(8,128)(2,1)}), bf16[32,64,128]{2,1,0:T(8,128)(2,1)S(1)}, u32[]{:S(2)}, u32[]{:S(2)}) async-start(bf16[32,64,128]{2,1,0:T(8,128)(2,1)} %bitcast.34), calls=%async_computation.3 | async-start | bytes 1048576 | tf_op jit(solution)/shard_map/all_to_all | solution.py:100
  45.9 1.0 copy-start.12
  48.5 2.4 copy-start.19
  50.9 12.7 %copy-start.1 = (f32[64,32,256]{2,1,0:T(8,128)}, f32[64,32,256]{2,1,0:T(8,128)S(1)}, u32[]{:S(2)}) copy-start(f32[64,32,256]{2,1,0:T(8,128)S(1)} %fusion.116) | copy-start | bytes 6291460
  53.5 2.2 copy-start.3
  53.5 2.2 copy-start.5
  332.7 21.8 %all-to-all-start.1 = ((bf16[32,64,128]{2,1,0:T(8,128)(2,1)}), bf16[32,64,128]{2,1,0:T(8,128)(2,1)S(1)}, u32[]{:S(2)}, u32[]{:S(2)}) async-start(bf16[32,64,128]{2,1,0:T(8,128)(2,1)} %bitcast.222), calls=%async_computation.1 | async-start | bytes 1048576 | tf_op jit(solution)/shard_map/all_to_all | solution.py:102
  342.9 5.2 copy-start.2
  342.9 5.2 copy-start.14
  355.0 2.8 copy-start.13
  361.5 3.1 copy-start.18
  362.9 1.7 copy-start.6
  362.9 2.3 copy-start.15
  362.9 2.8 copy-start.16
  362.9 3.4 copy-start.17
  371.7 12.4 %copy-start.9 = (f32[64,256,32]{1,2,0:T(8,128)}, f32[64,256,32]{1,2,0:T(8,128)S(1)}, u32[]{:S(2)}) copy-start(f32[64,256,32]{1,2,0:T(8,128)S(1)} %get-tuple-element.20) | copy-start | bytes 6291460
  384.1 1.6 copy-start.11
  386.8 1.6 copy-start.10
  388.4 2.7 copy-start.7
  391.0 1.6 copy-start.8
  411.6 17.7 %all-to-all-start.4 = ((bf16[64,32,128]{2,0,1:T(8,128)(2,1)}), bf16[64,32,128]{2,0,1:T(8,128)(2,1)S(1)}, u32[]{:S(2)}, u32[]{:S(2)}) async-start(bf16[64,32,128]{2,0,1:T(8,128)(2,1)} %copy.123), calls=%async_computation.5 | async-start | bytes 1048576 | tf_op jit(solution)/shard_map/all_to_all | solution.py:121
  418.0 40.9 %reduce-scatter.3.cloned.1.call-start = ((), (), s32[]{:S(2)}) async-start(), calls=%async_computation.8 | async-start | bytes 1310720 | tf_op jit(solution)/shard_map/reduce_scatter | solution.py:126
  418.3 3.3 copy-start.4
  427.8 772.9 %reduce-scatter.5.cloned.1.call-start = ((), (), s32[]{:S(2)}) async-start(), calls=%async_computation.9 | async-start | bytes 16908288 | tf_op jit(solution)/shard_map/reduce_scatter | solution.py:132
  437.4 1.3 copy-start.20
Sparse Core Ops, SparseCore 0:
  9.7 316.4 all-gather.1
  427.9 22.2 reduce-scatter.2
  452.7 747.9 reduce-scatter.4
where the time goes:
time: 1220 us; the launch traced here: 1210 us
  waiting for transfers between devices  1020 us (84%)
  matrix products  82.1 us (7%)
  starting transfers between devices  33.7 us (3%)
  local copies, waits for them, and re-layouts  30.7 us (3%)
  blocking collectives  18.9 us (2%)
  between operations  14.7 us (1%)
    reduce_scatter x1, waiting for transfers between devices, on_device(): lax.psum_scatter(jnp.dot(conv_t, cotangent, preferred_element_type=jnp.fl...  740 us
    all_gather x1, waiting for transfers between devices, on_device(): lax.all_gather(proj_weight, ('dp', 'ctx'), axis=0, tiled=True)  260 us
  transfers between devices with their start and end apart: 7, of which 6 were waited for; matrix products, arithmetic and copies ran while one was open for 4% of the time, Pallas kernels for 0%

commit v1 on v0

v1 whole, which is shorter than its diff:
```python
import functools, math
import jax, jax.numpy as jnp
from jax import lax
from jax.experimental import pallas as pl
from jax.experimental.pallas import tpu as pltpu

LANES = 128
GROUP = 4


def wide(taps, store):
    blocks = taps.shape[0]
    rows = lax.broadcasted_iota(jnp.int32, (LANES, LANES), 0)
    cols = lax.broadcasted_iota(jnp.int32, (LANES, LANES), 1)
    same = cols >= rows
    before = jnp.zeros((LANES, LANES), jnp.float32)
    for delta in range(blocks):
        line = jnp.broadcast_to(taps[delta : delta + 1, :], (LANES, LANES))
        turned = pltpu.roll(line, 0, 1, stride=1, stride_axis=0)
        store(delta, jnp.where(same, turned, before).astype(jnp.bfloat16))
        before = turned


def later(field, seqs):
    parts = [field]
    for step in range(1, GROUP):
        gap = jnp.zeros((step * seqs, LANES), field.dtype)
        parts.append(jnp.concatenate([gap, field[: field.shape[0] - step * seqs]], axis=0))
    return jnp.concatenate([p.astype(jnp.bfloat16) for p in parts], axis=1)


def earlier(field, seqs):
    parts = [field]
    for step in range(1, GROUP):
        gap = jnp.zeros((step * seqs, LANES), field.dtype)
        parts.append(jnp.concatenate([field[step * seqs :], gap], axis=0))
    return jnp.concatenate([p.astype(jnp.bfloat16) for p in parts], axis=1)


def conv_kernel(seqs, x_ref, h_ref, skip_ref, y_ref, m_ref, acc_ref):
    ch = pl.program_id(0)
    x = x_ref[0].astype(jnp.float32)
    rows = x.shape[0]
    def put(delta, m):
        m_ref[delta * LANES : (delta + 1) * LANES, :] = m
    wide(h_ref[0].astype(jnp.float32), put)
    moved = later(x, seqs)
    acc_ref[...] = x * skip_ref[ch]
    span = GROUP * seqs
    for k in range(rows // span):
        acc_ref[k * span :, :] += jnp.dot(
            moved[: rows - k * span], m_ref[k * GROUP * LANES : (k + 1) * GROUP * LANES, :],
            preferred_element_type=jnp.float32)
    y_ref[0] = acc_ref[...].astype(jnp.bfloat16)


def grad_kernel(seqs, scale, x_ref, d_ref, h_ref, skip_ref, gi_ref, gf_ref, m_ref, acc_ref):
    ch = pl.program_id(0)
    x = x_ref[0].astype(jnp.float32)
    dval = d_ref[0]
    d = dval.astype(jnp.float32)
    rows = x.shape[0]
    span = GROUP * seqs
    steps = rows // span
    def put(delta, m):
        m_ref[:, delta * LANES : (delta + 1) * LANES] = m
    wide(h_ref[0].astype(jnp.float32), put)
    dmoved = earlier(d, seqs)
    acc_ref[...] = d * skip_ref[ch]
    for k in range(steps):
        acc_ref[: rows - k * span, :] += lax.dot_general(
            dmoved[k * span :], m_ref[:, k * GROUP * LANES : (k + 1) * GROUP * LANES],
            (((1,), (1,)), ((), ())), preferred_element_type=jnp.float32)
    gi_ref[0] = acc_ref[...].astype(jnp.bfloat16)
    ri = lax.broadcasted_iota(jnp.int32, (LANES, LANES), 0)
    ci = lax.broadcasted_iota(jnp.int32, (LANES, LANES), 1)
    flip = (ri + ci == LANES - 1).astype(jnp.bfloat16)
    xmoved = later(jnp.dot(x_ref[0], flip, preferred_element_type=jnp.float32), seqs)
    same = ri + ci >= LANES - 1
    after = jnp.zeros((LANES, LANES), jnp.float32)
    for k in reversed(range(steps)):
        g = lax.dot_general(xmoved[: rows - k * span], dval[k * span :],
            (((0,), (0,)), ((), ())), preferred_element_type=jnp.float32)
        for v in reversed(range(GROUP)):
            here = g[v * LANES : (v + 1) * LANES]
            mixed = jnp.where(same, here, after)
            turned = pltpu.roll(mixed, 1, 1, stride=1, stride_axis=0)
            delta = k * GROUP + v
            gf_ref[0, delta : delta + 1, :] = jnp.sum(turned, axis=0, keepdims=True) * scale
            after = here


def conv_call(x, h, skip, seqs):
    chans, rows, _ = x.shape
    blocks = h.shape[1]
    return pl.pallas_call(
        functools.partial(conv_kernel, seqs), grid=(chans,),
        in_specs=[pl.BlockSpec((1, rows, LANES), lambda i: (i, 0, 0)),
                  pl.BlockSpec((1, blocks, LANES), lambda i: (i, 0, 0)),
                  pl.BlockSpec(memory_space=pltpu.SMEM)],
        out_specs=pl.BlockSpec((1, rows, LANES), lambda i: (i, 0, 0)),
        out_shape=jax.ShapeDtypeStruct(x.shape, jnp.bfloat16),
        scratch_shapes=[pltpu.VMEM((blocks * LANES, LANES), jnp.bfloat16), pltpu.VMEM((rows, LANES), jnp.float32)],
        compiler_params=pltpu.CompilerParams(vmem_limit_bytes=32 << 20),
    )(x, h, skip)


def grad_call(x, d, h, skip, seqs, scale):
    chans, rows, _ = x.shape
    blocks = h.shape[1]
    big = pl.BlockSpec((1, rows, LANES), lambda i: (i, 0, 0))
    small = pl.BlockSpec((1, blocks, LANES), lambda i: (i, 0, 0))
    return pl.pallas_call(
        functools.partial(grad_kernel, seqs, scale), grid=(chans,),
        in_specs=[big, big, small, pl.BlockSpec(memory_space=pltpu.SMEM)],
        out_specs=[big, small],
        out_shape=[jax.ShapeDtypeStruct(x.shape, jnp.bfloat16), jax.ShapeDtypeStruct((chans, blocks, LANES), jnp.float32)],
        scratch_shapes=[pltpu.VMEM((LANES, blocks * LANES), jnp.bfloat16), pltpu.VMEM((rows, LANES), jnp.float32)],
        compiler_params=pltpu.CompilerParams(vmem_limit_bytes=32 << 20),
    )(x, d, h, skip)


from jax.sharding import PartitionSpec as P


def on_device(quant_input, input_scales, out_grad, filter_taps, skip, proj_weight):
    tokens, width = quant_input.shape[1:]
    ctx = lax.axis_size("ctx")
    seqs = lax.axis_size("dp")
    me_dp, me_ctx = lax.axis_index("dp"), lax.axis_index("ctx")
    blocks = input_scales.shape[2]
    chans = width // (ctx * seqs)
    share = tokens // seqs
    bf16 = jnp.bfloat16

    with jax.named_scope("gather_cotangent"):
        cotangent = lax.all_gather(out_grad[0], "dp", axis=0)
    with jax.named_scope("gather_weight"):
        weight = lax.all_gather(proj_weight, "ctx", axis=0, tiled=True)

    with jax.named_scope("signal"):
        signal = (
            (quant_input[0].reshape(tokens, blocks, width // blocks) * input_scales[0][:, :, None])
            .reshape(tokens, width)
            .astype(bf16)
        )
        parts = signal.T.reshape(seqs, ctx, chans, tokens)
        taps = lax.dynamic_slice_in_dim(filter_taps, me_dp * share, share, axis=1)
        taps = taps.reshape(seqs, ctx, chans * share // LANES, LANES)
        load = jnp.concatenate([parts, taps], axis=2).transpose(1, 0, 2, 3)
        load = load.reshape(ctx * seqs, -1, LANES)
    with jax.named_scope("signal_a2a"):
        load = lax.all_to_all(load, ("ctx", "dp"), 0, 0)
    with jax.named_scope("signal_in"):
        x = load[:, :chans].transpose(1, 0, 2)
        h = load[:, chans:].reshape(ctx, seqs, chans, share).transpose(2, 0, 1, 3)
        h = h.reshape(chans, ctx, LANES)
        first = (me_dp * ctx + me_ctx) * chans
        own_skip = lax.dynamic_slice_in_dim(skip, first, chans)
    with jax.named_scope("conv"):
        conv = conv_call(x, h, own_skip, seqs)
        conv = conv.reshape(chans, ctx, seqs, LANES).transpose(1, 0, 2, 3)
    with jax.named_scope("conv_a2a"):
        conv = lax.all_to_all(conv, "ctx", 0, 0)
    with jax.named_scope("dconv"):
        dconv = lax.dot_general(
            weight, cotangent, (((1,), (2,)), ((), ())), preferred_element_type=jnp.float32
        ).astype(bf16)
        dconv = dconv.reshape(ctx, chans, seqs, LANES)
    with jax.named_scope("dconv_a2a"):
        dconv = lax.all_to_all(dconv, "ctx", 0, 0)
        dconv = dconv.transpose(1, 0, 2, 3).reshape(chans, ctx * seqs, LANES)
    factor = 1.0 / math.sqrt(seqs * tokens * ctx)
    with jax.named_scope("grad_proj"):
        partial = lax.dot_general(
            conv.reshape(ctx * chans, seqs, LANES),
            cotangent,
            (((1, 2), (0, 1)), ((), ())),
            preferred_element_type=jnp.float32,
        ).astype(bf16)
    with jax.named_scope("grad_proj_a2a"):
        partial = lax.all_to_all(partial.reshape(ctx, chans, width), "ctx", 0, 0)
        grad_proj = jnp.sum(partial.astype(jnp.float32), axis=0) * factor
    with jax.named_scope("grads"):
        grad_in, grad_taps = grad_call(x, dconv, h, own_skip, seqs, factor)
    with jax.named_scope("grad_in_a2a"):
        grad_in = lax.all_to_all(grad_in.transpose(1, 0, 2), ("ctx", "dp"), 0, 0)
        grad_in = grad_in.reshape(ctx, seqs, chans, LANES).transpose(1, 0, 2, 3)
        grad_in = grad_in.reshape(width, LANES).T
    with jax.named_scope("grad_filter"):
        span = ctx * LANES // seqs
        pieces = grad_taps.astype(bf16).reshape(chans, seqs, span).transpose(1, 0, 2)
        got = []
        for k in range(seqs):
            pairs = [
                (d * ctx + c, (c % seqs + k) % seqs * ctx + (d * ctx + c) // seqs)
                for d in range(seqs)
                for c in range(ctx)
            ]
            piece = lax.dynamic_index_in_dim(pieces, (me_ctx + k) % seqs, 0, keepdims=False)
            got.append(lax.ppermute(piece, ("dp", "ctx"), pairs))
        got = jnp.stack(got)
        grad_filter = jnp.concatenate(
            [
                lax.dynamic_index_in_dim(got, (me_dp - m + seqs) % seqs, 0, keepdims=False)
                for m in range(seqs)
            ],
            axis=0,
        ).astype(jnp.float32)
    return (grad_in[None], grad_filter, grad_proj)


def solution(mesh):
    placed = (
        P("dp", "ctx", None),
        P("dp", "ctx", None),
        P("dp", "ctx", None),
        P(None, "ctx"),
        P(),
        P(("dp", "ctx"), None),
    )
    return jax.shard_map(
        on_device,
        mesh=mesh,
        in_specs=placed,
        out_specs=(P("dp", "ctx", None), P("ctx", "dp"), P(("dp", "ctx"), None)),
        check_vma=False,
    )
```

time: 1220 us -> 264 us (0.22)
  the two profiles are of different devices: /device:TPU:64 before, /device:TPU:1 now
where the time goes in v1:
time: 264 us; the launch traced here: 261 us
  waiting for transfers between devices  126 us (48%)
  starting transfers between devices  59 us (22%)
  Pallas kernels  39.6 us (15%)
  between operations  14.4 us (5%)
  local copies, waits for them, and re-layouts  12.4 us (5%)
  matrix products  7.65 us (3%)
    all_gather x1, waiting for transfers between devices, on_device(): weight = lax.all_gather(proj_weight, 'ctx', axis=0, tiled=True)  75.1 us
    pallas_call x1, Pallas kernels, grad_call(): pl.pallas_call(functools.partial(grad_kernel, seqs, scale), grid=(chans,)...  29 us
    all_gather x1, waiting for transfers between devices, on_device(): cotangent = lax.all_gather(out_grad[0], 'dp', axis=0)  27.8 us
    ppermute x4, starting transfers between devices, on_device(): got.append(lax.ppermute(piece, ('dp', 'ctx'), pairs))  17.2 us
    ppermute x4, waiting for transfers between devices, on_device(): got.append(lax.ppermute(piece, ('dp', 'ctx'), pairs))  13.5 us
    all_to_all x1, starting transfers between devices, on_device(): grad_in = lax.all_to_all(grad_in.transpose(1, 0, 2), ('ctx', 'dp'), 0, 0)  12.3 us
    all_to_all x1, starting transfers between devices, on_device(): load = lax.all_to_all(load, ('ctx', 'dp'), 0, 0)  11.5 us
    pallas_call x1, Pallas kernels, conv_call(): pl.pallas_call(functools.partial(conv_kernel, seqs), grid=(chans,), in_sp...  10.6 us
  transfers between devices with their start and end apart: 11, of which 5 were waited for; matrix products, arithmetic and copies ran while one was open for 8% of the time, Pallas kernels for 15%

profile of v1, /device:TPU:1, one launch (start us, length us, event | category | flops | bytes accessed | tf_op | source)
XLA Modules:
  0.0 261.1 jit_solution(11620244517638510924)
XLA Ops:
  7.2 0.0 copy-start
  7.2 0.0 all-gather.5.cloned.1.call-start
  7.2 0.7 all-gather.5.cloned.1.call-update
  7.9 0.0 all-gather.3.cloned.1.call-start
  8.0 0.7 all-gather.3.cloned.1.call-update
  8.7 0.2 constant_dynamic-slice_fusion.4
  8.9 0.3 reshape.60
  9.2 0.3 copy.39
  9.5 0.1 fusion.5
  9.6 0.2 maximum_bitcast_fusion
  9.8 0.5 copy.40
  10.3 1.3 copy.41
  11.6 11.5 %all-to-all-start = ((bf16[128,20,128]{2,1,0:T(8,128)(2,1)}), bf16[128,20,128]{2,1,0:T(8,128)(2,1)S(1)}, u32[]{:S(2)}, u32[]{:S(2)}) async-start(bf16[128,20,128]{2,1,0:T(8,128)(2,1)} %copy.41), calls=%async_computation | async-start | bytes 1572864 | tf_op jit(solution)/shard_map/signal_a2a/all_to_all | solution.py:153
  23.1 27.8 %all-gather.5.cloned.1.call-done = bf16[4,128,2048]{2,1,0:T(8,128)(2,1)} async-done(((bf16[1,128,2048]{2,1,0:T(8,128)(2,1)}), bf16[4,128,2048]{2,1,0:T(8,128)(2,1)}) %all-gather.5.cloned.1.call-update) | async-done | bytes 2097168 | tf_op jit(solution)/shard_map/gather_cotangent/all_gather | solution.py:137
  50.9 75.1 %all-gather.3.cloned.1.call-done = bf16[512,2048]{1,0:T(8,128)(2,1)} async-done(((bf16[16,2048]{1,0:T(8,128)(2,1)}), bf16[512,2048]{1,0:T(8,128)(2,1)}) %all-gather.3.cloned.1.call-update) | async-done | bytes 2097168 | tf_op jit(solution)/shard_map/gather_weight/all_gather | solution.py:139
  126.0 3.5 %fusion.2 = bf16[512,4,128]{2,0,1:T(8,128)(2,1)S(1)} fusion(bf16[4,128,2048]{2,1,0:T(8,128)(2,1)} %all-gather.5.cloned.1.call-done, bf16[512,2048]{1,0:T(8,128)(2,1)} %all-gather.3.cloned.1.call-done), kind=kOutput, calls=%fused_computation.4 | convolution fusion | flops 1074003968 | bytes 4718592 | tf_op jit(solution)/shard_map/dconv/dot_general | solution.py:166
  129.5 1.2 copy.43
  130.7 0.0 all-to-all-done
  130.7 4.4 %all-to-all-start.1 = ((bf16[32,16,4,128]{3,2,1,0:T(4,128)(2,1)}), bf16[32,16,4,128]{3,2,1,0:T(4,128)(2,1)S(1)}, u32[]{:S(2)}, u32[]{:S(2)}) async-start(bf16[32,16,4,128]{3,2,1,0:T(4,128)(2,1)} %copy.43), calls=%async_computation.1 | async-start | bytes 1048576 | tf_op jit(solution)/shard_map/dconv_a2a/all_to_all | solution.py:171
  135.1 0.8 dynamic_slice.24.skip_ref
  135.9 0.2 reshape.64
  136.1 0.2 copy.45
  136.4 0.3 reshape.65.h_ref
  136.7 0.1 copy.66
  136.9 10.6 %conv.1 = bf16[16,128,128]{2,1,0:T(8,128)(2,1)S(1)} custom-call(bf16[16,128,128]{2,1,0:T(8,128)(2,1)S(1)} %bitcast.68, bf16[16,32,128]{2,1,0:T(8,128)(2,1)S(1)} %reshape.65.h_ref, f32[16]{0:T(128)S(1)} %dynamic_slice.24.skip_ref), custom_call_target="tpu_custom_call" | custom-call | tf_op jit(solution)/shard_map/conv/pallas_call | solution.py:96
  147.5 1.1 copy.67
  148.6 0.0 all-to-all-done.1
  148.6 9.4 %all-to-all-start.3 = ((bf16[32,16,4,128]{3,2,1,0:T(4,128)(2,1)}), bf16[32,16,4,128]{3,2,1,0:T(4,128)(2,1)}, u32[]{:S(2)}, u32[]{:S(2)}) async-start(bf16[32,16,4,128]{3,2,1,0:T(4,128)(2,1)} %bitcast.63), calls=%async_computation.3 | async-start | bytes 1048576 | tf_op jit(solution)/shard_map/conv_a2a/all_to_all | solution.py:164
  158.0 0.2 copy.44
  158.2 29.0 %grads.1 = (bf16[16,128,128]{2,1,0:T(8,128)(2,1)S(1)}, f32[16,32,128]{2,1,0:T(8,128)S(1)}) custom-call(bf16[16,128,128]{2,1,0:T(8,128)(2,1)S(1)} %bitcast.69, bf16[16,128,128]{2,1,0:T(8,128)(2,1)S(1)} %bitcast.70, bf16[16,32,128]{2,1,0:T(8,128)(2,1)S(1)} %reshape.65.h_ref, f32[16]{0:T(128)S(1)} %dynamic_slice.24.skip_ref), custom_call_target="tpu_custom_call" | custom-call | tf_op jit(solution)/shard_map/grads/pallas_call | solution.py:113
  187.2 1.1 copy.46
  188.4 12.3 %all-to-all-start.2 = ((bf16[128,16,128]{2,1,0:T(8,128)(2,1)}), bf16[128,16,128]{2,1,0:T(8,128)(2,1)S(1)}, u32[]{:S(2)}, u32[]{:S(2)}) async-start(bf16[128,16,128]{2,1,0:T(8,128)(2,1)} %copy.46), calls=%async_computation.2 | async-start | bytes 1048576 | tf_op jit(solution)/shard_map/grad_in_a2a/all_to_all | solution.py:187
  200.7 1.1 copy.53
  201.8 4.1 %bitcast_convert_fusion = bf16[512,2048]{1,0:T(8,128)(2,1)} fusion(bf16[512,4,128]{2,0,1:T(8,128)(2,1)S(1)} %bitcast.80, bf16[4,128,2048]{2,1,0:T(8,128)(2,1)} %all-gather.5.cloned.1.call-done), kind=kOutput, calls=%fused_computation | convolution fusion | flops 1074790400 | bytes 4718592 | tf_op jit(solution)/shard_map/grad_proj/dot_general | solution.py:175
  206.0 8.3 %all-to-all-done.2 = bf16[128,16,128]{2,1,0:T(8,128)(2,1)S(1)} async-done(((bf16[128,16,128]{2,1,0:T(8,128)(2,1)}), bf16[128,16,128]{2,1,0:T(8,128)(2,1)S(1)}, u32[]{:S(2)}, u32[]{:S(2)}) %all-to-all-start.2) | async-done | bytes 524320 | tf_op jit(solution)/shard_map/grad_in_a2a/all_to_all | solution.py:187
  214.3 4.1 %all-to-all-start.4 = ((bf16[32,16,2048]{2,1,0:T(8,128)(2,1)}), bf16[32,16,2048]{2,1,0:T(8,128)(2,1)S(1)}, u32[]{:S(2)}, u32[]{:S(2)}) async-start(bf16[32,16,2048]{2,1,0:T(8,128)(2,1)} %bitcast.75), calls=%async_computation.4 | async-start | bytes 4194304 | tf_op jit(solution)/shard_map/grad_proj_a2a/all_to_all | solution.py:182
  218.5 0.3 constant_dynamic-slice_fusion.3
  218.8 6.3 %collective-permute-start = (bf16[16,1024]{1,0:T(8,128)(2,1)S(1)}, bf16[16,1024]{1,0:T(8,128)(2,1)S(1)}, u32[]{:S(2)}, u32[]{:S(2)}) collective-permute-start(bf16[16,1024]{1,0:T(8,128)(2,1)S(1)} %bitcast.82), channel_id=1, source_target_pairs={{0,0},{1,32},{2,64},{3,96},{4,1},{5,33},{6,65},{7,97},{8,2},{9,34}... | collective-permute-start | bytes 98312 | tf_op jit(solution)/shard_map/grad_filter/ppermute | solution.py:201
  225.2 4.6 %collective-permute-start.1 = (bf16[16,1024]{1,0:T(8,128)(2,1)S(1)}, bf16[16,1024]{1,0:T(8,128)(2,1)S(1)}, u32[]{:S(2)}, u32[]{:S(2)}) collective-permute-start(bf16[16,1024]{1,0:T(8,128)(2,1)S(1)} %bitcast.83), channel_id=1, source_target_pairs={{0,32},{1,64},{2,96},{3,0},{4,33},{5,65},{6,97},{7,1},{8,34},{9,66... | collective-permute-start | bytes 98312 | tf_op jit(solution)/shard_map/grad_filter/ppermute | solution.py:201
  229.8 3.1 %collective-permute-start.2 = (bf16[16,1024]{1,0:T(8,128)(2,1)S(1)}, bf16[16,1024]{1,0:T(8,128)(2,1)S(1)}, u32[]{:S(2)}, u32[]{:S(2)}) collective-permute-start(bf16[16,1024]{1,0:T(8,128)(2,1)S(1)} %bitcast.84), channel_id=1, source_target_pairs={{0,64},{1,96},{2,0},{3,32},{4,65},{5,97},{6,1},{7,33},{8,66},{9,98... | collective-permute-start | bytes 98312 | tf_op jit(solution)/shard_map/grad_filter/ppermute | solution.py:201
  232.9 3.2 %collective-permute-start.3 = (bf16[16,1024]{1,0:T(8,128)(2,1)S(1)}, bf16[16,1024]{1,0:T(8,128)(2,1)S(1)}, u32[]{:S(2)}, u32[]{:S(2)}) collective-permute-start(bf16[16,1024]{1,0:T(8,128)(2,1)S(1)} %bitcast.85), channel_id=1, source_target_pairs={{0,96},{1,0},{2,32},{3,64},{4,97},{5,1},{6,33},{7,65},{8,98},{9,2}... | collective-permute-start | bytes 98312 | tf_op jit(solution)/shard_map/grad_filter/ppermute | solution.py:201
  236.2 9.9 %collective-permute-done = bf16[16,1024]{1,0:T(8,128)(2,1)S(1)} collective-permute-done((bf16[16,1024]{1,0:T(8,128)(2,1)S(1)}, bf16[16,1024]{1,0:T(8,128)(2,1)S(1)}, u32[]{:S(2)}, u32[]{:S(2)}) %collective-permute-start) | collective-permute-done | bytes 32800 | tf_op jit(solution)/shard_map/grad_filter/ppermute | solution.py:201
  246.1 3.6 %collective-permute-done.2 = bf16[16,1024]{1,0:T(8,128)(2,1)S(1)} collective-permute-done((bf16[16,1024]{1,0:T(8,128)(2,1)S(1)}, bf16[16,1024]{1,0:T(8,128)(2,1)S(1)}, u32[]{:S(2)}, u32[]{:S(2)}) %collective-permute-start.2) | collective-permute-done | bytes 32800 | tf_op jit(solution)/shard_map/grad_filter/ppermute | solution.py:201
  249.7 0.7 maximum_convert_fusion
  250.4 0.8 copy.47
  251.2 2.0 copy.54
  253.3 0.3 convert_reduce_fusion
  253.6 0.7 broadcast_multiply_fusion
  (19 shorter events, 0.3 us)
Async XLA Ops:
  7.2 1.5 copy-start
  7.2 2.0 copy-start.1
  7.2 2.3 copy-start.2
  7.2 43.7 %all-gather.5.cloned.1.call-start = ((), (), s32[]{:S(2)}) async-start(), calls=%async_computation.6 | async-start | bytes 2621440 | tf_op jit(solution)/shard_map/gather_cotangent/all_gather | solution.py:137
  7.9 118.1 %all-gather.3.cloned.1.call-start = ((), (), s32[]{:S(2)}) async-start(), calls=%async_computation.5 | async-start | bytes 2162688 | tf_op jit(solution)/shard_map/gather_weight/all_gather | solution.py:139
  11.6 119.1 %all-to-all-start = ((bf16[128,20,128]{2,1,0:T(8,128)(2,1)}), bf16[128,20,128]{2,1,0:T(8,128)(2,1)S(1)}, u32[]{:S(2)}, u32[]{:S(2)}) async-start(bf16[128,20,128]{2,1,0:T(8,128)(2,1)} %copy.41), calls=%async_computation | async-start | bytes 1572864 | tf_op jit(solution)/shard_map/signal_a2a/all_to_all | solution.py:153
  130.7 17.9 %all-to-all-start.1 = ((bf16[32,16,4,128]{3,2,1,0:T(4,128)(2,1)}), bf16[32,16,4,128]{3,2,1,0:T(4,128)(2,1)S(1)}, u32[]{:S(2)}, u32[]{:S(2)}) async-start(bf16[32,16,4,128]{3,2,1,0:T(4,128)(2,1)} %copy.43), calls=%async_computation.1 | async-start | bytes 1048576 | tf_op jit(solution)/shard_map/dconv_a2a/all_to_all | solution.py:171
  148.6 39.8 %all-to-all-start.3 = ((bf16[32,16,4,128]{3,2,1,0:T(4,128)(2,1)}), bf16[32,16,4,128]{3,2,1,0:T(4,128)(2,1)}, u32[]{:S(2)}, u32[]{:S(2)}) async-start(bf16[32,16,4,128]{3,2,1,0:T(4,128)(2,1)} %bitcast.63), calls=%async_computation.3 | async-start | bytes 1048576 | tf_op jit(solution)/shard_map/conv_a2a/all_to_all | solution.py:164
  188.4 25.9 %all-to-all-start.2 = ((bf16[128,16,128]{2,1,0:T(8,128)(2,1)}), bf16[128,16,128]{2,1,0:T(8,128)(2,1)S(1)}, u32[]{:S(2)}, u32[]{:S(2)}) async-start(bf16[128,16,128]{2,1,0:T(8,128)(2,1)} %copy.46), calls=%async_computation.2 | async-start | bytes 1048576 | tf_op jit(solution)/shard_map/grad_in_a2a/all_to_all | solution.py:187
  214.3 39.0 %all-to-all-start.4 = ((bf16[32,16,2048]{2,1,0:T(8,128)(2,1)}), bf16[32,16,2048]{2,1,0:T(8,128)(2,1)S(1)}, u32[]{:S(2)}, u32[]{:S(2)}) async-start(bf16[32,16,2048]{2,1,0:T(8,128)(2,1)} %bitcast.75), calls=%async_computation.4 | async-start | bytes 4194304 | tf_op jit(solution)/shard_map/grad_proj_a2a/all_to_all | solution.py:182
  218.8 27.2 %collective-permute-start = (bf16[16,1024]{1,0:T(8,128)(2,1)S(1)}, bf16[16,1024]{1,0:T(8,128)(2,1)S(1)}, u32[]{:S(2)}, u32[]{:S(2)}) collective-permute-start(bf16[16,1024]{1,0:T(8,128)(2,1)S(1)} %bitcast.82), channel_id=1, source_target_pairs={{0,0},{1,32},{2,64},{3,96},{4,1},{5,33},{6,65},{7,97},{8,2},{9,34}... | collective-permute-start | bytes 98312 | tf_op jit(solution)/shard_map/grad_filter/ppermute | solution.py:201
  225.2 20.9 %collective-permute-start.1 = (bf16[16,1024]{1,0:T(8,128)(2,1)S(1)}, bf16[16,1024]{1,0:T(8,128)(2,1)S(1)}, u32[]{:S(2)}, u32[]{:S(2)}) collective-permute-start(bf16[16,1024]{1,0:T(8,128)(2,1)S(1)} %bitcast.83), channel_id=1, source_target_pairs={{0,32},{1,64},{2,96},{3,0},{4,33},{5,65},{6,97},{7,1},{8,34},{9,66... | collective-permute-start | bytes 98312 | tf_op jit(solution)/shard_map/grad_filter/ppermute | solution.py:201
  229.8 19.8 %collective-permute-start.2 = (bf16[16,1024]{1,0:T(8,128)(2,1)S(1)}, bf16[16,1024]{1,0:T(8,128)(2,1)S(1)}, u32[]{:S(2)}, u32[]{:S(2)}) collective-permute-start(bf16[16,1024]{1,0:T(8,128)(2,1)S(1)} %bitcast.84), channel_id=1, source_target_pairs={{0,64},{1,96},{2,0},{3,32},{4,65},{5,97},{6,1},{7,33},{8,66},{9,98... | collective-permute-start | bytes 98312 | tf_op jit(solution)/shard_map/grad_filter/ppermute | solution.py:201
  232.9 16.7 %collective-permute-start.3 = (bf16[16,1024]{1,0:T(8,128)(2,1)S(1)}, bf16[16,1024]{1,0:T(8,128)(2,1)S(1)}, u32[]{:S(2)}, u32[]{:S(2)}) collective-permute-start(bf16[16,1024]{1,0:T(8,128)(2,1)S(1)} %bitcast.85), channel_id=1, source_target_pairs={{0,96},{1,0},{2,32},{3,64},{4,97},{5,1},{6,33},{7,65},{8,98},{9,2}... | collective-permute-start | bytes 98312 | tf_op jit(solution)/shard_map/grad_filter/ppermute | solution.py:201
Sparse Core Ops, SparseCore 0:
  9.7 41.1 all-gather.4
  54.0 71.9 all-gather.2

commit v2 on v1

v2 whole, which is shorter than its diff:
```python
import functools
import math

import jax
import jax.numpy as jnp
from jax import lax
from jax.experimental import pallas as pl
from jax.experimental.pallas import tpu as pltpu
from jax.sharding import Mesh, PartitionSpec as P

LANES = 128
HALF = LANES // 2
GROUP = 4
f32, bf16 = jnp.float32, jnp.bfloat16


def iota(rows, axis):
    return lax.broadcasted_iota(jnp.int32, (rows, LANES), axis)


def turn(field, by):
    return pltpu.roll(field, by, 1)


def moved(field, by):
    if by == 0:
        return field
    gap = jnp.zeros((abs(by), LANES), field.dtype)
    if by > 0:
        return jnp.concatenate([gap, field[:-by]], axis=0)
    return jnp.concatenate([field[-by:], gap], axis=0)


def mirror():
    return (iota(LANES, 0) + iota(LANES, 1) == LANES - 1).astype(bf16)


def tap_rows(taps, first, before):
    same = iota(HALF, 1) >= iota(HALF, 0)
    parts = []
    for delta in range(first, first + GROUP):
        line = jnp.broadcast_to(taps[delta : delta + 1, :], (HALF, LANES))
        here = pltpu.roll(line, 0, 1, stride=1, stride_axis=0)
        parts.append(jnp.where(same, here, before).astype(bf16))
        before = here
    return jnp.concatenate(parts, axis=0), before


def correlate(field, taps, seqs, sign):
    rows, span = field.shape[0], GROUP * seqs
    low = iota(rows, 1) < HALF
    beside = moved(field, sign * seqs)
    halves = [
        jnp.where(low, field, turn(beside, HALF)),
        jnp.where(low, turn(field, HALF), beside),
    ]
    wide = [
        jnp.concatenate([h.astype(bf16), moved(h, sign * 2 * seqs).astype(bf16)], axis=1)
        for h in halves
    ]
    total = [jnp.zeros((rows, LANES), f32)] * 2
    before = jnp.zeros((HALF, LANES), f32)
    for k in range(rows // span):
        matrix, before = tap_rows(taps, k * GROUP, before)
        cut = k * span
        kept = [w[: rows - cut] if sign > 0 else w[cut:] for w in wide]
        part = jnp.dot(jnp.concatenate(kept, axis=0), matrix, preferred_element_type=f32)
        for p in range(2):
            add = part[p * (rows - cut) : (p + 1) * (rows - cut)]
            if cut:
                gap = jnp.zeros((cut, LANES), f32)
                add = jnp.concatenate([gap, add] if sign > 0 else [add, gap], axis=0)
            total[p] = total[p] + add
    across = turn(total[1], HALF)
    return total[0] + jnp.where(low, moved(across, sign * seqs), across)


def conv_kernel(seqs, skip_ref, x_ref, h_ref, y_ref):
    x = x_ref[0].astype(f32)
    y = correlate(x, h_ref[0].astype(f32), seqs, 1)
    y_ref[0] = (y + x * skip_ref[pl.program_id(0)]).astype(bf16)


def back_kernel(seqs, skip_ref, d_ref, h_ref, y_ref):
    flip = mirror()
    d = jnp.dot(d_ref[0], flip, preferred_element_type=f32)
    y = correlate(d, h_ref[0].astype(f32), seqs, -1)
    y = (y + d * skip_ref[pl.program_id(0)]).astype(bf16)
    y_ref[0] = jnp.dot(y, flip, preferred_element_type=f32).astype(bf16)


def taps_kernel(seqs, scale, x_ref, d_ref, f_ref, long_ref):
    x, d = x_ref[0].astype(f32), d_ref[0].astype(f32)
    rows, span = x.shape[0], GROUP * seqs
    flip = mirror()
    left = []
    for v in range(GROUP):
        part = moved(x, v * seqs).astype(bf16)
        part = lax.dot_general(flip, part, (((1,), (1,)), ((), ())), preferred_element_type=f32)
        part = part.astype(bf16)
        left.append(jnp.concatenate([part[HALF:], part[:HALF]], axis=1))
    left = jnp.concatenate(left, axis=0)
    across = turn(d, HALF)
    shifted = jnp.where(iota(rows, 1) < HALF, across, moved(across, -seqs))
    for p, part in enumerate((d, shifted)):
        long_ref[p, :rows, :] = part.astype(bf16)
        long_ref[p, rows:, :] = jnp.zeros((rows, LANES), bf16)
    same = iota(HALF, 0) + iota(HALF, 1) >= HALF - 1
    after = jnp.zeros((HALF, LANES), f32)

    def outer(k):
        right = [
            jnp.concatenate(
                [long_ref[p, at * span : at * span + rows, :] for p in range(2)], axis=0
            )
            for at in (k, k + 1)
        ]
        return jnp.dot(left, jnp.concatenate(right, axis=1), preferred_element_type=f32)

    steps = list(reversed(range(0, rows // span, 2)))
    ready = outer(steps[0])
    for i, k in enumerate(steps):
        now = ready
        if i + 1 < len(steps):
            ready = outer(steps[i + 1])
        for j in reversed(range(2 * GROUP)):
            at, v = j // GROUP, j % GROUP
            here = now[v * HALF : (v + 1) * HALF, at * LANES : (at + 1) * LANES]
            lined = pltpu.roll(
                jnp.where(same, here, after), HALF + 1, 1, stride=1, stride_axis=0
            )
            delta = k * GROUP + j
            f_ref[0, delta : delta + 1, :] = jnp.sum(lined, axis=0, keepdims=True) * scale
            after = here


def per_channel(shape):
    return pl.BlockSpec((1, *shape[1:]), lambda i: (i, 0, 0))


def estimate(flops):
    return pl.CostEstimate(flops=flops, bytes_accessed=1 << 20, transcendentals=0)


def conv_call(kernel, field, taps, skip, seqs):
    chans, rows = taps.shape[0], field.shape[1]
    return pl.pallas_call(
        functools.partial(kernel, seqs),
        grid=(chans,),
        in_specs=[
            pl.BlockSpec(memory_space=pltpu.SMEM),
            per_channel(field.shape),
            per_channel(taps.shape),
        ],
        out_specs=per_channel(field.shape),
        out_shape=jax.ShapeDtypeStruct((chans, rows, LANES), bf16),
        compiler_params=pltpu.CompilerParams(vmem_limit_bytes=24 << 20),
        cost_estimate=estimate(5 << 30),
    )(skip, field, taps)


def taps_call(x, d, seqs, scale):
    chans, rows, _ = d.shape
    out = jax.ShapeDtypeStruct((chans, rows // seqs, LANES), f32)
    return pl.pallas_call(
        functools.partial(taps_kernel, seqs, scale),
        grid=(chans,),
        in_specs=[per_channel(x.shape)] * 2,
        out_specs=per_channel(out.shape),
        out_shape=out,
        scratch_shapes=[pltpu.VMEM((2, 2 * rows, LANES), bf16)],
        compiler_params=pltpu.CompilerParams(vmem_limit_bytes=24 << 20),
        cost_estimate=estimate(8 << 30),
    )(x, d)


def dconv_kernel(place_ref, w_ref, *refs):
    *pieces, out_ref = refs
    weight = w_ref[...]
    for j, piece in enumerate(pieces):
        part = lax.dot_general(
            weight, piece[...], (((1,), (1,)), ((), ())), preferred_element_type=jnp.float32
        )
        out_ref[:, pl.ds(place_ref[j], 1)] = (
            part.astype(jnp.bfloat16).reshape(out_ref.shape[0], 1, *out_ref.shape[2:])
        )


def proj_kernel(place_ref, c_ref, *refs):
    *pieces, out_ref, lhs_ref = refs
    rows, width = out_ref.shape
    for j in range(len(pieces)):
        part = c_ref[:, pl.ds(place_ref[j], 1)]
        lhs_ref[:, j * LANES : (j + 1) * LANES] = part.reshape(rows, LANES)
    step = 512
    for at in range(0, width, step):
        total = jnp.zeros((rows, step), jnp.float32)
        for j, piece in enumerate(pieces):
            total += jnp.dot(
                lhs_ref[:, j * LANES : (j + 1) * LANES],
                piece[:, at : at + step],
                preferred_element_type=jnp.float32,
            )
        out_ref[:, at : at + step] = total.astype(jnp.bfloat16)


def whole(count):
    return [pl.BlockSpec(memory_space=pltpu.VMEM)] * count


def dconv_call(place, weight, pieces, plane):
    rows = weight.shape[0]
    return pl.pallas_call(
        dconv_kernel,
        in_specs=[pl.BlockSpec(memory_space=pltpu.SMEM), *whole(1 + len(pieces))],
        out_specs=whole(1)[0],
        out_shape=jax.ShapeDtypeStruct((plane, len(pieces), rows // plane, LANES), jnp.bfloat16),
        compiler_params=pltpu.CompilerParams(vmem_limit_bytes=32 << 20),
        cost_estimate=pl.CostEstimate(flops=1 << 30, bytes_accessed=6 << 20, transcendentals=0),
    )(place, weight, *pieces)


def proj_call(place, conv, pieces):
    rows = conv.shape[0] * conv.shape[2]
    width = pieces[0].shape[1]
    return pl.pallas_call(
        proj_kernel,
        in_specs=[pl.BlockSpec(memory_space=pltpu.SMEM), *whole(1 + len(pieces))],
        out_specs=whole(1)[0],
        out_shape=jax.ShapeDtypeStruct((rows, width), jnp.bfloat16),
        scratch_shapes=[pltpu.VMEM((rows, len(pieces) * LANES), jnp.bfloat16)],
        compiler_params=pltpu.CompilerParams(vmem_limit_bytes=32 << 20),
        cost_estimate=pl.CostEstimate(flops=1 << 30, bytes_accessed=6 << 20, transcendentals=0),
    )(place, conv, *pieces)


SEQ = ("zl", "core")
POS = ("zh", "y", "x")
PLANE = ("y", "x")
COLUMN = ("zl", "core", "zh")


def column_pairs(step, other):
    pairs = []
    for z in range(4):
        for core in range(2):
            to, to_core = (z + step) % 4, core ^ other
            pairs.append(
                (z % 2 * 4 + core * 2 + z // 2, to % 2 * 4 + to_core * 2 + to // 2)
            )
    return pairs


def move(a, step, other=0):
    return lax.ppermute(a, COLUMN, column_pairs(step, other))


def places():
    z = 2 * lax.axis_index("zh") + lax.axis_index("zl")
    core = lax.axis_index("core")
    place = [(z + step) % 4 * 2 + (core + other) % 2 for other in (0, 1) for step in (0, 3, 1, 2)]
    return jnp.stack(place).astype(jnp.int32)


def on_device(quant_input, input_scales, out_grad, filter_taps, skip, proj_weight):
    tokens, width = quant_input.shape[1:]
    ctx, seqs, plane = (lax.axis_size(a) for a in (POS, SEQ, PLANE))
    me_dp, me_ctx = lax.axis_index(SEQ), lax.axis_index(POS)
    blocks = input_scales.shape[2]
    chans = width // (ctx * seqs)
    column = ctx * seqs // plane

    with jax.named_scope("share_cotangent"):
        own, place = out_grad[0], places()
        below, above, beside = move(own, 1), move(own, 3), move(own, 0, 1)
    with jax.named_scope("weight_a2a"):
        copies = jnp.broadcast_to(proj_weight[None], (plane, *proj_weight.shape))
        weight = lax.all_to_all(copies, PLANE, 0, 0).reshape(-1, width)
    with jax.named_scope("signal"):
        signal = (
            (quant_input[0].reshape(tokens, blocks, width // blocks) * input_scales[0][:, :, None])
            .reshape(tokens, width)
            .astype(bf16)
        )
        parts = signal.T.reshape(seqs, ctx, chans, tokens)
        taps = filter_taps.reshape(seqs, ctx, seqs, chans // seqs, tokens)
        taps = lax.dynamic_index_in_dim(taps, me_dp, 2, keepdims=False)
        load = jnp.concatenate([parts, taps], axis=2).transpose(1, 0, 2, 3)
        load = load.reshape(ctx * seqs, -1, LANES)
    with jax.named_scope("signal_a2a"):
        load, weight = lax.optimization_barrier((load, weight))
        load = lax.all_to_all(load, POS + SEQ, 0, 0)
    with jax.named_scope("share_far"):
        half = tokens // 2
        far = [move(below[:half], 1), move(above[half:], 3)]
        near = [move(a, 0, 1) for a in (below, above)]
        load, *far = lax.optimization_barrier((load, *far))
    with jax.named_scope("signal_in"):
        field = load.transpose(1, 0, 2)
        h = field[chans:].reshape(chans // seqs, ctx, seqs, LANES).transpose(2, 0, 1, 3)
        h = h.reshape(chans, ctx, LANES)
        first = (me_dp * ctx + me_ctx) * chans
        own_skip = lax.dynamic_slice_in_dim(skip, first, chans)
    with jax.named_scope("share_core"):
        far = jnp.concatenate(far, axis=0)
        pieces = [own, below, above, far, beside, *near, move(far, 0, 1)]
    with jax.named_scope("conv"):
        conv = conv_call(conv_kernel, field, h, own_skip, seqs)
        conv = conv.reshape(chans, ctx // plane, plane, seqs, LANES).transpose(2, 1, 3, 0, 4)
        conv = conv.reshape(plane, column, chans, LANES)
    with jax.named_scope("dconv"):
        dconv = dconv_call(place, weight, pieces, plane)
    with jax.named_scope("middle_a2a"):
        both = lax.all_to_all(jnp.concatenate([conv, dconv], axis=1), PLANE, 0, 0)
    with jax.named_scope("dconv_in"):
        dconv = both[:, column:].reshape(plane, ctx // plane, seqs, chans, LANES)
        dconv = dconv.transpose(3, 1, 0, 2, 4).reshape(chans, ctx * seqs, LANES)
    factor = 1.0 / math.sqrt(seqs * tokens * ctx)
    with jax.named_scope("grad_in"):
        grad_in = conv_call(back_kernel, dconv, h, own_skip, seqs).transpose(1, 0, 2)
        grad_in, conv, dconv = lax.optimization_barrier((grad_in, both[:, :column], dconv))
    with jax.named_scope("grad_in_a2a"):
        grad_in = lax.all_to_all(grad_in, POS + SEQ, 0, 0)
    with jax.named_scope("grad_taps"):
        grad_taps = taps_call(field, dconv, seqs, factor)
    with jax.named_scope("grad_proj"):
        conv, grad_taps = lax.optimization_barrier((conv, grad_taps))
        partial = proj_call(place, conv, pieces)
    with jax.named_scope("grad_proj_a2a"):
        partial, grad_in = lax.optimization_barrier((partial, grad_in))
        partial = lax.all_to_all(partial.reshape(plane, chans, width), PLANE, 0, 0)
        grad_proj = jnp.sum(partial.astype(jnp.float32), axis=0) * factor
    with jax.named_scope("grad_in_out"):
        grad_in = grad_in.reshape(ctx, seqs, chans, LANES).transpose(1, 0, 2, 3)
        grad_in = grad_in.reshape(width, LANES).T
    with jax.named_scope("grad_filter"):
        span = ctx * LANES // seqs
        rounded = grad_taps.astype(bf16).reshape(chans, seqs, span).transpose(1, 0, 2)
        got = []
        for k in range(seqs):
            pairs = [
                (d * ctx + c, (c % seqs + k) % seqs * ctx + (d * ctx + c) // seqs)
                for d in range(seqs)
                for c in range(ctx)
            ]
            piece = lax.dynamic_index_in_dim(rounded, (me_ctx + k) % seqs, 0, keepdims=False)
            got.append(lax.ppermute(piece, SEQ + POS, pairs))
        got = jnp.stack(got)
        grad_filter = jnp.concatenate(
            [
                lax.dynamic_index_in_dim(got, (me_dp - m + seqs) % seqs, 0, keepdims=False)
                for m in range(seqs)
            ],
            axis=0,
        ).astype(jnp.float32)
    return (grad_in[None], grad_filter, grad_proj)


def solution(mesh):
    mesh = Mesh(mesh.devices.reshape(2, 2, 2, 4, 4), SEQ + POS)
    placed = (
        P(SEQ, POS, None),
        P(SEQ, POS, None),
        P(SEQ, POS, None),
        P(None, POS),
        P(),
        P(SEQ + POS, None),
    )
    return jax.shard_map(
        on_device,
        mesh=mesh,
        in_specs=placed,
        out_specs=(P(SEQ, POS, None), P(POS, SEQ), P(SEQ + POS, None)),
        check_vma=False,
    )
```

time: 264 us -> 167 us (0.63)
  the two profiles are of different devices: /device:TPU:1 before, /device:TPU:14 now
where the time goes in v2:
time: 167 us; the launch traced here: 166 us
  starting transfers between devices  56.2 us (34%)
  Pallas kernels  40.4 us (24%)
  waiting for transfers between devices  31.7 us (19%)
  blocking collectives  21 us (13%)
  local copies, waits for them, and re-layouts  14.3 us (9%)
  other arithmetic  1.95 us (1%)
    all_to_all x1, blocking collectives, on_device(): both = lax.all_to_all(jnp.concatenate([conv, dconv], axis=1), PLANE, 0, 0)  21 us
    pallas_call x2, Pallas kernels, conv_call(): pl.pallas_call(functools.partial(kernel, seqs), grid=(chans,), in_specs=[...  20.6 us
    ppermute x4, starting transfers between devices, on_device(): got.append(lax.ppermute(piece, SEQ + POS, pairs))  15.3 us
    ppermute x8, waiting for transfers between devices, move(): return lax.ppermute(a, COLUMN, column_pairs(step, other))  13.8 us
    pallas_call x1, Pallas kernels, taps_call(): pl.pallas_call(functools.partial(taps_kernel, seqs, scale), grid=(chans,)...  10.8 us
    ppermute x4, waiting for transfers between devices, on_device(): got.append(lax.ppermute(piece, SEQ + POS, pairs))  10.1 us
    all_to_all x1, starting transfers between devices, on_device(): load = lax.all_to_all(load, POS + SEQ, 0, 0)  9.75 us
    ppermute x8, starting transfers between devices, move(): return lax.ppermute(a, COLUMN, column_pairs(step, other))  8.4 us
  transfers between devices with their start and end apart: 16, of which 4 were waited for; matrix products, arithmetic and copies ran while one was open for 6% of the time, Pallas kernels for 15%

profile of v2, /device:TPU:14, one launch (start us, length us, event | category | flops | bytes accessed | tf_op | source)
XLA Modules:
  0.0 166.5 jit_solution(1480591509905436771)
XLA Ops:
  0.6 0.0 copy-start
  0.6 2.0 %broadcast_in_dim.4 = bf16[16,16,2048]{2,1,0:T(8,128)(2,1)} broadcast(bf16[16,2048]{1,0:T(8,128)(2,1)} %param.11), dimensions={1,2} | broadcast | bytes 1114112 | tf_op jit(solution)/shard_map/weight_a2a/broadcast_in_dim | solution.py:277
  2.7 7.3 %all-to-all-start = ((bf16[16,16,2048]{2,1,0:T(8,128)(2,1)}), bf16[16,16,2048]{2,1,0:T(8,128)(2,1)S(1)}, u32[]{:S(2)}, u32[]{:S(2)}) async-start(bf16[16,16,2048]{2,1,0:T(8,128)(2,1)} %broadcast_in_dim.4), calls=%async_computation | async-start | bytes 2097152 | tf_op jit(solution)/shard_map/weight_a2a/all_to_all | solution.py:278
  10.0 2.0 %collective-permute-start = (bf16[128,2048]{1,0:T(8,128)(2,1)}, bf16[128,2048]{1,0:T(8,128)(2,1)S(1)}, u32[]{:S(2)}, u32[]{:S(2)}) collective-permute-start(bf16[128,2048]{1,0:T(8,128)(2,1)} %bitcast.18.refs_0_), channel_id=1, source_target_pairs={{0,64},{32,96},{64,16},{96,48},{16,80},{48,112},{80,0},{112,32},{1... | collective-permute-start | bytes 1572872 | tf_op jit(solution)/shard_map/share_cotangent/ppermute | solution.py:255
  12.0 2.2 %collective-permute-start.2 = (bf16[128,2048]{1,0:T(8,128)(2,1)}, bf16[128,2048]{1,0:T(8,128)(2,1)S(1)}, u32[]{:S(2)}, u32[]{:S(2)}) collective-permute-start(bf16[128,2048]{1,0:T(8,128)(2,1)} %bitcast.18.refs_0_), channel_id=1, source_target_pairs={{0,80},{32,112},{64,0},{96,32},{16,64},{48,96},{80,16},{112,48},{1... | collective-permute-start | bytes 1572872 | tf_op jit(solution)/shard_map/share_cotangent/ppermute | solution.py:255
  14.2 1.3 copy.40
  15.5 0.1 fusion
  15.7 0.2 maximum_bitcast_fusion
  15.8 0.5 copy.42
  16.4 7.7 %all-to-all-done = bf16[16,16,2048]{2,1,0:T(8,128)(2,1)S(1)} async-done(((bf16[16,16,2048]{2,1,0:T(8,128)(2,1)}), bf16[16,16,2048]{2,1,0:T(8,128)(2,1)S(1)}, u32[]{:S(2)}, u32[]{:S(2)}) %all-to-all-start) | async-done | bytes 1048608 | tf_op jit(solution)/shard_map/weight_a2a/all_to_all | solution.py:278
  24.1 1.4 copy.43
  25.4 9.7 %all-to-all-start.1 = ((bf16[128,20,128]{2,1,0:T(8,128)(2,1)}), bf16[128,20,128]{2,1,0:T(8,128)(2,1)}, u32[]{:S(2)}, u32[]{:S(2)}) async-start(bf16[128,20,128]{2,1,0:T(8,128)(2,1)} %copy.43), calls=%async_computation.1 | async-start | bytes 1572864 | tf_op jit(solution)/shard_map/signal_a2a/all_to_all | solution.py:292
  35.2 1.8 %collective-permute-start.1 = (bf16[64,2048]{1,0:T(8,128)(2,1)S(1)}, bf16[64,2048]{1,0:T(8,128)(2,1)S(1)}, u32[]{:S(2)}, u32[]{:S(2)}) collective-permute-start(bf16[64,2048]{1,0:T(8,128)(2,1)S(1)} %slice.20), channel_id=1, source_target_pairs={{0,64},{32,96},{64,16},{96,48},{16,80},{48,112},{80,0},{112,32},{1... | collective-permute-start | bytes 786440 | tf_op jit(solution)/shard_map/share_far/ppermute | solution.py:255
  37.0 1.8 %collective-permute-start.3 = (bf16[64,2048]{1,0:T(8,128)(2,1)S(1)}, bf16[64,2048]{1,0:T(8,128)(2,1)}, u32[]{:S(2)}, u32[]{:S(2)}) collective-permute-start(bf16[64,2048]{1,0:T(8,128)(2,1)S(1)} %slice.21), channel_id=1, source_target_pairs={{0,80},{32,112},{64,0},{96,32},{16,64},{48,96},{80,16},{112,48},{1... | collective-permute-start | bytes 786440 | tf_op jit(solution)/shard_map/share_far/ppermute | solution.py:255
  38.9 0.0 collective-permute-start.4
  38.9 0.5 collective-permute-start.5
  39.4 13.8 %collective-permute-done.1 = bf16[64,2048]{1,0:T(8,128)(2,1)S(1)} collective-permute-done((bf16[64,2048]{1,0:T(8,128)(2,1)S(1)}, bf16[64,2048]{1,0:T(8,128)(2,1)S(1)}, u32[]{:S(2)}, u32[]{:S(2)}) %collective-permute-start.1) | collective-permute-done | bytes 262176 | tf_op jit(solution)/shard_map/share_far/ppermute | solution.py:255
  53.2 1.0 constant_dynamic-update-slice_fusion.refs_3_
  54.2 0.1 collective-permute-start.7
  54.4 0.8 dynamic_slice.24.skip_ref
  55.1 0.1 stack.50.place_ref
  55.2 1.3 copy.65
  56.6 8.6 %conv.1 = bf16[16,128,128]{2,1,0:T(8,128)(2,1)S(1)} custom-call(f32[16]{0:T(128)S(1)} %dynamic_slice.24.skip_ref, bf16[20,128,128]{2,1,0:T(8,128)(2,1)S(1)} %bitcast.79, bf16[16,32,128]{2,1,0:T(8,128)(2,1)S(1)} %bitcast.85), custom_call_target="tpu_custom_call" | custom-call | flops 5368709120 | bytes 1048576 | tf_op jit(solution)/shard_map/conv/pallas_call | solution.py:147
  65.2 0.6 copy.46
  65.8 4.0 %dconv.1 = bf16[16,8,16,128]{3,2,1,0:T(8,128)(2,1)S(1)} custom-call(s32[8]{0:T(128)S(1)} %stack.50.place_ref, bf16[256,2048]{1,0:T(8,128)(2,1)S(1)} %bitcast.77, bf16[128,2048]{1,0:T(8,128)(2,1)} %bitcast.18.refs_0_, bf16[128,2048]{1,0:T(8,128)(2,1)S(1)} %collective-permute-done.refs_1_, bf16[128,2048]{1,0:T(8,128)(2,1)S(1)} %collective-permute-done.2.refs_2_, ...), custom_call_target="tpu_custom_call" | custom-call | flops 1073741824 | bytes 6291456 | tf_op jit(solution)/shard_map/dconv/pallas_call | solution.py:213
  69.9 0.1 pad_maximum_fusion
  70.0 21.0 %all_to_all.25 = bf16[16,16,16,128]{3,2,1,0:T(8,128)(2,1)S(1)} all-to-all(bf16[16,16,16,128]{3,2,1,0:T(8,128)(2,1)S(1)} %pad_maximum_fusion), channel_id=1, replica_groups=mesh['zl'=2,'core'=2,'zh'=2,'y'=4,'x'=4] {'y','x'}, dimensions={0} | all-to-all | bytes 2097152 | tf_op jit(solution)/shard_map/middle_a2a/all_to_all | solution.py:314
  90.9 0.3 fusion.1
  91.2 0.3 copy.47
  91.5 12.0 %grad_in.1 = bf16[16,128,128]{2,1,0:T(8,128)(2,1)S(1)} custom-call(f32[16]{0:T(128)S(1)} %dynamic_slice.24.skip_ref, bf16[16,128,128]{2,1,0:T(8,128)(2,1)S(1)} %bitcast.81, bf16[16,32,128]{2,1,0:T(8,128)(2,1)S(1)} %bitcast.86), custom_call_target="tpu_custom_call" | custom-call | flops 5368709120 | bytes 1048576 | tf_op jit(solution)/shard_map/grad_in/pallas_call | solution.py:147
  103.5 1.1 copy.48
  104.6 8.1 %all-to-all-start.3 = ((bf16[128,16,128]{2,1,0:T(8,128)(2,1)}), bf16[128,16,128]{2,1,0:T(8,128)(2,1)}, u32[]{:S(2)}, u32[]{:S(2)}) async-start(bf16[128,16,128]{2,1,0:T(8,128)(2,1)} %copy.48), calls=%async_computation.3 | async-start | bytes 1048576 | tf_op jit(solution)/shard_map/grad_in_a2a/all_to_all | solution.py:323
  112.8 1.1 copy-done.2
  113.9 10.8 %grad_taps.1 = f32[16,32,128]{2,1,0:T(8,128)S(1)} custom-call(bf16[20,128,128]{2,1,0:T(8,128)(2,1)S(1)} %bitcast.80, bf16[16,128,128]{2,1,0:T(8,128)(2,1)S(1)} %bitcast.82), custom_call_target="tpu_custom_call" | custom-call | flops 8589934592 | bytes 1048576 | tf_op jit(solution)/shard_map/grad_taps/pallas_call | solution.py:165
  124.6 5.0 %grad_proj.1 = bf16[256,2048]{1,0:T(8,128)(2,1)} custom-call(s32[8]{0:T(128)S(1)} %stack.50.place_ref, bf16[16,8,16,128]{3,2,1,0:T(8,128)(2,1)S(1)} %get-tuple-element.22.c_ref, bf16[128,2048]{1,0:T(8,128)(2,1)} %bitcast.18.refs_0_, bf16[128,2048]{1,0:T(8,128)(2,1)S(1)} %collective-permute-done.refs_1_, ...), custom_call_target="tpu_custom_call" | custom-call | flops 1073741824 | bytes 6291456 | tf_op jit(solution)/shard_map/grad_proj/pallas_call | solution.py:226
  129.6 7.3 %all-to-all-start.4 = ((bf16[16,16,2048]{2,1,0:T(8,128)(2,1)}), bf16[16,16,2048]{2,1,0:T(8,128)(2,1)S(1)}, u32[]{:S(2)}, u32[]{:S(2)}) async-start(bf16[16,16,2048]{2,1,0:T(8,128)(2,1)} %bitcast.47), calls=%async_computation.4 | async-start | bytes 2097152 | tf_op jit(solution)/shard_map/grad_proj_a2a/all_to_all | solution.py:331
  137.0 0.3 constant_dynamic-slice_fusion.3
  137.3 3.7 %collective-permute-start.8 = (bf16[16,1024]{1,0:T(8,128)(2,1)S(1)}, bf16[16,1024]{1,0:T(8,128)(2,1)S(1)}, u32[]{:S(2)}, u32[]{:S(2)}) collective-permute-start(bf16[16,1024]{1,0:T(8,128)(2,1)S(1)} %bitcast.93), channel_id=1, source_target_pairs={{0,0},{1,32},{2,64},{3,96},{4,1},{5,33},{6,65},{7,97},{8,2},{9,34}... | collective-permute-start | bytes 98312 | tf_op jit(solution)/shard_map/grad_filter/ppermute | solution.py:347
  141.0 1.9 %collective-permute-start.9 = (bf16[16,1024]{1,0:T(8,128)(2,1)S(1)}, bf16[16,1024]{1,0:T(8,128)(2,1)S(1)}, u32[]{:S(2)}, u32[]{:S(2)}) collective-permute-start(bf16[16,1024]{1,0:T(8,128)(2,1)S(1)} %bitcast.94), channel_id=1, source_target_pairs={{0,32},{1,64},{2,96},{3,0},{4,33},{5,65},{6,97},{7,1},{8,34},{9,66... | collective-permute-start | bytes 98312 | tf_op jit(solution)/shard_map/grad_filter/ppermute | solution.py:347
  143.0 7.7 %collective-permute-start.10 = (bf16[16,1024]{1,0:T(8,128)(2,1)S(1)}, bf16[16,1024]{1,0:T(8,128)(2,1)S(1)}, u32[]{:S(2)}, u32[]{:S(2)}) collective-permute-start(bf16[16,1024]{1,0:T(8,128)(2,1)S(1)} %bitcast.95), channel_id=1, source_target_pairs={{0,64},{1,96},{2,0},{3,32},{4,65},{5,97},{6,1},{7,33},{8,66},{9,98... | collective-permute-start | bytes 98312 | tf_op jit(solution)/shard_map/grad_filter/ppermute | solution.py:347
  150.7 2.0 %collective-permute-start.11 = (bf16[16,1024]{1,0:T(8,128)(2,1)S(1)}, bf16[16,1024]{1,0:T(8,128)(2,1)S(1)}, u32[]{:S(2)}, u32[]{:S(2)}) collective-permute-start(bf16[16,1024]{1,0:T(8,128)(2,1)S(1)} %bitcast.96), channel_id=1, source_target_pairs={{0,96},{1,0},{2,32},{3,64},{4,97},{5,1},{6,33},{7,65},{8,98},{9,2}... | collective-permute-start | bytes 98312 | tf_op jit(solution)/shard_map/grad_filter/ppermute | solution.py:347
  152.7 5.3 %collective-permute-done.8 = bf16[16,1024]{1,0:T(8,128)(2,1)S(1)} collective-permute-done((bf16[16,1024]{1,0:T(8,128)(2,1)S(1)}, bf16[16,1024]{1,0:T(8,128)(2,1)S(1)}, u32[]{:S(2)}, u32[]{:S(2)}) %collective-permute-start.8) | collective-permute-done | bytes 32800 | tf_op jit(solution)/shard_map/grad_filter/ppermute | solution.py:347
  158.0 4.8 %collective-permute-done.11 = bf16[16,1024]{1,0:T(8,128)(2,1)S(1)} collective-permute-done((bf16[16,1024]{1,0:T(8,128)(2,1)S(1)}, bf16[16,1024]{1,0:T(8,128)(2,1)S(1)}, u32[]{:S(2)}, u32[]{:S(2)}) %collective-permute-start.11) | collective-permute-done | bytes 32800 | tf_op jit(solution)/shard_map/grad_filter/ppermute | solution.py:347
  162.9 0.7 maximum_convert_fusion
  163.6 1.1 copy.49
  164.7 1.0 copy.54
  165.7 0.1 convert_reduce_fusion
  165.8 0.7 broadcast_multiply_fusion
  (33 shorter events, 0.3 us)
Async XLA Ops:
  0.6 13.5 %copy-start = (bf16[2048,128]{1,0:T(8,128)(2,1)S(1)}, bf16[2048,128]{1,0:T(8,128)(2,1)}, u32[]{:S(2)}) copy-start(bf16[2048,128]{1,0:T(8,128)(2,1)} %param.9) | copy-start | bytes 1572868
  2.7 21.4 %all-to-all-start = ((bf16[16,16,2048]{2,1,0:T(8,128)(2,1)}), bf16[16,16,2048]{2,1,0:T(8,128)(2,1)S(1)}, u32[]{:S(2)}, u32[]{:S(2)}) async-start(bf16[16,16,2048]{2,1,0:T(8,128)(2,1)} %broadcast_in_dim.4), calls=%async_computation | async-start | bytes 2097152 | tf_op jit(solution)/shard_map/weight_a2a/all_to_all | solution.py:278
  10.0 5.6 %copy-start.3 = (f32[1,128,16]{1,2,0:T(8,128)S(1)}, f32[1,128,16]{1,2,0:T(8,128)}, u32[]{:S(2)}) copy-start(f32[1,128,16]{1,2,0:T(8,128)} %param.7) | copy-start | bytes 24580
  10.0 25.2 %collective-permute-start = (bf16[128,2048]{1,0:T(8,128)(2,1)}, bf16[128,2048]{1,0:T(8,128)(2,1)S(1)}, u32[]{:S(2)}, u32[]{:S(2)}) collective-permute-start(bf16[128,2048]{1,0:T(8,128)(2,1)} %bitcast.18.refs_0_), channel_id=1, source_target_pairs={{0,64},{32,96},{64,16},{96,48},{16,80},{48,112},{80,0},{112,32},{1... | collective-permute-start | bytes 1572872 | tf_op jit(solution)/shard_map/share_cotangent/ppermute | solution.py:255
  12.0 25.1 %collective-permute-start.2 = (bf16[128,2048]{1,0:T(8,128)(2,1)}, bf16[128,2048]{1,0:T(8,128)(2,1)S(1)}, u32[]{:S(2)}, u32[]{:S(2)}) collective-permute-start(bf16[128,2048]{1,0:T(8,128)(2,1)} %bitcast.18.refs_0_), channel_id=1, source_target_pairs={{0,80},{32,112},{64,0},{96,32},{16,64},{48,96},{80,16},{112,48},{1... | collective-permute-start | bytes 1572872 | tf_op jit(solution)/shard_map/share_cotangent/ppermute | solution.py:255
  25.4 27.8 %all-to-all-start.1 = ((bf16[128,20,128]{2,1,0:T(8,128)(2,1)}), bf16[128,20,128]{2,1,0:T(8,128)(2,1)}, u32[]{:S(2)}, u32[]{:S(2)}) async-start(bf16[128,20,128]{2,1,0:T(8,128)(2,1)} %copy.43), calls=%async_computation.1 | async-start | bytes 1572864 | tf_op jit(solution)/shard_map/signal_a2a/all_to_all | solution.py:292
  35.2 18.0 %collective-permute-start.1 = (bf16[64,2048]{1,0:T(8,128)(2,1)S(1)}, bf16[64,2048]{1,0:T(8,128)(2,1)S(1)}, u32[]{:S(2)}, u32[]{:S(2)}) collective-permute-start(bf16[64,2048]{1,0:T(8,128)(2,1)S(1)} %slice.20), channel_id=1, source_target_pairs={{0,64},{32,96},{64,16},{96,48},{16,80},{48,112},{80,0},{112,32},{1... | collective-permute-start | bytes 786440 | tf_op jit(solution)/shard_map/share_far/ppermute | solution.py:255
  37.0 16.2 %collective-permute-start.3 = (bf16[64,2048]{1,0:T(8,128)(2,1)S(1)}, bf16[64,2048]{1,0:T(8,128)(2,1)}, u32[]{:S(2)}, u32[]{:S(2)}) collective-permute-start(bf16[64,2048]{1,0:T(8,128)(2,1)S(1)} %slice.21), channel_id=1, source_target_pairs={{0,80},{32,112},{64,0},{96,32},{16,64},{48,96},{80,16},{112,48},{1... | collective-permute-start | bytes 786440 | tf_op jit(solution)/shard_map/share_far/ppermute | solution.py:255
  38.9 26.9 %collective-permute-start.4 = (bf16[128,2048]{1,0:T(8,128)(2,1)}, bf16[128,2048]{1,0:T(8,128)(2,1)}, u32[]{:S(2)}, u32[]{:S(2)}) collective-permute-start(bf16[128,2048]{1,0:T(8,128)(2,1)} %bitcast.18.refs_0_), channel_id=1, source_target_pairs={{0,32},{32,0},{64,96},{96,64},{16,48},{48,16},{80,112},{112,80},{1... | collective-permute-start | bytes 1572872 | tf_op jit(solution)/shard_map/share_cotangent/ppermute | solution.py:255
  38.9 26.9 %collective-permute-start.5 = (bf16[128,2048]{1,0:T(8,128)(2,1)S(1)}, bf16[128,2048]{1,0:T(8,128)(2,1)}, u32[]{:S(2)}, u32[]{:S(2)}) collective-permute-start(bf16[128,2048]{1,0:T(8,128)(2,1)S(1)} %collective-permute-done.refs_1_), channel_id=1, source_target_pairs={{0,32},{32,0},{64,96},{96,64},{16,48},{48,16},{80,112},{112,80},{1... | collective-permute-start | bytes 1572872 | tf_op jit(solution)/shard_map/share_far/ppermute | solution.py:255
  39.4 26.4 %collective-permute-start.6 = (bf16[128,2048]{1,0:T(8,128)(2,1)S(1)}, bf16[128,2048]{1,0:T(8,128)(2,1)}, u32[]{:S(2)}, u32[]{:S(2)}) collective-permute-start(bf16[128,2048]{1,0:T(8,128)(2,1)S(1)} %collective-permute-done.2.refs_2_), channel_id=1, source_target_pairs={{0,32},{32,0},{64,96},{96,64},{16,48},{48,16},{80,112},{112,80},{1... | collective-permute-start | bytes 1572872 | tf_op jit(solution)/shard_map/share_far/ppermute | solution.py:255
  54.2 11.6 %collective-permute-start.7 = (bf16[128,2048]{1,0:T(8,128)(2,1)S(1)}, bf16[128,2048]{1,0:T(8,128)(2,1)}, u32[]{:S(2)}, u32[]{:S(2)}) collective-permute-start(bf16[128,2048]{1,0:T(8,128)(2,1)S(1)} %constant_dynamic-update-slice_fusion.refs_3_), channel_id=1, source_target_pairs={{0,32},{32,0},{64,96},{96,64},{16,48},{48,16},{80,112},{112,80},{1... | collective-permute-start | bytes 1572872 | tf_op jit(solution)/shard_map/share_core/ppermute | solution.py:255
  56.5 8.7 %copy-start.1 = (bf16[128,20,128]{2,0,1:T(8,128)(2,1)}, bf16[128,20,128]{2,0,1:T(8,128)(2,1)S(1)}, u32[]{:S(2)}) copy-start(bf16[128,20,128]{2,0,1:T(8,128)(2,1)S(1)} %copy.65) | copy-start | bytes 1966084
  104.6 25.0 %all-to-all-start.3 = ((bf16[128,16,128]{2,1,0:T(8,128)(2,1)}), bf16[128,16,128]{2,1,0:T(8,128)(2,1)}, u32[]{:S(2)}, u32[]{:S(2)}) async-start(bf16[128,16,128]{2,1,0:T(8,128)(2,1)} %copy.48), calls=%async_computation.3 | async-start | bytes 1048576 | tf_op jit(solution)/shard_map/grad_in_a2a/all_to_all | solution.py:323
  112.8 1.1 copy-start.2
  129.6 36.1 %all-to-all-start.4 = ((bf16[16,16,2048]{2,1,0:T(8,128)(2,1)}), bf16[16,16,2048]{2,1,0:T(8,128)(2,1)S(1)}, u32[]{:S(2)}, u32[]{:S(2)}) async-start(bf16[16,16,2048]{2,1,0:T(8,128)(2,1)} %bitcast.47), calls=%async_computation.4 | async-start | bytes 2097152 | tf_op jit(solution)/shard_map/grad_proj_a2a/all_to_all | solution.py:331
  137.3 20.7 %collective-permute-start.8 = (bf16[16,1024]{1,0:T(8,128)(2,1)S(1)}, bf16[16,1024]{1,0:T(8,128)(2,1)S(1)}, u32[]{:S(2)}, u32[]{:S(2)}) collective-permute-start(bf16[16,1024]{1,0:T(8,128)(2,1)S(1)} %bitcast.93), channel_id=1, source_target_pairs={{0,0},{1,32},{2,64},{3,96},{4,1},{5,33},{6,65},{7,97},{8,2},{9,34}... | collective-permute-start | bytes 98312 | tf_op jit(solution)/shard_map/grad_filter/ppermute | solution.py:347
  141.0 16.9 %collective-permute-start.9 = (bf16[16,1024]{1,0:T(8,128)(2,1)S(1)}, bf16[16,1024]{1,0:T(8,128)(2,1)S(1)}, u32[]{:S(2)}, u32[]{:S(2)}) collective-permute-start(bf16[16,1024]{1,0:T(8,128)(2,1)S(1)} %bitcast.94), channel_id=1, source_target_pairs={{0,32},{1,64},{2,96},{3,0},{4,33},{5,65},{6,97},{7,1},{8,34},{9,66... | collective-permute-start | bytes 98312 | tf_op jit(solution)/shard_map/grad_filter/ppermute | solution.py:347
  143.0 15.0 %collective-permute-start.10 = (bf16[16,1024]{1,0:T(8,128)(2,1)S(1)}, bf16[16,1024]{1,0:T(8,128)(2,1)S(1)}, u32[]{:S(2)}, u32[]{:S(2)}) collective-permute-start(bf16[16,1024]{1,0:T(8,128)(2,1)S(1)} %bitcast.95), channel_id=1, source_target_pairs={{0,64},{1,96},{2,0},{3,32},{4,65},{5,97},{6,1},{7,33},{8,66},{9,98... | collective-permute-start | bytes 98312 | tf_op jit(solution)/shard_map/grad_filter/ppermute | solution.py:347
  150.7 12.1 %collective-permute-start.11 = (bf16[16,1024]{1,0:T(8,128)(2,1)S(1)}, bf16[16,1024]{1,0:T(8,128)(2,1)S(1)}, u32[]{:S(2)}, u32[]{:S(2)}) collective-permute-start(bf16[16,1024]{1,0:T(8,128)(2,1)S(1)} %bitcast.96), channel_id=1, source_target_pairs={{0,96},{1,0},{2,32},{3,64},{4,97},{5,1},{6,33},{7,65},{8,98},{9,2}... | collective-permute-start | bytes 98312 | tf_op jit(solution)/shard_map/grad_filter/ppermute | solution.py:347

commit v3 on v2

v3 whole, which is shorter than its diff:
```python
import functools
import math

import jax
import jax.numpy as jnp
from jax import lax
from jax.experimental import pallas as pl
from jax.experimental.pallas import tpu as pltpu
from jax.sharding import Mesh, PartitionSpec as P

LANES = 128
HALF = LANES // 2
GROUP = 4
f32, bf16 = jnp.float32, jnp.bfloat16


def iota(rows, axis):
    return lax.broadcasted_iota(jnp.int32, (rows, LANES), axis)


def turn(field, by):
    return pltpu.roll(field, by, 1)


def moved(field, by):
    if by == 0:
        return field
    gap = jnp.zeros((abs(by), LANES), field.dtype)
    if by > 0:
        return jnp.concatenate([gap, field[:-by]], axis=0)
    return jnp.concatenate([field[-by:], gap], axis=0)


def mirror():
    return (iota(LANES, 0) + iota(LANES, 1) == LANES - 1).astype(bf16)


def tap_rows(taps, first, before):
    same = iota(HALF, 1) >= iota(HALF, 0)
    parts = []
    for delta in range(first, first + GROUP):
        line = jnp.broadcast_to(taps[delta : delta + 1, :], (HALF, LANES))
        here = pltpu.roll(line, 0, 1, stride=1, stride_axis=0)
        parts.append(jnp.where(same, here, before).astype(bf16))
        before = here
    return jnp.concatenate(parts, axis=0), before


def correlate(field, taps, seqs, sign):
    rows, span = field.shape[0], GROUP * seqs
    low = iota(rows, 1) < HALF
    beside = moved(field, sign * seqs)
    halves = [
        jnp.where(low, field, turn(beside, HALF)),
        jnp.where(low, turn(field, HALF), beside),
    ]
    wide = [
        jnp.concatenate([h.astype(bf16), moved(h, sign * 2 * seqs).astype(bf16)], axis=1)
        for h in halves
    ]
    total = [jnp.zeros((rows, LANES), f32)] * 2
    before = jnp.zeros((HALF, LANES), f32)
    for k in range(rows // span):
        matrix, before = tap_rows(taps, k * GROUP, before)
        cut = k * span
        kept = [w[: rows - cut] if sign > 0 else w[cut:] for w in wide]
        part = jnp.dot(jnp.concatenate(kept, axis=0), matrix, preferred_element_type=f32)
        for p in range(2):
            add = part[p * (rows - cut) : (p + 1) * (rows - cut)]
            if cut:
                gap = jnp.zeros((cut, LANES), f32)
                add = jnp.concatenate([gap, add] if sign > 0 else [add, gap], axis=0)
            total[p] = total[p] + add
    across = turn(total[1], HALF)
    return total[0] + jnp.where(low, moved(across, sign * seqs), across)


def conv_kernel(seqs, skip_ref, x_ref, h_ref, y_ref):
    many = x_ref.shape[0]
    for i in range(many):
        x = x_ref[i].astype(f32)
        y = correlate(x, h_ref[i].astype(f32), seqs, 1)
        y_ref[i] = (y + x * skip_ref[pl.program_id(0) * many + i]).astype(bf16)


def back_kernel(seqs, skip_ref, d_ref, h_ref, y_ref):
    many = d_ref.shape[0]
    for i in range(many):
        d = d_ref[i].astype(f32)
        y = correlate(d, h_ref[i].astype(f32), seqs, -1)
        y_ref[i] = (y + d * skip_ref[pl.program_id(0) * many + i]).astype(bf16)


def taps_kernel(seqs, scale_ref, x_ref, d_ref, f_ref, long_ref, sum_ref):
    many, rows, _ = x_ref.shape
    blocks, span = rows // seqs, GROUP * seqs
    same = (iota(LANES, 0) == iota(LANES, 1)).astype(bf16)
    keep = iota(HALF, 0) + iota(HALF, 1) < LANES
    step = pl.program_id(0)
    for i in range(many):
        x, d = x_ref[i].astype(f32), d_ref[i].astype(f32)
        left = []
        for v in range(GROUP):
            part = moved(x, v * seqs).astype(bf16)
            part = lax.dot_general(
                same, part, (((1,), (1,)), ((), ())), preferred_element_type=f32
            ).astype(bf16)
            left.append(jnp.concatenate([part[:HALF], part[HALF:]], axis=1))
        left = jnp.concatenate(left, axis=0)
        across = turn(d, HALF)
        shifted = jnp.where(iota(rows, 1) < HALF, moved(across, -seqs), across)
        for p, part in enumerate((d, shifted)):
            long_ref[i, p, :rows, :] = part.astype(bf16)
            long_ref[i, p, rows:, :] = jnp.zeros((rows, LANES), bf16)
        after = jnp.zeros((HALF, LANES), f32)

        def outer(k):
            right = [
                jnp.concatenate(
                    [long_ref[i, p, at * span : at * span + rows, :] for p in range(2)], axis=0
                )
                for at in (k, k + 1)
            ]
            return jnp.dot(left, jnp.concatenate(right, axis=1), preferred_element_type=f32)

        steps = list(reversed(range(0, rows // span, 2)))
        ready = outer(steps[0])
        for n, k in enumerate(steps):
            now = ready
            if n + 1 < len(steps):
                ready = outer(steps[n + 1])
            for j in reversed(range(2 * GROUP)):
                at, v = j // GROUP, j % GROUP
                here = now[v * HALF : (v + 1) * HALF, at * LANES : (at + 1) * LANES]
                lined = pltpu.roll(jnp.where(keep, here, after), 0, 1, stride=1, stride_axis=0)
                delta = k * GROUP + j
                sum_ref[pl.ds((step * many + i) * blocks + delta, 1), :] = (
                    jnp.sum(lined, axis=0, keepdims=True) * scale_ref[0]
                )
                after = here

    @pl.when(step == pl.num_programs(0) - 1)
    def _():
        f_ref[...] = jnp.dot(
            sum_ref[...].astype(bf16), mirror(), preferred_element_type=f32
        ).astype(bf16)


MANY = 4


def per_channel(many, shape):
    return pl.BlockSpec((many, *shape[1:]), lambda i: (i, 0, 0))


def estimate(flops):
    return pl.CostEstimate(flops=flops, bytes_accessed=1 << 16, transcendentals=0)


def conv_call(kernel, field, taps, skip, seqs):
    chans, rows = taps.shape[0], field.shape[1]
    return pl.pallas_call(
        functools.partial(kernel, seqs),
        grid=(chans // MANY,),
        in_specs=[
            pl.BlockSpec(memory_space=pltpu.SMEM),
            per_channel(MANY, field.shape),
            per_channel(MANY, taps.shape),
        ],
        out_specs=per_channel(MANY, field.shape),
        out_shape=jax.ShapeDtypeStruct((chans, rows, LANES), bf16),
        compiler_params=pltpu.CompilerParams(vmem_limit_bytes=24 << 20),
        cost_estimate=estimate(1 << 20),
    )(skip, field, taps)


def taps_call(x, d, seqs, scale):
    chans, rows, _ = d.shape
    out = jax.ShapeDtypeStruct((chans * rows // seqs, LANES), bf16)
    return pl.pallas_call(
        functools.partial(taps_kernel, seqs),
        grid=(chans // MANY,),
        in_specs=[
            pl.BlockSpec(memory_space=pltpu.SMEM),
            per_channel(MANY, x.shape),
            per_channel(MANY, d.shape),
        ],
        out_specs=pl.BlockSpec(out.shape, lambda i: (0, 0)),
        out_shape=out,
        scratch_shapes=[
            pltpu.VMEM((MANY, 2, 2 * rows, LANES), bf16),
            pltpu.VMEM(out.shape, f32),
        ],
        compiler_params=pltpu.CompilerParams(vmem_limit_bytes=24 << 20),
        cost_estimate=estimate(1 << 20),
    )(scale, x, d).reshape(chans, rows // seqs, LANES)


def dconv_kernel(place_ref, w_ref, *refs):
    *pieces, out_ref, weight_ref = refs
    for k in range(weight_ref.shape[1] // LANES):
        weight_ref[:, k * LANES : (k + 1) * LANES] = w_ref[:, k].reshape(-1, LANES)
    flip = mirror()
    for first in range(0, len(pieces), GROUP):
        block = jnp.concatenate([piece[...] for piece in pieces[first : first + GROUP]], axis=0)
        wide = lax.dot_general(
            weight_ref[...], block, (((1,), (1,)), ((), ())), preferred_element_type=f32
        ).astype(bf16)
        for j in range(GROUP):
            part = wide[:, j * LANES : (j + 1) * LANES]
            part = jnp.dot(part, flip, preferred_element_type=f32).astype(bf16)
            out_ref[:, pl.ds(place_ref[first + j], 1)] = part.reshape(
                out_ref.shape[0], 1, *out_ref.shape[2:]
            )


def proj_kernel(place_ref, c_ref, *refs):
    *pieces, out_ref, lhs_ref = refs
    rows, width = out_ref.shape
    ahead = c_ref.shape[1] - len(pieces)
    for j in range(len(pieces)):
        part = c_ref[:, pl.ds(ahead + place_ref[j], 1)]
        lhs_ref[:, j * LANES : (j + 1) * LANES] = part.reshape(rows, LANES)
    step = 512
    for at in range(0, width, step):
        block = jnp.concatenate([piece[:, at : at + step] for piece in pieces], axis=0)
        out_ref[:, at : at + step] = jnp.dot(
            lhs_ref[...], block, preferred_element_type=f32
        ).astype(bf16)


def whole(count):
    return [pl.BlockSpec(memory_space=pltpu.VMEM)] * count


def dconv_call(place, load, pieces):
    plane, _, chans, _ = load.shape
    return pl.pallas_call(
        dconv_kernel,
        in_specs=[pl.BlockSpec(memory_space=pltpu.SMEM), *whole(1 + len(pieces))],
        out_specs=whole(1)[0],
        out_shape=jax.ShapeDtypeStruct((plane, len(pieces), chans, LANES), bf16),
        scratch_shapes=[pltpu.VMEM((plane * chans, pieces[0].shape[1]), bf16)],
        compiler_params=pltpu.CompilerParams(vmem_limit_bytes=32 << 20),
        cost_estimate=pl.CostEstimate(flops=1 << 30, bytes_accessed=6 << 20, transcendentals=0),
    )(place, load, *pieces)


def proj_call(place, conv, pieces):
    rows = conv.shape[0] * conv.shape[2]
    width = pieces[0].shape[1]
    return pl.pallas_call(
        proj_kernel,
        in_specs=[pl.BlockSpec(memory_space=pltpu.SMEM), *whole(1 + len(pieces))],
        out_specs=whole(1)[0],
        out_shape=jax.ShapeDtypeStruct((rows, width), jnp.bfloat16),
        scratch_shapes=[pltpu.VMEM((rows, len(pieces) * LANES), jnp.bfloat16)],
        compiler_params=pltpu.CompilerParams(vmem_limit_bytes=32 << 20),
        cost_estimate=pl.CostEstimate(flops=1 << 30, bytes_accessed=6 << 20, transcendentals=0),
    )(place, conv, *pieces)


SEQ = ("zl", "core")
POS = ("zh", "y", "x")
PLANE = ("y", "x")
COLUMN = ("zl", "core", "zh")


def column_pairs(step, other):
    pairs = []
    for z in range(4):
        for core in range(2):
            to, to_core = (z + step) % 4, core ^ other
            pairs.append(
                (z % 2 * 4 + core * 2 + z // 2, to % 2 * 4 + to_core * 2 + to // 2)
            )
    return pairs


def move(a, step, other=0):
    return lax.ppermute(a, COLUMN, column_pairs(step, other))


def places():
    z = 2 * lax.axis_index("zh") + lax.axis_index("zl")
    core = lax.axis_index("core")
    place = [(z + step) % 4 * 2 + (core + other) % 2 for other in (0, 1) for step in (0, 3, 1, 2)]
    return jnp.stack(place).astype(jnp.int32)


def on_device(quant_input, input_scales, out_grad, filter_taps, skip, proj_weight):
    tokens, width = quant_input.shape[1:]
    ctx, seqs, plane = (lax.axis_size(a) for a in (POS, SEQ, PLANE))
    me_dp, me_ctx = lax.axis_index(SEQ), lax.axis_index(POS)
    blocks = input_scales.shape[2]
    chans = width // (ctx * seqs)
    column = ctx * seqs // plane

    with jax.named_scope("signal"):
        signal = (
            (quant_input[0].reshape(tokens, blocks, width // blocks) * input_scales[0][:, :, None])
            .reshape(tokens, width)
            .astype(bf16)
        )
        parts = signal.T.reshape(seqs, ctx, chans, tokens)
        taps = filter_taps.reshape(seqs, ctx, seqs, chans // seqs, tokens)
        taps = lax.dynamic_index_in_dim(taps, me_dp, 2, keepdims=False)
        load = jnp.concatenate([parts, taps], axis=2).transpose(1, 0, 2, 3)
        load = load.reshape(ctx * seqs, -1, LANES)
    with jax.named_scope("signal_a2a"):
        load = lax.all_to_all(load, POS + SEQ, 0, 0)
    with jax.named_scope("signal_in"):
        x = load[:, :chans].transpose(1, 0, 2)
        h = load[:, chans:].reshape(ctx, seqs, chans // seqs, LANES).transpose(1, 2, 0, 3)
        h = h.reshape(chans, ctx, LANES)
        first = (me_dp * ctx + me_ctx) * chans
        own_skip = lax.dynamic_slice_in_dim(skip, first, chans)
    with jax.named_scope("share_cotangent"):
        own, h = lax.optimization_barrier((out_grad[0], h))
        place = places()
        below, above, beside = move(own, 1), move(own, 3), move(own, 0, 1)
        half = tokens // 2
        far = jnp.concatenate([move(below[:half], 1), move(above[half:], 3)], axis=0)
        pieces = [own, below, above, far, beside]
        pieces += [move(a, 0, 1) for a in (below, above, far)]
    with jax.named_scope("conv"):
        conv = conv_call(conv_kernel, x, h, own_skip, seqs)
        conv = conv.reshape(chans, ctx // plane, plane, seqs, LANES).transpose(2, 1, 3, 0, 4)
        conv = conv.reshape(plane, column, chans, LANES)
    with jax.named_scope("conv_a2a"):
        rows = proj_weight.reshape(chans, width // LANES, LANES).transpose(1, 0, 2)
        rows = jnp.broadcast_to(rows[None], (plane, *rows.shape))
        load = lax.all_to_all(jnp.concatenate([rows, conv], axis=1), PLANE, 0, 0)
    with jax.named_scope("dconv"):
        dconv = dconv_call(place, load, pieces)
    with jax.named_scope("dconv_a2a"):
        dconv = lax.all_to_all(dconv, PLANE, 0, 0)
        dconv = dconv.reshape(plane, ctx // plane, seqs, chans, LANES)
        dconv = dconv.transpose(3, 1, 0, 2, 4).reshape(chans, ctx * seqs, LANES)
    factor = 1.0 / math.sqrt(seqs * tokens * ctx)
    with jax.named_scope("grad_proj"):
        partial = proj_call(place, load, pieces)
        partial, scale, own_skip = lax.optimization_barrier(
            (partial, jnp.full((1,), factor, f32), own_skip)
        )
    with jax.named_scope("grad_taps"):
        grad_taps = taps_call(x, dconv, seqs, scale)
        pairs = []
        for d in range(seqs):
            for c in range(ctx):
                at, x_row = (d * ctx + c) // seqs, c % seqs
                pairs.append((d * ctx + c, x_row * ctx + at))
        held = lax.ppermute(grad_taps, SEQ + POS, pairs)
    with jax.named_scope("grad_in"):
        grad_in = conv_call(back_kernel, dconv, h, own_skip, seqs).transpose(1, 0, 2)
    with jax.named_scope("grad_proj_a2a"):
        partial = lax.all_to_all(partial.reshape(plane, chans, width), PLANE, 0, 0)
        partial, held = lax.optimization_barrier((partial, held))
        grad_proj = jnp.sum(partial.astype(f32), axis=0) * factor
    with jax.named_scope("grad_in_a2a"):
        grad_in = lax.all_to_all(grad_in, POS + SEQ, 0, 0)
    with jax.named_scope("grad_in_out"):
        grad_in = grad_in.reshape(ctx, seqs, chans, LANES).transpose(1, 0, 2, 3)
        grad_in = lax.dot_general(
            mirror(), grad_in.reshape(width, LANES), (((1,), (1,)), ((), ())),
            preferred_element_type=f32,
        ).astype(bf16)
    with jax.named_scope("grad_filter"):
        held = held.reshape(chans, seqs, ctx // seqs, LANES).transpose(1, 0, 2, 3)
        got = []
        for k in range(seqs):
            piece = lax.dynamic_index_in_dim(held, me_dp ^ k, 0, keepdims=False)
            if k:
                piece = lax.ppermute(piece, SEQ, [(i, i ^ k) for i in range(seqs)])
            got.append(piece)
        got = jnp.stack(got)
        grad_filter = jnp.concatenate(
            [lax.dynamic_index_in_dim(got, me_dp ^ m, 0, keepdims=False) for m in range(seqs)],
            axis=0,
        )
        grad_filter = grad_filter.reshape(seqs * chans, -1).astype(f32)
    return (grad_in[None], grad_filter, grad_proj)


def solution(mesh):
    mesh = Mesh(mesh.devices.reshape(2, 2, 2, 4, 4), SEQ + POS)
    placed = (
        P(SEQ, POS, None),
        P(SEQ, POS, None),
        P(SEQ, POS, None),
        P(None, POS),
        P(),
        P(SEQ + POS, None),
    )
    return jax.shard_map(
        on_device,
        mesh=mesh,
        in_specs=placed,
        out_specs=(P(SEQ, POS, None), P(POS, SEQ), P(SEQ + POS, None)),
        check_vma=False,
    )
```

time: 167 us -> 137 us (0.82)
  the two profiles are of different devices: /device:TPU:14 before, /device:TPU:1 now
where the time goes in v3:
time: 137 us
  starting transfers between devices  53.1 us (39%)
  waiting for transfers between devices  41.6 us (30%)
  Pallas kernels  24.3 us (18%)
  local copies, waits for them, and re-layouts  12 us (9%)
  other arithmetic  3.82 us (3%)
    all_to_all x1, waiting for transfers between devices, on_device(): load = lax.all_to_all(load, POS + SEQ, 0, 0)  15.5 us
    all_to_all x1, starting transfers between devices, on_device(): load = lax.all_to_all(load, POS + SEQ, 0, 0)  11.5 us
    ppermute x8, starting transfers between devices, move(): return lax.ppermute(a, COLUMN, column_pairs(step, other))  10.7 us
    pallas_call x2, Pallas kernels, conv_call(): pl.pallas_call(functools.partial(kernel, seqs), grid=(chans // MANY,), in...  10.2 us
    all_to_all x1, waiting for transfers between devices, on_device(): grad_in = lax.all_to_all(grad_in, POS + SEQ, 0, 0)  9.79 us
    all_to_all x1, waiting for transfers between devices, on_device(): load = lax.all_to_all(jnp.concatenate([rows, conv], axis=1), PLANE, 0, 0)  7.26 us
    ppermute x1, starting transfers between devices, on_device(): held = lax.ppermute(grad_taps, SEQ + POS, pairs)  7.16 us
    pallas_call x1, Pallas kernels, taps_call(): pl.pallas_call(functools.partial(taps_kernel, seqs), grid=(chans // MANY,...  7.05 us
  transfers between devices with their start and end apart: 17, of which 7 were waited for; matrix products, arithmetic and copies ran while one was open for 7% of the time, Pallas kernels for 15%

profile of v3, /device:TPU:1, one launch (start us, length us, event | category | flops | bytes accessed | tf_op | source)
XLA Modules:
  0.0 136.8 jit_solution(2775755389058165068)
XLA Ops:
  0.7 1.4 copy.33
  2.1 0.8 fusion.1
  2.9 0.2 maximum_bitcast_fusion
  3.1 0.5 copy.35
  3.6 1.3 copy.36
  4.9 11.5 %all-to-all-start = ((bf16[128,20,128]{2,1,0:T(8,128)(2,1)}), bf16[128,20,128]{2,1,0:T(8,128)(2,1)S(1)}, u32[]{:S(2)}, u32[]{:S(2)}) async-start(bf16[128,20,128]{2,1,0:T(8,128)(2,1)} %copy.36), calls=%async_computation | async-start | bytes 1572864 | tf_op jit(solution)/shard_map/signal_a2a/all_to_all | solution.py:311
  16.5 0.8 dynamic_slice.26.skip_ref
  17.2 15.5 %all-to-all-done = bf16[128,20,128]{2,1,0:T(8,128)(2,1)S(1)} async-done(((bf16[128,20,128]{2,1,0:T(8,128)(2,1)}), bf16[128,20,128]{2,1,0:T(8,128)(2,1)S(1)}, u32[]{:S(2)}, u32[]{:S(2)}) %all-to-all-start) | async-done | bytes 655392 | tf_op jit(solution)/shard_map/signal_a2a/all_to_all | solution.py:311
  32.9 2.7 %collective-permute-start.1 = (bf16[128,2048]{1,0:T(8,128)(2,1)}, bf16[128,2048]{1,0:T(8,128)(2,1)}, u32[]{:S(2)}, u32[]{:S(2)}) collective-permute-start(bf16[128,2048]{1,0:T(8,128)(2,1)} %bitcast.19.refs_0_), channel_id=1, source_target_pairs={{0,80},{32,112},{64,0},{96,32},{16,64},{48,96},{80,16},{112,48},{1... | collective-permute-start | bytes 1572872 | tf_op jit(solution)/shard_map/share_cotangent/ppermute | solution.py:281
  35.6 0.1 copy.56
  35.8 5.0 %conv.1 = bf16[16,128,128]{2,1,0:T(8,128)(2,1)S(1)} custom-call(f32[16]{0:T(128)S(1)} %dynamic_slice.26.skip_ref, bf16[16,128,128]{2,1,0:T(8,128)(2,1)S(1)} %bitcast.87, bf16[16,32,128]{2,1,0:T(8,128)(2,1)S(1)} %bitcast.94), custom_call_target="tpu_custom_call" | custom-call | flops 1048576 | bytes 65536 | tf_op jit(solution)/shard_map/conv/pallas_call | solution.py:162
  40.8 0.6 copy.39
  41.4 0.2 broadcast_in_dim.4
  41.7 1.3 pad_maximum_fusion
  42.9 3.7 %all-to-all-start.1 = ((bf16[16,24,16,128]{3,2,1,0:T(8,128)(2,1)}), bf16[16,24,16,128]{3,2,1,0:T(8,128)(2,1)S(1)}, u32[]{:S(2)}, u32[]{:S(2)}) async-start(bf16[16,24,16,128]{3,2,1,0:T(8,128)(2,1)} %pad_maximum_fusion), calls=%async_computation.1 | async-start | bytes 3145728 | tf_op jit(solution)/shard_map/conv_a2a/all_to_all | solution.py:333
  46.6 0.4 collective-permute-done.refs_1_
  47.1 1.0 slice.19
  48.1 2.7 %collective-permute-start.3 = (bf16[64,2048]{1,0:T(8,128)(2,1)S(1)}, bf16[64,2048]{1,0:T(8,128)(2,1)S(1)}, u32[]{:S(2)}, u32[]{:S(2)}) collective-permute-start(bf16[64,2048]{1,0:T(8,128)(2,1)S(1)} %slice.19), channel_id=1, source_target_pairs={{0,80},{32,112},{64,0},{96,32},{16,64},{48,96},{80,16},{112,48},{1... | collective-permute-start | bytes 786440 | tf_op jit(solution)/shard_map/share_cotangent/ppermute | solution.py:281
  50.8 2.1 %collective-permute-start.4 = (bf16[128,2048]{1,0:T(8,128)(2,1)}, bf16[128,2048]{1,0:T(8,128)(2,1)}, u32[]{:S(2)}, u32[]{:S(2)}) collective-permute-start(bf16[128,2048]{1,0:T(8,128)(2,1)} %bitcast.19.refs_0_), channel_id=1, source_target_pairs={{0,32},{32,0},{64,96},{96,64},{16,48},{48,16},{80,112},{112,80},{1... | collective-permute-start | bytes 1572872 | tf_op jit(solution)/shard_map/share_cotangent/ppermute | solution.py:281
  53.0 0.5 collective-permute-start.6
  53.5 1.1 collective-permute-done.2
  54.5 0.7 constant_dynamic-update-slice_fusion.1
  55.3 0.7 constant_dynamic-update-slice_fusion.refs_3_
  56.0 2.5 %collective-permute-start.7 = (bf16[128,2048]{1,0:T(8,128)(2,1)}, bf16[128,2048]{1,0:T(8,128)(2,1)}, u32[]{:S(2)}, u32[]{:S(2)}) collective-permute-start(bf16[128,2048]{1,0:T(8,128)(2,1)} %constant_dynamic-update-slice_fusion.refs_3_), channel_id=1, source_target_pairs={{0,32},{32,0},{64,96},{96,64},{16,48},{48,16},{80,112},{112,80},{1... | collective-permute-start | bytes 1572872 | tf_op jit(solution)/shard_map/share_cotangent/ppermute | solution.py:281
  58.5 0.1 stack.48.place_ref
  58.6 1.8 %collective-permute-done.7.refs_7_ = bf16[128,2048]{1,0:T(8,128)(2,1)} collective-permute-done((bf16[128,2048]{1,0:T(8,128)(2,1)}, bf16[128,2048]{1,0:T(8,128)(2,1)}, u32[]{:S(2)}, u32[]{:S(2)}) %collective-permute-start.7) | collective-permute-done | bytes 524320 | tf_op jit(solution)/shard_map/share_cotangent/ppermute | solution.py:281
  60.4 7.3 %all-to-all-done.1.c_ref.w_ref = bf16[16,24,16,128]{3,2,1,0:T(8,128)(2,1)S(1)} async-done(((bf16[16,24,16,128]{3,2,1,0:T(8,128)(2,1)}), bf16[16,24,16,128]{3,2,1,0:T(8,128)(2,1)S(1)}, u32[]{:S(2)}, u32[]{:S(2)}) %all-to-all-start.1) | async-done | bytes 1572896 | tf_op jit(solution)/shard_map/conv_a2a/all_to_all | solution.py:333
  67.6 3.7 %dconv.1 = bf16[16,8,16,128]{3,2,1,0:T(8,128)(2,1)S(1)} custom-call(s32[8]{0:T(128)S(1)} %stack.48.place_ref, bf16[16,24,16,128]{3,2,1,0:T(8,128)(2,1)S(1)} %all-to-all-done.1.c_ref.w_ref, bf16[128,2048]{1,0:T(8,128)(2,1)} %bitcast.19.refs_0_, bf16[128,2048]{1,0:T(8,128)(2,1)S(1)} %collective-permute-done.refs_1_, ...), custom_call_target="tpu_custom_call" | custom-call | flops 1073741824 | bytes 6291456 | tf_op jit(solution)/shard_map/dconv/pallas_call | solution.py:238
  71.3 0.8 copy-done.2
  72.1 6.3 %all-to-all-start.2 = ((bf16[16,8,16,128]{3,2,1,0:T(8,128)(2,1)}), bf16[16,8,16,128]{3,2,1,0:T(8,128)(2,1)}, u32[]{:S(2)}, u32[]{:S(2)}) async-start(bf16[16,8,16,128]{3,2,1,0:T(8,128)(2,1)} %copy-done.2), calls=%async_computation.2 | async-start | bytes 1048576 | tf_op jit(solution)/shard_map/dconv_a2a/all_to_all | solution.py:337
  78.4 3.3 %grad_proj.1 = bf16[256,2048]{1,0:T(8,128)(2,1)S(1)} custom-call(s32[8]{0:T(128)S(1)} %stack.48.place_ref, bf16[16,24,16,128]{3,2,1,0:T(8,128)(2,1)S(1)} %all-to-all-done.1.c_ref.w_ref, bf16[128,2048]{1,0:T(8,128)(2,1)} %bitcast.19.refs_0_, bf16[128,2048]{1,0:T(8,128)(2,1)S(1)} %collective-permute-done.refs_1_, ...), custom_call_target="tpu_custom_call" | custom-call | flops 1073741824 | bytes 6291456 | tf_op jit(solution)/shard_map/grad_proj/pallas_call | solution.py:252
  81.7 1.0 copy-done.1
  82.8 5.8 %all-to-all-done.2 = bf16[16,8,16,128]{3,2,1,0:T(8,128)(2,1)} async-done(((bf16[16,8,16,128]{3,2,1,0:T(8,128)(2,1)}), bf16[16,8,16,128]{3,2,1,0:T(8,128)(2,1)}, u32[]{:S(2)}, u32[]{:S(2)}) %all-to-all-start.2) | async-done | bytes 524320 | tf_op jit(solution)/shard_map/dconv_a2a/all_to_all | solution.py:337
  88.6 3.8 %all-to-all-start.4 = ((bf16[16,16,2048]{2,1,0:T(8,128)(2,1)}), bf16[16,16,2048]{2,1,0:T(8,128)(2,1)S(1)}, u32[]{:S(2)}, u32[]{:S(2)}) async-start(bf16[16,16,2048]{2,1,0:T(8,128)(2,1)} %bitcast.91), calls=%async_computation.4 | async-start | bytes 2097152 | tf_op jit(solution)/shard_map/grad_proj_a2a/all_to_all | solution.py:357
  92.4 1.3 copy.40
  93.7 7.0 %grad_taps.1 = bf16[512,128]{1,0:T(8,128)(2,1)S(1)} custom-call(f32[1]{0:T(128)} %constant.116.clone.1.scale_ref, bf16[16,128,128]{2,1,0:T(8,128)(2,1)S(1)} %bitcast.88, bf16[16,128,128]{2,1,0:T(8,128)(2,1)S(1)} %bitcast.89), custom_call_target="tpu_custom_call" | custom-call | flops 1048576 | bytes 65536 | tf_op jit(solution)/shard_map/grad_taps/pallas_call | solution.py:180
  100.8 7.2 %collective-permute-start.8 = (bf16[16,32,128]{2,1,0:T(8,128)(2,1)S(1)}, bf16[16,32,128]{2,1,0:T(8,128)(2,1)S(1)}, u32[]{:S(2)}, u32[]{:S(2)}) collective-permute-start(bf16[16,32,128]{2,1,0:T(8,128)(2,1)S(1)} %bitcast.96), channel_id=1, source_target_pairs={{0,0},{1,32},{2,64},{3,96},{4,1},{5,33},{6,65},{7,97},{8,2},{9,34}... | collective-permute-start | bytes 393224 | tf_op jit(solution)/shard_map/grad_taps/ppermute | solution.py:353
  108.0 5.2 %grad_in.1 = bf16[16,128,128]{2,1,0:T(8,128)(2,1)S(1)} custom-call(f32[16]{0:T(128)S(1)} %dynamic_slice.26.skip_ref, bf16[16,128,128]{2,1,0:T(8,128)(2,1)S(1)} %bitcast.90, bf16[16,32,128]{2,1,0:T(8,128)(2,1)S(1)} %bitcast.95), custom_call_target="tpu_custom_call" | custom-call | flops 1048576 | bytes 65536 | tf_op jit(solution)/shard_map/grad_in/pallas_call | solution.py:162
  113.2 1.1 copy.41
  114.3 7.0 %all-to-all-start.3 = ((bf16[128,16,128]{2,1,0:T(8,128)(2,1)}), bf16[128,16,128]{2,1,0:T(8,128)(2,1)S(1)}, u32[]{:S(2)}, u32[]{:S(2)}) async-start(bf16[128,16,128]{2,1,0:T(8,128)(2,1)} %copy.41), calls=%async_computation.3 | async-start | bytes 1048576 | tf_op jit(solution)/shard_map/grad_in_a2a/all_to_all | solution.py:361
  121.4 1.1 collective-permute-start.9
  122.5 0.8 collective-permute-start.10
  123.3 0.9 collective-permute-start.11
  124.2 0.1 convert_reduce_fusion
  124.4 0.7 broadcast_multiply_fusion
  125.0 9.8 %all-to-all-done.3 = bf16[128,16,128]{2,1,0:T(8,128)(2,1)S(1)} async-done(((bf16[128,16,128]{2,1,0:T(8,128)(2,1)}), bf16[128,16,128]{2,1,0:T(8,128)(2,1)S(1)}, u32[]{:S(2)}, u32[]{:S(2)}) %all-to-all-start.3) | async-done | bytes 524320 | tf_op jit(solution)/shard_map/grad_in_a2a/all_to_all | solution.py:361
  134.9 1.1 fusion
  136.1 0.7 maximum_convert_fusion
  (31 shorter events, 0.5 us)
Async XLA Ops:
  0.6 1.4 %copy-start = (bf16[2048,128]{1,0:T(8,128)(2,1)S(1)}, bf16[2048,128]{1,0:T(8,128)(2,1)}, u32[]{:S(2)}) copy-start(bf16[2048,128]{1,0:T(8,128)(2,1)} %param.9) | copy-start | bytes 1572868
  3.6 29.3 %copy-start.3 = (bf16[16,2048]{1,0:T(8,128)(2,1)S(1)}, bf16[16,2048]{1,0:T(8,128)(2,1)}, u32[]{:S(2)}) copy-start(bf16[16,2048]{1,0:T(8,128)(2,1)} %param.11) | copy-start | bytes 196612
  4.9 27.7 %all-to-all-start = ((bf16[128,20,128]{2,1,0:T(8,128)(2,1)}), bf16[128,20,128]{2,1,0:T(8,128)(2,1)S(1)}, u32[]{:S(2)}, u32[]{:S(2)}) async-start(bf16[128,20,128]{2,1,0:T(8,128)(2,1)} %copy.36), calls=%async_computation | async-start | bytes 1572864 | tf_op jit(solution)/shard_map/signal_a2a/all_to_all | solution.py:311
  32.8 14.2 %collective-permute-start = (bf16[128,2048]{1,0:T(8,128)(2,1)}, bf16[128,2048]{1,0:T(8,128)(2,1)S(1)}, u32[]{:S(2)}, u32[]{:S(2)}) collective-permute-start(bf16[128,2048]{1,0:T(8,128)(2,1)} %bitcast.19.refs_0_), channel_id=1, source_target_pairs={{0,64},{32,96},{64,16},{96,48},{16,80},{48,112},{80,0},{112,32},{1... | collective-permute-start | bytes 1572872 | tf_op jit(solution)/shard_map/share_cotangent/ppermute | solution.py:281
  32.9 14.2 %collective-permute-start.1 = (bf16[128,2048]{1,0:T(8,128)(2,1)}, bf16[128,2048]{1,0:T(8,128)(2,1)}, u32[]{:S(2)}, u32[]{:S(2)}) collective-permute-start(bf16[128,2048]{1,0:T(8,128)(2,1)} %bitcast.19.refs_0_), channel_id=1, source_target_pairs={{0,80},{32,112},{64,0},{96,32},{16,64},{48,96},{80,16},{112,48},{1... | collective-permute-start | bytes 1572872 | tf_op jit(solution)/shard_map/share_cotangent/ppermute | solution.py:281
  42.9 24.7 %all-to-all-start.1 = ((bf16[16,24,16,128]{3,2,1,0:T(8,128)(2,1)}), bf16[16,24,16,128]{3,2,1,0:T(8,128)(2,1)S(1)}, u32[]{:S(2)}, u32[]{:S(2)}) async-start(bf16[16,24,16,128]{3,2,1,0:T(8,128)(2,1)} %pad_maximum_fusion), calls=%async_computation.1 | async-start | bytes 3145728 | tf_op jit(solution)/shard_map/conv_a2a/all_to_all | solution.py:333
  47.0 7.5 %collective-permute-start.2 = (bf16[64,2048]{1,0:T(8,128)(2,1)S(1)}, bf16[64,2048]{1,0:T(8,128)(2,1)S(1)}, u32[]{:S(2)}, u32[]{:S(2)}) collective-permute-start(bf16[64,2048]{1,0:T(8,128)(2,1)S(1)} %slice.18), channel_id=1, source_target_pairs={{0,64},{32,96},{64,16},{96,48},{16,80},{48,112},{80,0},{112,32},{1... | collective-permute-start | bytes 786440 | tf_op jit(solution)/shard_map/share_cotangent/ppermute | solution.py:281
  48.1 7.2 %collective-permute-start.3 = (bf16[64,2048]{1,0:T(8,128)(2,1)S(1)}, bf16[64,2048]{1,0:T(8,128)(2,1)S(1)}, u32[]{:S(2)}, u32[]{:S(2)}) collective-permute-start(bf16[64,2048]{1,0:T(8,128)(2,1)S(1)} %slice.19), channel_id=1, source_target_pairs={{0,80},{32,112},{64,0},{96,32},{16,64},{48,96},{80,16},{112,48},{1... | collective-permute-start | bytes 786440 | tf_op jit(solution)/shard_map/share_cotangent/ppermute | solution.py:281
  50.8 7.7 %collective-permute-start.4 = (bf16[128,2048]{1,0:T(8,128)(2,1)}, bf16[128,2048]{1,0:T(8,128)(2,1)}, u32[]{:S(2)}, u32[]{:S(2)}) collective-permute-start(bf16[128,2048]{1,0:T(8,128)(2,1)} %bitcast.19.refs_0_), channel_id=1, source_target_pairs={{0,32},{32,0},{64,96},{96,64},{16,48},{48,16},{80,112},{112,80},{1... | collective-permute-start | bytes 1572872 | tf_op jit(solution)/shard_map/share_cotangent/ppermute | solution.py:281
  53.0 5.6 %collective-permute-start.5 = (bf16[128,2048]{1,0:T(8,128)(2,1)S(1)}, bf16[128,2048]{1,0:T(8,128)(2,1)}, u32[]{:S(2)}, u32[]{:S(2)}) collective-permute-start(bf16[128,2048]{1,0:T(8,128)(2,1)S(1)} %collective-permute-done.refs_1_), channel_id=1, source_target_pairs={{0,32},{32,0},{64,96},{96,64},{16,48},{48,16},{80,112},{112,80},{1... | collective-permute-start | bytes 1572872 | tf_op jit(solution)/shard_map/share_cotangent/ppermute | solution.py:281
  53.0 5.6 %collective-permute-start.6 = (bf16[128,2048]{1,0:T(8,128)(2,1)}, bf16[128,2048]{1,0:T(8,128)(2,1)}, u32[]{:S(2)}, u32[]{:S(2)}) collective-permute-start(bf16[128,2048]{1,0:T(8,128)(2,1)} %collective-permute-done.1.refs_2_), channel_id=1, source_target_pairs={{0,32},{32,0},{64,96},{96,64},{16,48},{48,16},{80,112},{112,80},{1... | collective-permute-start | bytes 1572872 | tf_op jit(solution)/shard_map/share_cotangent/ppermute | solution.py:281
  56.0 4.4 %collective-permute-start.7 = (bf16[128,2048]{1,0:T(8,128)(2,1)}, bf16[128,2048]{1,0:T(8,128)(2,1)}, u32[]{:S(2)}, u32[]{:S(2)}) collective-permute-start(bf16[128,2048]{1,0:T(8,128)(2,1)} %constant_dynamic-update-slice_fusion.refs_3_), channel_id=1, source_target_pairs={{0,32},{32,0},{64,96},{96,64},{16,48},{48,16},{80,112},{112,80},{1... | collective-permute-start | bytes 1572872 | tf_op jit(solution)/shard_map/share_cotangent/ppermute | solution.py:281
  71.3 0.8 copy-start.2
  72.1 16.4 %all-to-all-start.2 = ((bf16[16,8,16,128]{3,2,1,0:T(8,128)(2,1)}), bf16[16,8,16,128]{3,2,1,0:T(8,128)(2,1)}, u32[]{:S(2)}, u32[]{:S(2)}) async-start(bf16[16,8,16,128]{3,2,1,0:T(8,128)(2,1)} %copy-done.2), calls=%async_computation.2 | async-start | bytes 1048576 | tf_op jit(solution)/shard_map/dconv_a2a/all_to_all | solution.py:337
  81.7 1.0 copy-start.1
  88.6 25.7 %all-to-all-start.4 = ((bf16[16,16,2048]{2,1,0:T(8,128)(2,1)}), bf16[16,16,2048]{2,1,0:T(8,128)(2,1)S(1)}, u32[]{:S(2)}, u32[]{:S(2)}) async-start(bf16[16,16,2048]{2,1,0:T(8,128)(2,1)} %bitcast.91), calls=%async_computation.4 | async-start | bytes 2097152 | tf_op jit(solution)/shard_map/grad_proj_a2a/all_to_all | solution.py:357
  100.8 20.5 %collective-permute-start.8 = (bf16[16,32,128]{2,1,0:T(8,128)(2,1)S(1)}, bf16[16,32,128]{2,1,0:T(8,128)(2,1)S(1)}, u32[]{:S(2)}, u32[]{:S(2)}) collective-permute-start(bf16[16,32,128]{2,1,0:T(8,128)(2,1)S(1)} %bitcast.96), channel_id=1, source_target_pairs={{0,0},{1,32},{2,64},{3,96},{4,1},{5,33},{6,65},{7,97},{8,2},{9,34}... | collective-permute-start | bytes 393224 | tf_op jit(solution)/shard_map/grad_taps/ppermute | solution.py:353
  114.3 20.5 %all-to-all-start.3 = ((bf16[128,16,128]{2,1,0:T(8,128)(2,1)}), bf16[128,16,128]{2,1,0:T(8,128)(2,1)S(1)}, u32[]{:S(2)}, u32[]{:S(2)}) async-start(bf16[128,16,128]{2,1,0:T(8,128)(2,1)} %copy.41), calls=%async_computation.3 | async-start | bytes 1048576 | tf_op jit(solution)/shard_map/grad_in_a2a/all_to_all | solution.py:361
  121.4 14.6 %collective-permute-start.9 = (bf16[16,8,128]{2,1,0:T(8,128)(2,1)S(1)}, bf16[16,8,128]{2,1,0:T(8,128)(2,1)S(1)}, u32[]{:S(2)}, u32[]{:S(2)}) collective-permute-start(bf16[16,8,128]{2,1,0:T(8,128)(2,1)S(1)} %get-tuple-element.24), channel_id=1, source_target_pairs={{0,32},{32,0},{64,96},{96,64},{1,33},{33,1},{65,97},{97,65},{2,34}... | collective-permute-start | bytes 98312 | tf_op jit(solution)/shard_map/grad_filter/ppermute | solution.py:374
  122.5 13.5 %collective-permute-start.10 = (bf16[16,8,128]{2,1,0:T(8,128)(2,1)S(1)}, bf16[16,8,128]{2,1,0:T(8,128)(2,1)S(1)}, u32[]{:S(2)}, u32[]{:S(2)}) collective-permute-start(bf16[16,8,128]{2,1,0:T(8,128)(2,1)S(1)} %get-tuple-element.23), channel_id=1, source_target_pairs={{0,64},{32,96},{64,0},{96,32},{1,65},{33,97},{65,1},{97,33},{2,66}... | collective-permute-start | bytes 98312 | tf_op jit(solution)/shard_map/grad_filter/ppermute | solution.py:374
  123.3 12.7 %collective-permute-start.11 = (bf16[16,8,128]{2,1,0:T(8,128)(2,1)S(1)}, bf16[16,8,128]{2,1,0:T(8,128)(2,1)S(1)}, u32[]{:S(2)}, u32[]{:S(2)}) collective-permute-start(bf16[16,8,128]{2,1,0:T(8,128)(2,1)S(1)} %get-tuple-element.22), channel_id=1, source_target_pairs={{0,96},{32,64},{64,32},{96,0},{1,97},{33,65},{65,33},{97,1},{2,98}... | collective-permute-start | bytes 98312 | tf_op jit(solution)/shard_map/grad_filter/ppermute | solution.py:374

commit v4 on v3

--- a/solution.py
+++ b/solution.py
@@ -306,9 +306,10 @@
         taps = filter_taps.reshape(seqs, ctx, seqs, chans // seqs, tokens)
         taps = lax.dynamic_index_in_dim(taps, me_dp, 2, keepdims=False)
         load = jnp.concatenate([parts, taps], axis=2).transpose(1, 0, 2, 3)
-        load = load.reshape(ctx * seqs, -1, LANES)
+        load = load.reshape(ctx * seqs, -1, chans // seqs, LANES)
     with jax.named_scope("signal_a2a"):
         load = lax.all_to_all(load, POS + SEQ, 0, 0)
+        load = load.reshape(ctx * seqs, -1, LANES)
     with jax.named_scope("signal_in"):
         x = load[:, :chans].transpose(1, 0, 2)
         h = load[:, chans:].reshape(ctx, seqs, chans // seqs, LANES).transpose(1, 2, 0, 3)
@@ -316,7 +317,7 @@
         first = (me_dp * ctx + me_ctx) * chans
         own_skip = lax.dynamic_slice_in_dim(skip, first, chans)
     with jax.named_scope("share_cotangent"):
-        own, h = lax.optimization_barrier((out_grad[0], h))
+        own = out_grad[0]
         place = places()
         below, above, beside = move(own, 1), move(own, 3), move(own, 0, 1)
         half = tokens // 2
@@ -359,12 +360,6 @@
         grad_proj = jnp.sum(partial.astype(f32), axis=0) * factor
     with jax.named_scope("grad_in_a2a"):
         grad_in = lax.all_to_all(grad_in, POS + SEQ, 0, 0)
-    with jax.named_scope("grad_in_out"):
-        grad_in = grad_in.reshape(ctx, seqs, chans, LANES).transpose(1, 0, 2, 3)
-        grad_in = lax.dot_general(
-            mirror(), grad_in.reshape(width, LANES), (((1,), (1,)), ((), ())),
-            preferred_element_type=f32,
-        ).astype(bf16)
     with jax.named_scope("grad_filter"):
         held = held.reshape(chans, seqs, ctx // seqs, LANES).transpose(1, 0, 2, 3)
         got = []
@@ -379,6 +374,13 @@
             axis=0,
         )
         grad_filter = grad_filter.reshape(seqs * chans, -1).astype(f32)
+        flip, grad_filter = lax.optimization_barrier((mirror(), grad_filter))
+    with jax.named_scope("grad_in_out"):
+        grad_in = grad_in.reshape(ctx, seqs, chans, LANES).transpose(1, 0, 2, 3)
+        grad_in = lax.dot_general(
+            flip, grad_in.reshape(width, LANES), (((1,), (1,)), ((), ())),
+            preferred_element_type=f32,
+        ).astype(bf16)
     return (grad_in[None], grad_filter, grad_proj)
 
 

time: 137 us -> 134 us (0.978)
  starting transfers between devices: 53.1 us -> 51.1 us
  waiting for transfers between devices: 41.6 us -> 39.7 us
    all_to_all x1, waiting for transfers between devices: 15.5 us -> 10.7 us  [on_device(): load = lax.all_to_all(load, POS + SEQ, 0, 0)]
    all_to_all x1, waiting for transfers between devices: 7.26 us -> 9.64 us  [on_device(): load = lax.all_to_all(jnp.concatenate([rows, conv], axis=1), PLANE, 0, 0)]
    all_to_all x1, starting transfers between devices: 6.3 us -> 4.49 us  [on_device(): dconv = lax.all_to_all(dconv, PLANE, 0, 0)]
    unnamed x11 -> x10, local copies, waits for them, and re-layouts: 4.03 us -> 3.89 us
  transfers between devices with their start and end apart: 17 -> 17, of which waited for: 7 -> 6; matrix products, arithmetic and copies ran while one was open for 7% -> 7% of each run, Pallas kernels for 15% -> 15%
where the time goes in v4:
time: 134 us; the launch traced here: 133 us
  starting transfers between devices  51.1 us (38%)
  waiting for transfers between devices  39.7 us (30%)
  Pallas kernels  24.3 us (18%)
  local copies, waits for them, and re-layouts  11.9 us (9%)
  other arithmetic  3.83 us (3%)
    all_to_all x1, starting transfers between devices, on_device(): load = lax.all_to_all(load, POS + SEQ, 0, 0)  11.5 us
    all_to_all x1, waiting for transfers between devices, on_device(): load = lax.all_to_all(load, POS + SEQ, 0, 0)  10.7 us
    pallas_call x2, Pallas kernels, conv_call(): pl.pallas_call(functools.partial(kernel, seqs), grid=(chans // MANY,), in...  10.2 us
    ppermute x8, starting transfers between devices, move(): return lax.ppermute(a, COLUMN, column_pairs(step, other))  9.95 us
    all_to_all x1, waiting for transfers between devices, on_device(): grad_in = lax.all_to_all(grad_in, POS + SEQ, 0, 0)  9.79 us
    all_to_all x1, waiting for transfers between devices, on_device(): load = lax.all_to_all(jnp.concatenate([rows, conv], axis=1), PLANE, 0, 0)  9.64 us
    ppermute x1, starting transfers between devices, on_device(): held = lax.ppermute(grad_taps, SEQ + POS, pairs)  7.69 us
    all_to_all x1, starting transfers between devices, on_device(): grad_in = lax.all_to_all(grad_in, POS + SEQ, 0, 0)  7.06 us
  transfers between devices with their start and end apart: 17, of which 6 were waited for; matrix products, arithmetic and copies ran while one was open for 7% of the time, Pallas kernels for 15%

profile of v4, /device:TPU:1, one launch (start us, length us, event | category | flops | bytes accessed | tf_op | source)
XLA Modules:
  0.0 132.9 jit_solution(10242832371994106036)
XLA Ops:
  0.7 1.4 %copy.43 = bf16[1,128,2048]{1,2,0:T(8,128)(2,1)S(1)} copy(bf16[1,128,2048]{2,1,0:T(8,128)(2,1)} %param.6) | data formatting | bytes 1048576 | tf_op args[0]
  2.1 0.8 fusion.1
  2.9 0.2 maximum_bitcast_fusion
  3.1 0.5 copy.46
  3.6 1.4 %copy.47 = bf16[128,5,4,128]{3,2,1,0:T(4,128)(2,1)} copy(bf16[128,5,4,128]{3,0,2,1:T(8,128)(2,1)S(1)} %bitcast.96) | data formatting | bytes 1310720 | tf_op jit(solution)/shard_map/signal/reshape | solution.py:309
  5.0 11.5 %all-to-all-start = ((bf16[128,5,4,128]{3,2,1,0:T(4,128)(2,1)}), bf16[128,5,4,128]{3,2,1,0:T(4,128)(2,1)S(1)}, u32[]{:S(2)}, u32[]{:S(2)}) async-start(bf16[128,5,4,128]{3,2,1,0:T(4,128)(2,1)} %copy.47), calls=%async_computation | async-start | bytes 1310720 | tf_op jit(solution)/shard_map/signal_a2a/all_to_all | solution.py:311
  16.5 1.6 %collective-permute-start = (bf16[128,2048]{1,0:T(8,128)(2,1)}, bf16[128,2048]{1,0:T(8,128)(2,1)S(1)}, u32[]{:S(2)}, u32[]{:S(2)}) collective-permute-start(bf16[128,2048]{1,0:T(8,128)(2,1)} %bitcast.26.refs_0_), channel_id=1, source_target_pairs={{0,64},{32,96},{64,16},{96,48},{16,80},{48,112},{80,0},{112,32},{1... | collective-permute-start | bytes 1572872 | tf_op jit(solution)/shard_map/share_cotangent/ppermute | solution.py:281
  18.1 1.8 %collective-permute-start.1 = (bf16[128,2048]{1,0:T(8,128)(2,1)}, bf16[128,2048]{1,0:T(8,128)(2,1)}, u32[]{:S(2)}, u32[]{:S(2)}) collective-permute-start(bf16[128,2048]{1,0:T(8,128)(2,1)} %bitcast.26.refs_0_), channel_id=1, source_target_pairs={{0,80},{32,112},{64,0},{96,32},{16,64},{48,96},{80,16},{112,48},{1... | collective-permute-start | bytes 1572872 | tf_op jit(solution)/shard_map/share_cotangent/ppermute | solution.py:281
  19.9 0.8 dynamic_slice.26.skip_ref
  20.7 10.7 %all-to-all-done = bf16[128,5,4,128]{3,2,1,0:T(4,128)(2,1)S(1)} async-done(((bf16[128,5,4,128]{3,2,1,0:T(4,128)(2,1)}), bf16[128,5,4,128]{3,2,1,0:T(4,128)(2,1)S(1)}, u32[]{:S(2)}, u32[]{:S(2)}) %all-to-all-start) | async-done | bytes 655392 | tf_op jit(solution)/shard_map/signal_a2a/all_to_all | solution.py:311
  31.4 0.1 copy.48
  31.6 5.0 %conv.1 = bf16[16,128,128]{2,1,0:T(8,128)(2,1)S(1)} custom-call(f32[16]{0:T(128)S(1)} %dynamic_slice.26.skip_ref, bf16[16,128,128]{2,1,0:T(8,128)(2,1)S(1)} %slice_bitcast_fusion.x_ref, bf16[16,32,128]{2,1,0:T(8,128)(2,1)S(1)} %bitcast.91), custom_call_target="tpu_custom_call" | custom-call | flops 1048576 | bytes 65536 | tf_op jit(solution)/shard_map/conv/pallas_call | solution.py:162
  36.6 0.6 copy.50
  37.3 0.2 broadcast_in_dim.4
  37.5 1.3 pad_maximum_fusion
  38.7 3.7 %all-to-all-start.1 = ((bf16[16,24,16,128]{3,2,1,0:T(8,128)(2,1)}), bf16[16,24,16,128]{3,2,1,0:T(8,128)(2,1)S(1)}, u32[]{:S(2)}, u32[]{:S(2)}) async-start(bf16[16,24,16,128]{3,2,1,0:T(8,128)(2,1)} %pad_maximum_fusion), calls=%async_computation.1 | async-start | bytes 3145728 | tf_op jit(solution)/shard_map/conv_a2a/all_to_all | solution.py:334
  42.5 0.2 collective-permute-start.2
  42.7 1.0 slice.19
  43.7 2.6 %collective-permute-start.3 = (bf16[64,2048]{1,0:T(8,128)(2,1)S(1)}, bf16[64,2048]{1,0:T(8,128)(2,1)S(1)}, u32[]{:S(2)}, u32[]{:S(2)}) collective-permute-start(bf16[64,2048]{1,0:T(8,128)(2,1)S(1)} %slice.19), channel_id=1, source_target_pairs={{0,80},{32,112},{64,0},{96,32},{16,64},{48,96},{80,16},{112,48},{1... | collective-permute-start | bytes 786440 | tf_op jit(solution)/shard_map/share_cotangent/ppermute | solution.py:281
  46.3 1.4 %collective-permute-start.4 = (bf16[128,2048]{1,0:T(8,128)(2,1)}, bf16[128,2048]{1,0:T(8,128)(2,1)}, u32[]{:S(2)}, u32[]{:S(2)}) collective-permute-start(bf16[128,2048]{1,0:T(8,128)(2,1)} %bitcast.26.refs_0_), channel_id=1, source_target_pairs={{0,32},{32,0},{64,96},{96,64},{16,48},{48,16},{80,112},{112,80},{1... | collective-permute-start | bytes 1572872 | tf_op jit(solution)/shard_map/share_cotangent/ppermute | solution.py:281
  47.7 0.5 collective-permute-start.6
  48.2 2.5 %collective-permute-done.2 = bf16[64,2048]{1,0:T(8,128)(2,1)S(1)} collective-permute-done((bf16[64,2048]{1,0:T(8,128)(2,1)S(1)}, bf16[64,2048]{1,0:T(8,128)(2,1)S(1)}, u32[]{:S(2)}, u32[]{:S(2)}) %collective-permute-start.2) | collective-permute-done | bytes 262176 | tf_op jit(solution)/shard_map/share_cotangent/ppermute | solution.py:281
  50.7 0.7 constant_dynamic-update-slice_fusion.1
  51.4 0.7 constant_dynamic-update-slice_fusion.refs_3_
  52.2 1.8 %collective-permute-start.7 = (bf16[128,2048]{1,0:T(8,128)(2,1)}, bf16[128,2048]{1,0:T(8,128)(2,1)}, u32[]{:S(2)}, u32[]{:S(2)}) collective-permute-start(bf16[128,2048]{1,0:T(8,128)(2,1)} %constant_dynamic-update-slice_fusion.refs_3_), channel_id=1, source_target_pairs={{0,32},{32,0},{64,96},{96,64},{16,48},{48,16},{80,112},{112,80},{1... | collective-permute-start | bytes 1572872 | tf_op jit(solution)/shard_map/share_cotangent/ppermute | solution.py:281
  54.0 1.8 %collective-permute-done.7.refs_7_ = bf16[128,2048]{1,0:T(8,128)(2,1)} collective-permute-done((bf16[128,2048]{1,0:T(8,128)(2,1)}, bf16[128,2048]{1,0:T(8,128)(2,1)}, u32[]{:S(2)}, u32[]{:S(2)}) %collective-permute-start.7) | collective-permute-done | bytes 524320 | tf_op jit(solution)/shard_map/share_cotangent/ppermute | solution.py:281
  55.8 9.6 %all-to-all-done.1.c_ref.w_ref = bf16[16,24,16,128]{3,2,1,0:T(8,128)(2,1)S(1)} async-done(((bf16[16,24,16,128]{3,2,1,0:T(8,128)(2,1)}), bf16[16,24,16,128]{3,2,1,0:T(8,128)(2,1)S(1)}, u32[]{:S(2)}, u32[]{:S(2)}) %all-to-all-start.1) | async-done | bytes 1572896 | tf_op jit(solution)/shard_map/conv_a2a/all_to_all | solution.py:334
  65.5 3.7 %dconv.1 = bf16[16,8,16,128]{3,2,1,0:T(8,128)(2,1)S(1)} custom-call(s32[8]{0:T(128)S(1)} %stack.48.place_ref, bf16[16,24,16,128]{3,2,1,0:T(8,128)(2,1)S(1)} %all-to-all-done.1.c_ref.w_ref, bf16[128,2048]{1,0:T(8,128)(2,1)} %bitcast.26.refs_0_, bf16[128,2048]{1,0:T(8,128)(2,1)S(1)} %collective-permute-done.refs_1_, ...), custom_call_target="tpu_custom_call" | custom-call | flops 1073741824 | bytes 6291456 | tf_op jit(solution)/shard_map/dconv/pallas_call | solution.py:238
  69.2 0.8 copy-done.2
  70.0 4.5 %all-to-all-start.3 = ((bf16[16,8,16,128]{3,2,1,0:T(8,128)(2,1)}), bf16[16,8,16,128]{3,2,1,0:T(8,128)(2,1)}, u32[]{:S(2)}, u32[]{:S(2)}) async-start(bf16[16,8,16,128]{3,2,1,0:T(8,128)(2,1)} %copy-done.2), calls=%async_computation.3 | async-start | bytes 1048576 | tf_op jit(solution)/shard_map/dconv_a2a/all_to_all | solution.py:338
  74.5 3.3 %grad_proj.1 = bf16[256,2048]{1,0:T(8,128)(2,1)S(1)} custom-call(s32[8]{0:T(128)S(1)} %stack.48.place_ref, bf16[16,24,16,128]{3,2,1,0:T(8,128)(2,1)S(1)} %all-to-all-done.1.c_ref.w_ref, bf16[128,2048]{1,0:T(8,128)(2,1)} %bitcast.26.refs_0_, bf16[128,2048]{1,0:T(8,128)(2,1)S(1)} %collective-permute-done.refs_1_, ...), custom_call_target="tpu_custom_call" | custom-call | flops 1073741824 | bytes 6291456 | tf_op jit(solution)/shard_map/grad_proj/pallas_call | solution.py:252
  77.8 1.0 copy-done.1
  78.8 5.3 %all-to-all-done.3 = bf16[16,8,16,128]{3,2,1,0:T(8,128)(2,1)} async-done(((bf16[16,8,16,128]{3,2,1,0:T(8,128)(2,1)}), bf16[16,8,16,128]{3,2,1,0:T(8,128)(2,1)}, u32[]{:S(2)}, u32[]{:S(2)}) %all-to-all-start.3) | async-done | bytes 524320 | tf_op jit(solution)/shard_map/dconv_a2a/all_to_all | solution.py:338
  84.1 3.8 %all-to-all-start.2 = ((bf16[16,16,2048]{2,1,0:T(8,128)(2,1)}), bf16[16,16,2048]{2,1,0:T(8,128)(2,1)S(1)}, u32[]{:S(2)}, u32[]{:S(2)}) async-start(bf16[16,16,2048]{2,1,0:T(8,128)(2,1)} %bitcast.88), calls=%async_computation.2 | async-start | bytes 2097152 | tf_op jit(solution)/shard_map/grad_proj_a2a/all_to_all | solution.py:358
  87.9 1.3 copy.51
  89.2 7.0 %grad_taps.1 = bf16[512,128]{1,0:T(8,128)(2,1)S(1)} custom-call(f32[1]{0:T(128)} %constant.116.clone.1.scale_ref, bf16[16,128,128]{2,1,0:T(8,128)(2,1)S(1)} %slice_bitcast_fusion.x_ref, bf16[16,128,128]{2,1,0:T(8,128)(2,1)S(1)} %bitcast.86), custom_call_target="tpu_custom_call" | custom-call | flops 1048576 | bytes 65536 | tf_op jit(solution)/shard_map/grad_taps/pallas_call | solution.py:180
  96.3 7.7 %collective-permute-start.8 = (bf16[16,32,128]{2,1,0:T(8,128)(2,1)S(1)}, bf16[16,32,128]{2,1,0:T(8,128)(2,1)S(1)}, u32[]{:S(2)}, u32[]{:S(2)}) collective-permute-start(bf16[16,32,128]{2,1,0:T(8,128)(2,1)S(1)} %bitcast.93), channel_id=1, source_target_pairs={{0,0},{1,32},{2,64},{3,96},{4,1},{5,33},{6,65},{7,97},{8,2},{9,34}... | collective-permute-start | bytes 393224 | tf_op jit(solution)/shard_map/grad_taps/ppermute | solution.py:354
  104.0 5.2 %grad_in.1 = bf16[16,128,128]{2,1,0:T(8,128)(2,1)S(1)} custom-call(f32[16]{0:T(128)S(1)} %dynamic_slice.26.skip_ref, bf16[16,128,128]{2,1,0:T(8,128)(2,1)S(1)} %bitcast.87, bf16[16,32,128]{2,1,0:T(8,128)(2,1)S(1)} %bitcast.92), custom_call_target="tpu_custom_call" | custom-call | flops 1048576 | bytes 65536 | tf_op jit(solution)/shard_map/grad_in/pallas_call | solution.py:162
  109.2 1.1 copy.52
  110.4 7.1 %all-to-all-start.4 = ((bf16[128,16,128]{2,1,0:T(8,128)(2,1)}), bf16[128,16,128]{2,1,0:T(8,128)(2,1)S(1)}, u32[]{:S(2)}, u32[]{:S(2)}) async-start(bf16[128,16,128]{2,1,0:T(8,128)(2,1)} %copy.52), calls=%async_computation.4 | async-start | bytes 1048576 | tf_op jit(solution)/shard_map/grad_in_a2a/all_to_all | solution.py:362
  117.5 1.1 collective-permute-start.9
  118.6 0.8 collective-permute-start.10
  119.4 0.9 collective-permute-start.11
  120.4 0.1 convert_reduce_fusion
  120.5 0.7 broadcast_multiply_fusion
  121.2 9.8 %all-to-all-done.4 = bf16[128,16,128]{2,1,0:T(8,128)(2,1)S(1)} async-done(((bf16[128,16,128]{2,1,0:T(8,128)(2,1)}), bf16[128,16,128]{2,1,0:T(8,128)(2,1)S(1)}, u32[]{:S(2)}, u32[]{:S(2)}) %all-to-all-start.4) | async-done | bytes 524320 | tf_op jit(solution)/shard_map/grad_in_a2a/all_to_all | solution.py:362
  131.1 0.7 maximum_convert_fusion
  131.8 1.1 fusion
  (32 shorter events, 0.4 us)
Async XLA Ops:
  0.6 1.4 %copy-start = (bf16[2048,128]{1,0:T(8,128)(2,1)S(1)}, bf16[2048,128]{1,0:T(8,128)(2,1)}, u32[]{:S(2)}) copy-start(bf16[2048,128]{1,0:T(8,128)(2,1)} %param.9) | copy-start | bytes 1572868
  3.6 17.0 %copy-start.3 = (bf16[16,2048]{1,0:T(8,128)(2,1)S(1)}, bf16[16,2048]{1,0:T(8,128)(2,1)}, u32[]{:S(2)}) copy-start(bf16[16,2048]{1,0:T(8,128)(2,1)} %param.11) | copy-start | bytes 196612
  5.0 26.4 %all-to-all-start = ((bf16[128,5,4,128]{3,2,1,0:T(4,128)(2,1)}), bf16[128,5,4,128]{3,2,1,0:T(4,128)(2,1)S(1)}, u32[]{:S(2)}, u32[]{:S(2)}) async-start(bf16[128,5,4,128]{3,2,1,0:T(4,128)(2,1)} %copy.47), calls=%async_computation | async-start | bytes 1310720 | tf_op jit(solution)/shard_map/signal_a2a/all_to_all | solution.py:311
  16.5 26.0 %collective-permute-start = (bf16[128,2048]{1,0:T(8,128)(2,1)}, bf16[128,2048]{1,0:T(8,128)(2,1)S(1)}, u32[]{:S(2)}, u32[]{:S(2)}) collective-permute-start(bf16[128,2048]{1,0:T(8,128)(2,1)} %bitcast.26.refs_0_), channel_id=1, source_target_pairs={{0,64},{32,96},{64,16},{96,48},{16,80},{48,112},{80,0},{112,32},{1... | collective-permute-start | bytes 1572872 | tf_op jit(solution)/shard_map/share_cotangent/ppermute | solution.py:281
  18.1 24.7 %collective-permute-start.1 = (bf16[128,2048]{1,0:T(8,128)(2,1)}, bf16[128,2048]{1,0:T(8,128)(2,1)}, u32[]{:S(2)}, u32[]{:S(2)}) collective-permute-start(bf16[128,2048]{1,0:T(8,128)(2,1)} %bitcast.26.refs_0_), channel_id=1, source_target_pairs={{0,80},{32,112},{64,0},{96,32},{16,64},{48,96},{80,16},{112,48},{1... | collective-permute-start | bytes 1572872 | tf_op jit(solution)/shard_map/share_cotangent/ppermute | solution.py:281
  38.7 26.7 %all-to-all-start.1 = ((bf16[16,24,16,128]{3,2,1,0:T(8,128)(2,1)}), bf16[16,24,16,128]{3,2,1,0:T(8,128)(2,1)S(1)}, u32[]{:S(2)}, u32[]{:S(2)}) async-start(bf16[16,24,16,128]{3,2,1,0:T(8,128)(2,1)} %pad_maximum_fusion), calls=%async_computation.1 | async-start | bytes 3145728 | tf_op jit(solution)/shard_map/conv_a2a/all_to_all | solution.py:334
  42.5 8.2 %collective-permute-start.2 = (bf16[64,2048]{1,0:T(8,128)(2,1)S(1)}, bf16[64,2048]{1,0:T(8,128)(2,1)S(1)}, u32[]{:S(2)}, u32[]{:S(2)}) collective-permute-start(bf16[64,2048]{1,0:T(8,128)(2,1)S(1)} %slice.18), channel_id=1, source_target_pairs={{0,64},{32,96},{64,16},{96,48},{16,80},{48,112},{80,0},{112,32},{1... | collective-permute-start | bytes 786440 | tf_op jit(solution)/shard_map/share_cotangent/ppermute | solution.py:281
  43.7 7.7 %collective-permute-start.3 = (bf16[64,2048]{1,0:T(8,128)(2,1)S(1)}, bf16[64,2048]{1,0:T(8,128)(2,1)S(1)}, u32[]{:S(2)}, u32[]{:S(2)}) collective-permute-start(bf16[64,2048]{1,0:T(8,128)(2,1)S(1)} %slice.19), channel_id=1, source_target_pairs={{0,80},{32,112},{64,0},{96,32},{16,64},{48,96},{80,16},{112,48},{1... | collective-permute-start | bytes 786440 | tf_op jit(solution)/shard_map/share_cotangent/ppermute | solution.py:281
  46.3 7.7 %collective-permute-start.4 = (bf16[128,2048]{1,0:T(8,128)(2,1)}, bf16[128,2048]{1,0:T(8,128)(2,1)}, u32[]{:S(2)}, u32[]{:S(2)}) collective-permute-start(bf16[128,2048]{1,0:T(8,128)(2,1)} %bitcast.26.refs_0_), channel_id=1, source_target_pairs={{0,32},{32,0},{64,96},{96,64},{16,48},{48,16},{80,112},{112,80},{1... | collective-permute-start | bytes 1572872 | tf_op jit(solution)/shard_map/share_cotangent/ppermute | solution.py:281
  47.7 6.3 %collective-permute-start.5 = (bf16[128,2048]{1,0:T(8,128)(2,1)S(1)}, bf16[128,2048]{1,0:T(8,128)(2,1)}, u32[]{:S(2)}, u32[]{:S(2)}) collective-permute-start(bf16[128,2048]{1,0:T(8,128)(2,1)S(1)} %collective-permute-done.refs_1_), channel_id=1, source_target_pairs={{0,32},{32,0},{64,96},{96,64},{16,48},{48,16},{80,112},{112,80},{1... | collective-permute-start | bytes 1572872 | tf_op jit(solution)/shard_map/share_cotangent/ppermute | solution.py:281
  47.7 6.3 %collective-permute-start.6 = (bf16[128,2048]{1,0:T(8,128)(2,1)}, bf16[128,2048]{1,0:T(8,128)(2,1)}, u32[]{:S(2)}, u32[]{:S(2)}) collective-permute-start(bf16[128,2048]{1,0:T(8,128)(2,1)} %collective-permute-done.1.refs_2_), channel_id=1, source_target_pairs={{0,32},{32,0},{64,96},{96,64},{16,48},{48,16},{80,112},{112,80},{1... | collective-permute-start | bytes 1572872 | tf_op jit(solution)/shard_map/share_cotangent/ppermute | solution.py:281
  52.2 3.7 %collective-permute-start.7 = (bf16[128,2048]{1,0:T(8,128)(2,1)}, bf16[128,2048]{1,0:T(8,128)(2,1)}, u32[]{:S(2)}, u32[]{:S(2)}) collective-permute-start(bf16[128,2048]{1,0:T(8,128)(2,1)} %constant_dynamic-update-slice_fusion.refs_3_), channel_id=1, source_target_pairs={{0,32},{32,0},{64,96},{96,64},{16,48},{48,16},{80,112},{112,80},{1... | collective-permute-start | bytes 1572872 | tf_op jit(solution)/shard_map/share_cotangent/ppermute | solution.py:281
  69.2 0.8 copy-start.2
  70.0 14.1 %all-to-all-start.3 = ((bf16[16,8,16,128]{3,2,1,0:T(8,128)(2,1)}), bf16[16,8,16,128]{3,2,1,0:T(8,128)(2,1)}, u32[]{:S(2)}, u32[]{:S(2)}) async-start(bf16[16,8,16,128]{3,2,1,0:T(8,128)(2,1)} %copy-done.2), calls=%async_computation.3 | async-start | bytes 1048576 | tf_op jit(solution)/shard_map/dconv_a2a/all_to_all | solution.py:338
  77.8 1.0 copy-start.1
  84.1 26.3 %all-to-all-start.2 = ((bf16[16,16,2048]{2,1,0:T(8,128)(2,1)}), bf16[16,16,2048]{2,1,0:T(8,128)(2,1)S(1)}, u32[]{:S(2)}, u32[]{:S(2)}) async-start(bf16[16,16,2048]{2,1,0:T(8,128)(2,1)} %bitcast.88), calls=%async_computation.2 | async-start | bytes 2097152 | tf_op jit(solution)/shard_map/grad_proj_a2a/all_to_all | solution.py:358
  96.3 21.1 %collective-permute-start.8 = (bf16[16,32,128]{2,1,0:T(8,128)(2,1)S(1)}, bf16[16,32,128]{2,1,0:T(8,128)(2,1)S(1)}, u32[]{:S(2)}, u32[]{:S(2)}) collective-permute-start(bf16[16,32,128]{2,1,0:T(8,128)(2,1)S(1)} %bitcast.93), channel_id=1, source_target_pairs={{0,0},{1,32},{2,64},{3,96},{4,1},{5,33},{6,65},{7,97},{8,2},{9,34}... | collective-permute-start | bytes 393224 | tf_op jit(solution)/shard_map/grad_taps/ppermute | solution.py:354
  110.4 20.6 %all-to-all-start.4 = ((bf16[128,16,128]{2,1,0:T(8,128)(2,1)}), bf16[128,16,128]{2,1,0:T(8,128)(2,1)S(1)}, u32[]{:S(2)}, u32[]{:S(2)}) async-start(bf16[128,16,128]{2,1,0:T(8,128)(2,1)} %copy.52), calls=%async_computation.4 | async-start | bytes 1048576 | tf_op jit(solution)/shard_map/grad_in_a2a/all_to_all | solution.py:362
  117.5 13.5 %collective-permute-start.9 = (bf16[16,8,128]{2,1,0:T(8,128)(2,1)S(1)}, bf16[16,8,128]{2,1,0:T(8,128)(2,1)S(1)}, u32[]{:S(2)}, u32[]{:S(2)}) collective-permute-start(bf16[16,8,128]{2,1,0:T(8,128)(2,1)S(1)} %get-tuple-element.24), channel_id=1, source_target_pairs={{0,32},{32,0},{64,96},{96,64},{1,33},{33,1},{65,97},{97,65},{2,34}... | collective-permute-start | bytes 98312 | tf_op jit(solution)/shard_map/grad_filter/ppermute | solution.py:369
  118.6 12.4 %collective-permute-start.10 = (bf16[16,8,128]{2,1,0:T(8,128)(2,1)S(1)}, bf16[16,8,128]{2,1,0:T(8,128)(2,1)S(1)}, u32[]{:S(2)}, u32[]{:S(2)}) collective-permute-start(bf16[16,8,128]{2,1,0:T(8,128)(2,1)S(1)} %get-tuple-element.23), channel_id=1, source_target_pairs={{0,64},{32,96},{64,0},{96,32},{1,65},{33,97},{65,1},{97,33},{2,66}... | collective-permute-start | bytes 98312 | tf_op jit(solution)/shard_map/grad_filter/ppermute | solution.py:369
  119.4 11.6 %collective-permute-start.11 = (bf16[16,8,128]{2,1,0:T(8,128)(2,1)S(1)}, bf16[16,8,128]{2,1,0:T(8,128)(2,1)S(1)}, u32[]{:S(2)}, u32[]{:S(2)}) collective-permute-start(bf16[16,8,128]{2,1,0:T(8,128)(2,1)S(1)} %get-tuple-element.22), channel_id=1, source_target_pairs={{0,96},{32,64},{64,32},{96,0},{1,97},{33,65},{65,33},{97,1},{2,98}... | collective-permute-start | bytes 98312 | tf_op jit(solution)/shard_map/grad_filter/ppermute | solution.py:369

commit v5 on v4

--- a/solution.py
+++ b/solution.py
@@ -147,6 +147,7 @@
 
 
 MANY = 4
+TAPS_MANY = 8
 
 
 def per_channel(many, shape):
@@ -179,16 +180,16 @@
     out = jax.ShapeDtypeStruct((chans * rows // seqs, LANES), bf16)
     return pl.pallas_call(
         functools.partial(taps_kernel, seqs),
-        grid=(chans // MANY,),
+        grid=(chans // TAPS_MANY,),
         in_specs=[
             pl.BlockSpec(memory_space=pltpu.SMEM),
-            per_channel(MANY, x.shape),
-            per_channel(MANY, d.shape),
+            per_channel(TAPS_MANY, x.shape),
+            per_channel(TAPS_MANY, d.shape),
         ],
         out_specs=pl.BlockSpec(out.shape, lambda i: (0, 0)),
         out_shape=out,
         scratch_shapes=[
-            pltpu.VMEM((MANY, 2, 2 * rows, LANES), bf16),
+            pltpu.VMEM((TAPS_MANY, 2, 2 * rows, LANES), bf16),
             pltpu.VMEM(out.shape, f32),
         ],
         compiler_params=pltpu.CompilerParams(vmem_limit_bytes=24 << 20),
@@ -261,8 +262,8 @@
 
 
 SEQ = ("zl", "core")
-POS = ("zh", "y", "x")
-PLANE = ("y", "x")
+POS = ("zh", "yh", "yl", "xh", "xl")
+PLANE = ("yl", "yh", "xl", "xh")
 COLUMN = ("zl", "core", "zh")
 
 
@@ -302,11 +303,12 @@
             .reshape(tokens, width)
             .astype(bf16)
         )
-        parts = signal.T.reshape(seqs, ctx, chans, tokens)
+        few = chans // seqs
+        parts = signal.T.reshape(seqs, ctx, seqs, few, tokens)
         taps = filter_taps.reshape(seqs, ctx, seqs, chans // seqs, tokens)
-        taps = lax.dynamic_index_in_dim(taps, me_dp, 2, keepdims=False)
-        load = jnp.concatenate([parts, taps], axis=2).transpose(1, 0, 2, 3)
-        load = load.reshape(ctx * seqs, -1, chans // seqs, LANES)
+        taps = lax.dynamic_index_in_dim(taps, me_dp, 2)
+        load = jnp.concatenate([parts, taps], axis=2).transpose(1, 0, 2, 3, 4)
+        load = load.reshape(ctx * seqs, -1, few, LANES)
     with jax.named_scope("signal_a2a"):
         load = lax.all_to_all(load, POS + SEQ, 0, 0)
         load = load.reshape(ctx * seqs, -1, LANES)
@@ -324,20 +326,27 @@
         far = jnp.concatenate([move(below[:half], 1), move(above[half:], 3)], axis=0)
         pieces = [own, below, above, far, beside]
         pieces += [move(a, 0, 1) for a in (below, above, far)]
+    with jax.named_scope("weight_load"):
+        rows = proj_weight.reshape(chans, width // LANES, LANES).transpose(1, 0, 2)
+        rows = jnp.broadcast_to(rows[None], (plane, *rows.shape))
+        load = jnp.pad(rows, ((0, 0), (0, column), (0, 0), (0, 0)))
+        load, h = lax.optimization_barrier((load, h))
     with jax.named_scope("conv"):
         conv = conv_call(conv_kernel, x, h, own_skip, seqs)
-        conv = conv.reshape(chans, ctx // plane, plane, seqs, LANES).transpose(2, 1, 3, 0, 4)
+        order = [POS.index(name) for name in PLANE]
+        conv = conv.reshape(chans, ctx // plane, 2, 2, 2, 2, seqs, LANES)
+        conv = conv.transpose(*(1 + at for at in order), 1, 6, 0, 7)
         conv = conv.reshape(plane, column, chans, LANES)
     with jax.named_scope("conv_a2a"):
-        rows = proj_weight.reshape(chans, width // LANES, LANES).transpose(1, 0, 2)
-        rows = jnp.broadcast_to(rows[None], (plane, *rows.shape))
-        load = lax.all_to_all(jnp.concatenate([rows, conv], axis=1), PLANE, 0, 0)
+        load = lax.dynamic_update_slice(load, conv, (0, width // LANES, 0, 0))
+        load = lax.all_to_all(load, PLANE, 0, 0)
     with jax.named_scope("dconv"):
         dconv = dconv_call(place, load, pieces)
     with jax.named_scope("dconv_a2a"):
         dconv = lax.all_to_all(dconv, PLANE, 0, 0)
-        dconv = dconv.reshape(plane, ctx // plane, seqs, chans, LANES)
-        dconv = dconv.transpose(3, 1, 0, 2, 4).reshape(chans, ctx * seqs, LANES)
+        dconv = dconv.reshape(2, 2, 2, 2, ctx // plane, seqs, chans, LANES)
+        back = [PLANE.index(name) for name in POS[1:]]
+        dconv = dconv.transpose(6, 4, *back, 5, 7).reshape(chans, ctx * seqs, LANES)
     factor = 1.0 / math.sqrt(seqs * tokens * ctx)
     with jax.named_scope("grad_proj"):
         partial = proj_call(place, load, pieces)
@@ -385,7 +394,7 @@
 
 
 def solution(mesh):
-    mesh = Mesh(mesh.devices.reshape(2, 2, 2, 4, 4), SEQ + POS)
+    mesh = Mesh(mesh.devices.reshape((2,) * 7), SEQ + POS)
     placed = (
         P(SEQ, POS, None),
         P(SEQ, POS, None),

time: 134 us -> 131 us (0.978)
  waiting for transfers between devices: 39.7 us -> 35.6 us
  local copies, waits for them, and re-layouts: 11.9 us -> 14.3 us
    all_to_all x1, waiting for transfers between devices: 9.64 us -> 7.43 us  [on_device(): load = lax.all_to_all(load, PLANE, 0, 0)]
    all_to_all x1, waiting for transfers between devices: 10.7 us -> 9.03 us  [on_device(): load = lax.all_to_all(load, POS + SEQ, 0, 0)]
    pad x0 -> x1, local copies, waits for them, and re-layouts: none -> 1.47 us  [on_device(): load = jnp.pad(rows, ((0, 0), (0, column), (0, 0), (0, 0)))]
  transfers between devices with their start and end apart: 17 -> 17, of which waited for: 6 -> 6; matrix products, arithmetic and copies ran while one was open for 7% -> 8% of each run, Pallas kernels for 15% -> 15%
where the time goes in v5:
time: 131 us; the launch traced here: 130 us
  starting transfers between devices  51.5 us (39%)
  waiting for transfers between devices  35.6 us (27%)
  Pallas kernels  23.5 us (18%)
  local copies, waits for them, and re-layouts  14.3 us (11%)
  other arithmetic  2.82 us (2%)
    all_to_all x1, starting transfers between devices, on_device(): load = lax.all_to_all(load, POS + SEQ, 0, 0)  11.5 us
    pallas_call x2, Pallas kernels, conv_call(): pl.pallas_call(functools.partial(kernel, seqs), grid=(chans // MANY,), in...  10.2 us
    ppermute x8, starting transfers between devices, move(): return lax.ppermute(a, COLUMN, column_pairs(step, other))  9.96 us
    all_to_all x1, waiting for transfers between devices, on_device(): grad_in = lax.all_to_all(grad_in, POS + SEQ, 0, 0)  9.79 us
    all_to_all x1, waiting for transfers between devices, on_device(): load = lax.all_to_all(load, POS + SEQ, 0, 0)  9.03 us
    ppermute x1, starting transfers between devices, on_device(): held = lax.ppermute(grad_taps, SEQ + POS, pairs)  7.68 us
    all_to_all x1, waiting for transfers between devices, on_device(): load = lax.all_to_all(load, PLANE, 0, 0)  7.43 us
    all_to_all x1, starting transfers between devices, on_device(): grad_in = lax.all_to_all(grad_in, POS + SEQ, 0, 0)  6.96 us
  transfers between devices with their start and end apart: 17, of which 6 were waited for; matrix products, arithmetic and copies ran while one was open for 8% of the time, Pallas kernels for 15%

profile of v5, /device:TPU:1, one launch (start us, length us, event | category | flops | bytes accessed | tf_op | source)
XLA Modules:
  0.0 129.9 jit_solution(10884802614661741460)
XLA Ops:
  0.7 1.4 %copy.39 = bf16[1,128,2048]{1,2,0:T(8,128)(2,1)S(1)} copy(bf16[1,128,2048]{2,1,0:T(8,128)(2,1)} %param.6) | data formatting | bytes 1048576 | tf_op args[0]
  2.1 0.8 fusion.1
  2.9 0.4 maximum_bitcast_fusion
  3.4 0.5 copy.40
  3.9 1.4 %copy.41 = bf16[128,5,4,128]{3,2,1,0:T(4,128)(2,1)} copy(bf16[128,5,4,128]{3,0,2,1:T(8,128)(2,1)S(1)} %bitcast.94) | data formatting | bytes 1310720 | tf_op jit(solution)/shard_map/signal/reshape | solution.py:311
  5.2 11.5 %all-to-all-start = ((bf16[128,5,4,128]{3,2,1,0:T(4,128)(2,1)}), bf16[128,5,4,128]{3,2,1,0:T(4,128)(2,1)S(1)}, u32[]{:S(2)}, u32[]{:S(2)}) async-start(bf16[128,5,4,128]{3,2,1,0:T(4,128)(2,1)} %copy.41), calls=%async_computation | async-start | bytes 1310720 | tf_op jit(solution)/shard_map/signal_a2a/all_to_all | solution.py:313
  16.8 1.6 %collective-permute-start = (bf16[128,2048]{1,0:T(8,128)(2,1)}, bf16[128,2048]{1,0:T(8,128)(2,1)S(1)}, u32[]{:S(2)}, u32[]{:S(2)}) collective-permute-start(bf16[128,2048]{1,0:T(8,128)(2,1)} %bitcast.25.refs_0_), channel_id=1, source_target_pairs={{0,64},{32,96},{64,16},{96,48},{16,80},{48,112},{80,0},{112,32},{1... | collective-permute-start | bytes 1572872 | tf_op jit(solution)/shard_map/share_cotangent/ppermute | solution.py:282
  18.3 1.8 %collective-permute-start.1 = (bf16[128,2048]{1,0:T(8,128)(2,1)}, bf16[128,2048]{1,0:T(8,128)(2,1)}, u32[]{:S(2)}, u32[]{:S(2)}) collective-permute-start(bf16[128,2048]{1,0:T(8,128)(2,1)} %bitcast.25.refs_0_), channel_id=1, source_target_pairs={{0,80},{32,112},{64,0},{96,32},{16,64},{48,96},{80,16},{112,48},{1... | collective-permute-start | bytes 1572872 | tf_op jit(solution)/shard_map/share_cotangent/ppermute | solution.py:282
  20.2 0.8 dynamic_slice.27.skip_ref
  20.9 0.2 broadcast_in_dim.4
  21.1 1.5 %pad.4 = bf16[16,24,16,128]{3,2,1,0:T(8,128)(2,1)} pad(bf16[16,16,16,128]{3,2,1,0:T(8,128)(2,1)S(1)} %broadcast_in_dim.4, bf16[]{:T(256)} %constant.118.clone.1), padding=0_0x0_8x0_0x0_0 | pad | bytes 2621442 | tf_op jit(solution)/shard_map/weight_load/jit(_pad)/pad | solution.py:332
  22.6 9.0 %all-to-all-done = bf16[128,5,4,128]{3,2,1,0:T(4,128)(2,1)S(1)} async-done(((bf16[128,5,4,128]{3,2,1,0:T(4,128)(2,1)}), bf16[128,5,4,128]{3,2,1,0:T(4,128)(2,1)S(1)}, u32[]{:S(2)}, u32[]{:S(2)}) %all-to-all-start) | async-done | bytes 655392 | tf_op jit(solution)/shard_map/signal_a2a/all_to_all | solution.py:313
  31.9 5.0 %conv.1 = bf16[16,128,128]{2,1,0:T(8,128)(2,1)S(1)} custom-call(f32[16]{0:T(128)S(1)} %dynamic_slice.27.skip_ref, bf16[16,128,128]{2,1,0:T(8,128)(2,1)S(1)} %slice_bitcast_fusion.x_ref, bf16[16,32,128]{2,1,0:T(8,128)(2,1)S(1)} %bitcast.89), custom_call_target="tpu_custom_call" | custom-call | flops 1048576 | bytes 65536 | tf_op jit(solution)/shard_map/conv/pallas_call | solution.py:163
  36.9 0.6 copy.44
  37.5 0.9 constant_dynamic-update-slice_fusion.2
  38.4 3.7 %all-to-all-start.1 = ((bf16[16,24,16,128]{3,2,1,0:T(8,128)(2,1)}), bf16[16,24,16,128]{3,2,1,0:T(8,128)(2,1)S(1)}, u32[]{:S(2)}, u32[]{:S(2)}) async-start(bf16[16,24,16,128]{3,2,1,0:T(8,128)(2,1)} %constant_dynamic-update-slice_fusion.2), calls=%async_computation.1 | async-start | bytes 3145728 | tf_op jit(solution)/shard_map/conv_a2a/all_to_all | solution.py:342
  42.2 0.2 collective-permute-start.2
  42.4 1.0 slice.19
  43.4 2.6 %collective-permute-start.3 = (bf16[64,2048]{1,0:T(8,128)(2,1)S(1)}, bf16[64,2048]{1,0:T(8,128)(2,1)S(1)}, u32[]{:S(2)}, u32[]{:S(2)}) collective-permute-start(bf16[64,2048]{1,0:T(8,128)(2,1)S(1)} %slice.19), channel_id=1, source_target_pairs={{0,80},{32,112},{64,0},{96,32},{16,64},{48,96},{80,16},{112,48},{1... | collective-permute-start | bytes 786440 | tf_op jit(solution)/shard_map/share_cotangent/ppermute | solution.py:282
  46.0 1.4 %collective-permute-start.4 = (bf16[128,2048]{1,0:T(8,128)(2,1)}, bf16[128,2048]{1,0:T(8,128)(2,1)}, u32[]{:S(2)}, u32[]{:S(2)}) collective-permute-start(bf16[128,2048]{1,0:T(8,128)(2,1)} %bitcast.25.refs_0_), channel_id=1, source_target_pairs={{0,32},{32,0},{64,96},{96,64},{16,48},{48,16},{80,112},{112,80},{1... | collective-permute-start | bytes 1572872 | tf_op jit(solution)/shard_map/share_cotangent/ppermute | solution.py:282
  47.4 0.5 collective-permute-start.6
  47.9 2.5 %collective-permute-done.2 = bf16[64,2048]{1,0:T(8,128)(2,1)S(1)} collective-permute-done((bf16[64,2048]{1,0:T(8,128)(2,1)S(1)}, bf16[64,2048]{1,0:T(8,128)(2,1)S(1)}, u32[]{:S(2)}, u32[]{:S(2)}) %collective-permute-start.2) | collective-permute-done | bytes 262176 | tf_op jit(solution)/shard_map/share_cotangent/ppermute | solution.py:282
  50.4 0.7 constant_dynamic-update-slice_fusion.1
  51.1 0.7 constant_dynamic-update-slice_fusion.refs_3_
  51.8 1.8 %collective-permute-start.7 = (bf16[128,2048]{1,0:T(8,128)(2,1)}, bf16[128,2048]{1,0:T(8,128)(2,1)}, u32[]{:S(2)}, u32[]{:S(2)}) collective-permute-start(bf16[128,2048]{1,0:T(8,128)(2,1)} %constant_dynamic-update-slice_fusion.refs_3_), channel_id=1, source_target_pairs={{0,32},{32,0},{64,96},{96,64},{16,48},{48,16},{80,112},{112,80},{1... | collective-permute-start | bytes 1572872 | tf_op jit(solution)/shard_map/share_cotangent/ppermute | solution.py:282
  53.7 1.8 %collective-permute-done.7.refs_7_ = bf16[128,2048]{1,0:T(8,128)(2,1)} collective-permute-done((bf16[128,2048]{1,0:T(8,128)(2,1)}, bf16[128,2048]{1,0:T(8,128)(2,1)}, u32[]{:S(2)}, u32[]{:S(2)}) %collective-permute-start.7) | collective-permute-done | bytes 524320 | tf_op jit(solution)/shard_map/share_cotangent/ppermute | solution.py:282
  55.5 7.4 %all-to-all-done.1.c_ref.w_ref = bf16[16,24,16,128]{3,2,1,0:T(8,128)(2,1)S(1)} async-done(((bf16[16,24,16,128]{3,2,1,0:T(8,128)(2,1)}), bf16[16,24,16,128]{3,2,1,0:T(8,128)(2,1)S(1)}, u32[]{:S(2)}, u32[]{:S(2)}) %all-to-all-start.1) | async-done | bytes 1572896 | tf_op jit(solution)/shard_map/conv_a2a/all_to_all | solution.py:342
  62.9 3.7 %dconv.1 = bf16[16,8,16,128]{3,2,1,0:T(8,128)(2,1)S(1)} custom-call(s32[8]{0:T(128)S(1)} %stack.48.place_ref, bf16[16,24,16,128]{3,2,1,0:T(8,128)(2,1)S(1)} %all-to-all-done.1.c_ref.w_ref, bf16[128,2048]{1,0:T(8,128)(2,1)} %bitcast.25.refs_0_, bf16[128,2048]{1,0:T(8,128)(2,1)S(1)} %collective-permute-done.refs_1_, ...), custom_call_target="tpu_custom_call" | custom-call | flops 1073741824 | bytes 6291456 | tf_op jit(solution)/shard_map/dconv/pallas_call | solution.py:239
  66.6 0.8 copy-done.2
  67.4 5.0 %all-to-all-start.3 = ((bf16[16,8,16,128]{3,2,1,0:T(8,128)(2,1)}), bf16[16,8,16,128]{3,2,1,0:T(8,128)(2,1)}, u32[]{:S(2)}, u32[]{:S(2)}) async-start(bf16[16,8,16,128]{3,2,1,0:T(8,128)(2,1)} %copy-done.2), calls=%async_computation.3 | async-start | bytes 1048576 | tf_op jit(solution)/shard_map/dconv_a2a/all_to_all | solution.py:346
  72.4 3.3 %grad_proj.1 = bf16[256,2048]{1,0:T(8,128)(2,1)S(1)} custom-call(s32[8]{0:T(128)S(1)} %stack.48.place_ref, bf16[16,24,16,128]{3,2,1,0:T(8,128)(2,1)S(1)} %all-to-all-done.1.c_ref.w_ref, bf16[128,2048]{1,0:T(8,128)(2,1)} %bitcast.25.refs_0_, bf16[128,2048]{1,0:T(8,128)(2,1)S(1)} %collective-permute-done.refs_1_, ...), custom_call_target="tpu_custom_call" | custom-call | flops 1073741824 | bytes 6291456 | tf_op jit(solution)/shard_map/grad_proj/pallas_call | solution.py:253
  75.7 1.0 copy-done.1
  76.7 5.1 %all-to-all-done.3 = bf16[16,8,16,128]{3,2,1,0:T(8,128)(2,1)} async-done(((bf16[16,8,16,128]{3,2,1,0:T(8,128)(2,1)}), bf16[16,8,16,128]{3,2,1,0:T(8,128)(2,1)}, u32[]{:S(2)}, u32[]{:S(2)}) %all-to-all-start.3) | async-done | bytes 524320 | tf_op jit(solution)/shard_map/dconv_a2a/all_to_all | solution.py:346
  81.8 3.8 %all-to-all-start.2 = ((bf16[16,16,2048]{2,1,0:T(8,128)(2,1)}), bf16[16,16,2048]{2,1,0:T(8,128)(2,1)S(1)}, u32[]{:S(2)}, u32[]{:S(2)}) async-start(bf16[16,16,2048]{2,1,0:T(8,128)(2,1)} %bitcast.86), calls=%async_computation.2 | async-start | bytes 2097152 | tf_op jit(solution)/shard_map/grad_proj_a2a/all_to_all | solution.py:367
  85.6 1.3 %copy.45 = bf16[2,2,2,2,2,4,16,128]{7,5,2,3,0,1,4,6:T(4,128)(2,1)S(1)} copy(bf16[2,2,2,2,2,4,16,128]{7,6,5,4,3,2,1,0:T(8,128)(2,1)} %bitcast.27) | data formatting | bytes 1048576 | tf_op jit(solution)/shard_map/dconv_a2a/reshape | solution.py:347
  87.0 6.3 %grad_taps.1 = bf16[512,128]{1,0:T(8,128)(2,1)S(1)} custom-call(f32[1]{0:T(128)} %constant.125.clone.1.scale_ref, bf16[16,128,128]{2,1,0:T(8,128)(2,1)S(1)} %slice_bitcast_fusion.x_ref, bf16[16,128,128]{2,1,0:T(8,128)(2,1)S(1)} %bitcast.84), custom_call_target="tpu_custom_call" | custom-call | flops 1048576 | bytes 65536 | tf_op jit(solution)/shard_map/grad_taps/pallas_call | solution.py:181
  93.3 7.7 %collective-permute-start.8 = (bf16[16,32,128]{2,1,0:T(8,128)(2,1)S(1)}, bf16[16,32,128]{2,1,0:T(8,128)(2,1)S(1)}, u32[]{:S(2)}, u32[]{:S(2)}) collective-permute-start(bf16[16,32,128]{2,1,0:T(8,128)(2,1)S(1)} %bitcast.91), channel_id=1, source_target_pairs={{0,0},{1,32},{2,64},{3,96},{4,1},{5,33},{6,65},{7,97},{8,2},{9,34}... | collective-permute-start | bytes 393224 | tf_op jit(solution)/shard_map/grad_taps/ppermute | solution.py:363
  101.0 5.2 %grad_in.1 = bf16[16,128,128]{2,1,0:T(8,128)(2,1)S(1)} custom-call(f32[16]{0:T(128)S(1)} %dynamic_slice.27.skip_ref, bf16[16,128,128]{2,1,0:T(8,128)(2,1)S(1)} %bitcast.85, bf16[16,32,128]{2,1,0:T(8,128)(2,1)S(1)} %bitcast.90), custom_call_target="tpu_custom_call" | custom-call | flops 1048576 | bytes 65536 | tf_op jit(solution)/shard_map/grad_in/pallas_call | solution.py:163
  106.3 1.1 copy.46
  107.4 7.0 %all-to-all-start.4 = ((bf16[128,16,128]{2,1,0:T(8,128)(2,1)}), bf16[128,16,128]{2,1,0:T(8,128)(2,1)S(1)}, u32[]{:S(2)}, u32[]{:S(2)}) async-start(bf16[128,16,128]{2,1,0:T(8,128)(2,1)} %copy.46), calls=%async_computation.4 | async-start | bytes 1048576 | tf_op jit(solution)/shard_map/grad_in_a2a/all_to_all | solution.py:371
  114.4 1.1 collective-permute-start.9
  115.6 0.8 collective-permute-start.10
  116.4 0.9 collective-permute-start.11
  117.3 0.1 convert_reduce_fusion
  117.4 0.7 broadcast_multiply_fusion
  118.1 9.8 %all-to-all-done.4 = bf16[128,16,128]{2,1,0:T(8,128)(2,1)S(1)} async-done(((bf16[128,16,128]{2,1,0:T(8,128)(2,1)}), bf16[128,16,128]{2,1,0:T(8,128)(2,1)S(1)}, u32[]{:S(2)}, u32[]{:S(2)}) %all-to-all-start.4) | async-done | bytes 524320 | tf_op jit(solution)/shard_map/grad_in_a2a/all_to_all | solution.py:371
  128.1 0.7 maximum_convert_fusion
  128.8 1.1 fusion
  (33 shorter events, 0.6 us)
Async XLA Ops:
  0.6 1.4 %copy-start = (bf16[2048,128]{1,0:T(8,128)(2,1)S(1)}, bf16[2048,128]{1,0:T(8,128)(2,1)}, u32[]{:S(2)}) copy-start(bf16[2048,128]{1,0:T(8,128)(2,1)} %param.9) | copy-start | bytes 1572868
  3.9 17.0 %copy-start.3 = (bf16[16,2048]{1,0:T(8,128)(2,1)S(1)}, bf16[16,2048]{1,0:T(8,128)(2,1)}, u32[]{:S(2)}) copy-start(bf16[16,2048]{1,0:T(8,128)(2,1)} %param.11) | copy-start | bytes 196612
  5.2 26.4 %all-to-all-start = ((bf16[128,5,4,128]{3,2,1,0:T(4,128)(2,1)}), bf16[128,5,4,128]{3,2,1,0:T(4,128)(2,1)S(1)}, u32[]{:S(2)}, u32[]{:S(2)}) async-start(bf16[128,5,4,128]{3,2,1,0:T(4,128)(2,1)} %copy.41), calls=%async_computation | async-start | bytes 1310720 | tf_op jit(solution)/shard_map/signal_a2a/all_to_all | solution.py:313
  16.8 25.4 %collective-permute-start = (bf16[128,2048]{1,0:T(8,128)(2,1)}, bf16[128,2048]{1,0:T(8,128)(2,1)S(1)}, u32[]{:S(2)}, u32[]{:S(2)}) collective-permute-start(bf16[128,2048]{1,0:T(8,128)(2,1)} %bitcast.25.refs_0_), channel_id=1, source_target_pairs={{0,64},{32,96},{64,16},{96,48},{16,80},{48,112},{80,0},{112,32},{1... | collective-permute-start | bytes 1572872 | tf_op jit(solution)/shard_map/share_cotangent/ppermute | solution.py:282
  18.3 24.1 %collective-permute-start.1 = (bf16[128,2048]{1,0:T(8,128)(2,1)}, bf16[128,2048]{1,0:T(8,128)(2,1)}, u32[]{:S(2)}, u32[]{:S(2)}) collective-permute-start(bf16[128,2048]{1,0:T(8,128)(2,1)} %bitcast.25.refs_0_), channel_id=1, source_target_pairs={{0,80},{32,112},{64,0},{96,32},{16,64},{48,96},{80,16},{112,48},{1... | collective-permute-start | bytes 1572872 | tf_op jit(solution)/shard_map/share_cotangent/ppermute | solution.py:282
  38.4 24.5 %all-to-all-start.1 = ((bf16[16,24,16,128]{3,2,1,0:T(8,128)(2,1)}), bf16[16,24,16,128]{3,2,1,0:T(8,128)(2,1)S(1)}, u32[]{:S(2)}, u32[]{:S(2)}) async-start(bf16[16,24,16,128]{3,2,1,0:T(8,128)(2,1)} %constant_dynamic-update-slice_fusion.2), calls=%async_computation.1 | async-start | bytes 3145728 | tf_op jit(solution)/shard_map/conv_a2a/all_to_all | solution.py:342
  42.2 8.2 %collective-permute-start.2 = (bf16[64,2048]{1,0:T(8,128)(2,1)S(1)}, bf16[64,2048]{1,0:T(8,128)(2,1)S(1)}, u32[]{:S(2)}, u32[]{:S(2)}) collective-permute-start(bf16[64,2048]{1,0:T(8,128)(2,1)S(1)} %slice.18), channel_id=1, source_target_pairs={{0,64},{32,96},{64,16},{96,48},{16,80},{48,112},{80,0},{112,32},{1... | collective-permute-start | bytes 786440 | tf_op jit(solution)/shard_map/share_cotangent/ppermute | solution.py:282
  43.4 7.7 %collective-permute-start.3 = (bf16[64,2048]{1,0:T(8,128)(2,1)S(1)}, bf16[64,2048]{1,0:T(8,128)(2,1)S(1)}, u32[]{:S(2)}, u32[]{:S(2)}) collective-permute-start(bf16[64,2048]{1,0:T(8,128)(2,1)S(1)} %slice.19), channel_id=1, source_target_pairs={{0,80},{32,112},{64,0},{96,32},{16,64},{48,96},{80,16},{112,48},{1... | collective-permute-start | bytes 786440 | tf_op jit(solution)/shard_map/share_cotangent/ppermute | solution.py:282
  46.0 7.7 %collective-permute-start.4 = (bf16[128,2048]{1,0:T(8,128)(2,1)}, bf16[128,2048]{1,0:T(8,128)(2,1)}, u32[]{:S(2)}, u32[]{:S(2)}) collective-permute-start(bf16[128,2048]{1,0:T(8,128)(2,1)} %bitcast.25.refs_0_), channel_id=1, source_target_pairs={{0,32},{32,0},{64,96},{96,64},{16,48},{48,16},{80,112},{112,80},{1... | collective-permute-start | bytes 1572872 | tf_op jit(solution)/shard_map/share_cotangent/ppermute | solution.py:282
  47.4 6.3 %collective-permute-start.5 = (bf16[128,2048]{1,0:T(8,128)(2,1)S(1)}, bf16[128,2048]{1,0:T(8,128)(2,1)}, u32[]{:S(2)}, u32[]{:S(2)}) collective-permute-start(bf16[128,2048]{1,0:T(8,128)(2,1)S(1)} %collective-permute-done.refs_1_), channel_id=1, source_target_pairs={{0,32},{32,0},{64,96},{96,64},{16,48},{48,16},{80,112},{112,80},{1... | collective-permute-start | bytes 1572872 | tf_op jit(solution)/shard_map/share_cotangent/ppermute | solution.py:282
  47.4 6.3 %collective-permute-start.6 = (bf16[128,2048]{1,0:T(8,128)(2,1)}, bf16[128,2048]{1,0:T(8,128)(2,1)}, u32[]{:S(2)}, u32[]{:S(2)}) collective-permute-start(bf16[128,2048]{1,0:T(8,128)(2,1)} %collective-permute-done.1.refs_2_), channel_id=1, source_target_pairs={{0,32},{32,0},{64,96},{96,64},{16,48},{48,16},{80,112},{112,80},{1... | collective-permute-start | bytes 1572872 | tf_op jit(solution)/shard_map/share_cotangent/ppermute | solution.py:282
  51.8 3.7 %collective-permute-start.7 = (bf16[128,2048]{1,0:T(8,128)(2,1)}, bf16[128,2048]{1,0:T(8,128)(2,1)}, u32[]{:S(2)}, u32[]{:S(2)}) collective-permute-start(bf16[128,2048]{1,0:T(8,128)(2,1)} %constant_dynamic-update-slice_fusion.refs_3_), channel_id=1, source_target_pairs={{0,32},{32,0},{64,96},{96,64},{16,48},{48,16},{80,112},{112,80},{1... | collective-permute-start | bytes 1572872 | tf_op jit(solution)/shard_map/share_cotangent/ppermute | solution.py:282
  66.6 0.8 copy-start.2
  67.4 14.4 %all-to-all-start.3 = ((bf16[16,8,16,128]{3,2,1,0:T(8,128)(2,1)}), bf16[16,8,16,128]{3,2,1,0:T(8,128)(2,1)}, u32[]{:S(2)}, u32[]{:S(2)}) async-start(bf16[16,8,16,128]{3,2,1,0:T(8,128)(2,1)} %copy-done.2), calls=%async_computation.3 | async-start | bytes 1048576 | tf_op jit(solution)/shard_map/dconv_a2a/all_to_all | solution.py:346
  75.7 1.0 copy-start.1
  81.8 25.6 %all-to-all-start.2 = ((bf16[16,16,2048]{2,1,0:T(8,128)(2,1)}), bf16[16,16,2048]{2,1,0:T(8,128)(2,1)S(1)}, u32[]{:S(2)}, u32[]{:S(2)}) async-start(bf16[16,16,2048]{2,1,0:T(8,128)(2,1)} %bitcast.86), calls=%async_computation.2 | async-start | bytes 2097152 | tf_op jit(solution)/shard_map/grad_proj_a2a/all_to_all | solution.py:367
  93.3 21.1 %collective-permute-start.8 = (bf16[16,32,128]{2,1,0:T(8,128)(2,1)S(1)}, bf16[16,32,128]{2,1,0:T(8,128)(2,1)S(1)}, u32[]{:S(2)}, u32[]{:S(2)}) collective-permute-start(bf16[16,32,128]{2,1,0:T(8,128)(2,1)S(1)} %bitcast.91), channel_id=1, source_target_pairs={{0,0},{1,32},{2,64},{3,96},{4,1},{5,33},{6,65},{7,97},{8,2},{9,34}... | collective-permute-start | bytes 393224 | tf_op jit(solution)/shard_map/grad_taps/ppermute | solution.py:363
  107.4 20.5 %all-to-all-start.4 = ((bf16[128,16,128]{2,1,0:T(8,128)(2,1)}), bf16[128,16,128]{2,1,0:T(8,128)(2,1)S(1)}, u32[]{:S(2)}, u32[]{:S(2)}) async-start(bf16[128,16,128]{2,1,0:T(8,128)(2,1)} %copy.46), calls=%async_computation.4 | async-start | bytes 1048576 | tf_op jit(solution)/shard_map/grad_in_a2a/all_to_all | solution.py:371
  114.4 13.5 %collective-permute-start.9 = (bf16[16,8,128]{2,1,0:T(8,128)(2,1)S(1)}, bf16[16,8,128]{2,1,0:T(8,128)(2,1)S(1)}, u32[]{:S(2)}, u32[]{:S(2)}) collective-permute-start(bf16[16,8,128]{2,1,0:T(8,128)(2,1)S(1)} %get-tuple-element.28), channel_id=1, source_target_pairs={{0,32},{32,0},{64,96},{96,64},{1,33},{33,1},{65,97},{97,65},{2,34}... | collective-permute-start | bytes 98312 | tf_op jit(solution)/shard_map/grad_filter/ppermute | solution.py:378
  115.6 12.4 %collective-permute-start.10 = (bf16[16,8,128]{2,1,0:T(8,128)(2,1)S(1)}, bf16[16,8,128]{2,1,0:T(8,128)(2,1)S(1)}, u32[]{:S(2)}, u32[]{:S(2)}) collective-permute-start(bf16[16,8,128]{2,1,0:T(8,128)(2,1)S(1)} %get-tuple-element.27), channel_id=1, source_target_pairs={{0,64},{32,96},{64,0},{96,32},{1,65},{33,97},{65,1},{97,33},{2,66}... | collective-permute-start | bytes 98312 | tf_op jit(solution)/shard_map/grad_filter/ppermute | solution.py:378
  116.4 11.6 %collective-permute-start.11 = (bf16[16,8,128]{2,1,0:T(8,128)(2,1)S(1)}, bf16[16,8,128]{2,1,0:T(8,128)(2,1)S(1)}, u32[]{:S(2)}, u32[]{:S(2)}) collective-permute-start(bf16[16,8,128]{2,1,0:T(8,128)(2,1)S(1)} %get-tuple-element.26), channel_id=1, source_target_pairs={{0,96},{32,64},{64,32},{96,0},{1,97},{33,65},{65,33},{97,1},{2,98}... | collective-permute-start | bytes 98312 | tf_op jit(solution)/shard_map/grad_filter/ppermute | solution.py:378

commit v6 on v5

--- a/solution.py
+++ b/solution.py
@@ -146,8 +146,7 @@
         ).astype(bf16)
 
 
-MANY = 4
-TAPS_MANY = 8
+MANY = 8
 
 
 def per_channel(many, shape):
@@ -180,16 +179,16 @@
     out = jax.ShapeDtypeStruct((chans * rows // seqs, LANES), bf16)
     return pl.pallas_call(
         functools.partial(taps_kernel, seqs),
-        grid=(chans // TAPS_MANY,),
+        grid=(chans // MANY,),
         in_specs=[
             pl.BlockSpec(memory_space=pltpu.SMEM),
-            per_channel(TAPS_MANY, x.shape),
-            per_channel(TAPS_MANY, d.shape),
+            per_channel(MANY, x.shape),
+            per_channel(MANY, d.shape),
         ],
         out_specs=pl.BlockSpec(out.shape, lambda i: (0, 0)),
         out_shape=out,
         scratch_shapes=[
-            pltpu.VMEM((TAPS_MANY, 2, 2 * rows, LANES), bf16),
+            pltpu.VMEM((MANY, 2, 2 * rows, LANES), bf16),
             pltpu.VMEM(out.shape, f32),
         ],
         compiler_params=pltpu.CompilerParams(vmem_limit_bytes=24 << 20),
@@ -230,6 +229,29 @@
         ).astype(bf16)
 
 
+def load_kernel(me_ref, q_ref, scale_ref, taps_ref, out_ref):
+    seqs, few = out_ref.shape[2] - 1, out_ref.shape[3]
+    chans = few * seqs
+    same = (iota(LANES, 0) == iota(LANES, 1)).astype(bf16)
+    count = LANES // chans
+    rows, cols = iota(few * count, 0), iota(few * count, 1)
+    pick = (cols == rows // few * chans + rows % few + me_ref[0] * few).astype(bf16)
+    blocks = q_ref.shape[1] // LANES
+    for b in range(blocks):
+        part = lax.dot_general(
+            same, q_ref[:, b * LANES : (b + 1) * LANES], (((1,), (1,)), ((), ())),
+            preferred_element_type=f32,
+        )
+        scale = scale_ref[pl.ds(pl.program_id(0) * blocks + b, 1), :]
+        part = (part * scale).reshape(count, seqs, few, LANES)
+        taps = jnp.dot(pick, taps_ref[b * LANES : (b + 1) * LANES, :], preferred_element_type=f32)
+        taps = taps.reshape(count, few, LANES)
+        each = blocks // out_ref.shape[1]
+        for k in range(count):
+            out_ref[b % each * count + k, b // each, :seqs] = part[k].astype(bf16)
+            out_ref[b % each * count + k, b // each, seqs] = taps[k].astype(bf16)
+
+
 def whole(count):
     return [pl.BlockSpec(memory_space=pltpu.VMEM)] * count
 
@@ -245,6 +267,29 @@
         compiler_params=pltpu.CompilerParams(vmem_limit_bytes=32 << 20),
         cost_estimate=pl.CostEstimate(flops=1 << 30, bytes_accessed=6 << 20, transcendentals=0),
     )(place, load, *pieces)
+
+
+def load_call(me, values, scales, taps, owners, seqs):
+    steps = 2
+    width = taps.shape[0] // steps
+    few = taps.shape[0] // owners // seqs
+    owners = owners // seqs
+    shape = (owners, seqs, seqs + 1, few, LANES)
+    load = pl.pallas_call(
+        load_kernel,
+        grid=(steps,),
+        in_specs=[
+            pl.BlockSpec(memory_space=pltpu.SMEM),
+            pl.BlockSpec((values.shape[0], width), lambda i: (0, i)),
+            pl.BlockSpec(scales.shape, lambda i: (0, 0)),
+            pl.BlockSpec((width, LANES), lambda i: (i, 0)),
+        ],
+        out_specs=pl.BlockSpec((owners, seqs // steps, *shape[2:]), lambda i: (0, i, 0, 0, 0)),
+        out_shape=jax.ShapeDtypeStruct(shape, bf16),
+        compiler_params=pltpu.CompilerParams(vmem_limit_bytes=60 << 20),
+        cost_estimate=estimate(1 << 20),
+    )(me, values, scales, taps)
+    return load.reshape(owners * seqs, *shape[2:])
 
 
 def proj_call(place, conv, pieces):
@@ -293,22 +338,12 @@
     tokens, width = quant_input.shape[1:]
     ctx, seqs, plane = (lax.axis_size(a) for a in (POS, SEQ, PLANE))
     me_dp, me_ctx = lax.axis_index(SEQ), lax.axis_index(POS)
-    blocks = input_scales.shape[2]
     chans = width // (ctx * seqs)
     column = ctx * seqs // plane
 
     with jax.named_scope("signal"):
-        signal = (
-            (quant_input[0].reshape(tokens, blocks, width // blocks) * input_scales[0][:, :, None])
-            .reshape(tokens, width)
-            .astype(bf16)
-        )
-        few = chans // seqs
-        parts = signal.T.reshape(seqs, ctx, seqs, few, tokens)
-        taps = filter_taps.reshape(seqs, ctx, seqs, chans // seqs, tokens)
-        taps = lax.dynamic_index_in_dim(taps, me_dp, 2)
-        load = jnp.concatenate([parts, taps], axis=2).transpose(1, 0, 2, 3, 4)
-        load = load.reshape(ctx * seqs, -1, few, LANES)
+        me = jnp.full((1,), me_dp, jnp.int32)
+        load = load_call(me, quant_input[0], input_scales[0].T, filter_taps, ctx * seqs, seqs)
     with jax.named_scope("signal_a2a"):
         load = lax.all_to_all(load, POS + SEQ, 0, 0)
         load = load.reshape(ctx * seqs, -1, LANES)

time: 131 us -> 128 us (0.977)
  local copies, waits for them, and re-layouts: 14.3 us -> 9.04 us
  Pallas kernels: 23.5 us -> 26.2 us
    pallas_call x1 -> x2, Pallas kernels: 6.34 us -> 8.97 us  [the longest x1 6.39 us: taps_call(): pl.pallas_call(functools.partial(taps_kernel, seqs), grid=(chans // MANY,...]
    unnamed x10 -> x5, local copies, waits for them, and re-layouts: 3.87 us -> 1.51 us
    reshape x1 -> x0, local copies, waits for them, and re-layouts: 1.36 us -> none  [on_device(): load = load.reshape(ctx * seqs, -1, few, LANES)]
  transfers between devices with their start and end apart: 17 -> 17, of which waited for: 6 -> 6; matrix products, arithmetic and copies ran while one was open for 8% -> 7% of each run, Pallas kernels for 15% -> 16%
where the time goes in v6:
time: 128 us; the launch traced here: 127 us
  starting transfers between devices  51.5 us (40%)
  waiting for transfers between devices  36.8 us (29%)
  Pallas kernels  26.2 us (20%)
  local copies, waits for them, and re-layouts  9.04 us (7%)
  other arithmetic  1.57 us (1%)
    all_to_all x1, starting transfers between devices, on_device(): load = lax.all_to_all(load, POS + SEQ, 0, 0)  11.5 us
    ppermute x8, starting transfers between devices, move(): return lax.ppermute(a, COLUMN, column_pairs(step, other))  9.95 us
    all_to_all x1, waiting for transfers between devices, on_device(): grad_in = lax.all_to_all(grad_in, POS + SEQ, 0, 0)  9.79 us
    pallas_call x2, Pallas kernels, conv_call(): pl.pallas_call(functools.partial(kernel, seqs), grid=(chans // MANY,), in...  9.61 us
    all_to_all x1, waiting for transfers between devices, on_device(): load = lax.all_to_all(load, POS + SEQ, 0, 0)  9.04 us
    ppermute x1, starting transfers between devices, on_device(): held = lax.ppermute(grad_taps, SEQ + POS, pairs)  7.68 us
    all_to_all x1, waiting for transfers between devices, on_device(): load = lax.all_to_all(load, PLANE, 0, 0)  7.44 us
    all_to_all x1, starting transfers between devices, on_device(): grad_in = lax.all_to_all(grad_in, POS + SEQ, 0, 0)  6.95 us
  transfers between devices with their start and end apart: 17, of which 6 were waited for; matrix products, arithmetic and copies ran while one was open for 7% of the time, Pallas kernels for 16%

profile of v6, /device:TPU:1, one launch (start us, length us, event | category | flops | bytes accessed | tf_op | source)
XLA Modules:
  0.0 127.2 jit_solution(15533524986217730017)
XLA Ops:
  0.6 0.0 copy-start
  0.7 2.6 %signal.1 = bf16[32,4,5,4,128]{4,3,2,1,0:T(4,128)(2,1)} custom-call(s32[1]{0:T(128)} %bitcast.9.me_ref, bf16[128,2048]{1,0:T(8,128)(2,1)} %bitcast.89, f32[16,128]{1,0:T(8,128)} %bitcast.99, bf16[2048,128]{1,0:T(8,128)(2,1)} %taps_ref.1), custom_call_target="tpu_custom_call" | custom-call | flops 1048576 | bytes 65536 | tf_op jit(solution)/shard_map/signal/pallas_call | solution.py:278
  3.2 11.5 %all-to-all-start = ((bf16[128,5,4,128]{3,2,1,0:T(4,128)(2,1)}), bf16[128,5,4,128]{3,2,1,0:T(4,128)(2,1)S(1)}, u32[]{:S(2)}, u32[]{:S(2)}) async-start(bf16[128,5,4,128]{3,2,1,0:T(4,128)(2,1)} %bitcast.83), calls=%async_computation | async-start | bytes 1310720 | tf_op jit(solution)/shard_map/signal_a2a/all_to_all | solution.py:348
  14.7 1.6 %collective-permute-start = (bf16[128,2048]{1,0:T(8,128)(2,1)}, bf16[128,2048]{1,0:T(8,128)(2,1)S(1)}, u32[]{:S(2)}, u32[]{:S(2)}) collective-permute-start(bf16[128,2048]{1,0:T(8,128)(2,1)} %bitcast.22.refs_0_), channel_id=1, source_target_pairs={{0,64},{32,96},{64,16},{96,48},{16,80},{48,112},{80,0},{112,32},{1... | collective-permute-start | bytes 1572872 | tf_op jit(solution)/shard_map/share_cotangent/ppermute | solution.py:327
  16.3 1.8 %collective-permute-start.1 = (bf16[128,2048]{1,0:T(8,128)(2,1)}, bf16[128,2048]{1,0:T(8,128)(2,1)S(1)}, u32[]{:S(2)}, u32[]{:S(2)}) collective-permute-start(bf16[128,2048]{1,0:T(8,128)(2,1)} %bitcast.22.refs_0_), channel_id=1, source_target_pairs={{0,80},{32,112},{64,0},{96,32},{16,64},{48,96},{80,16},{112,48},{1... | collective-permute-start | bytes 1572872 | tf_op jit(solution)/shard_map/share_cotangent/ppermute | solution.py:327
  18.2 0.8 dynamic_slice.22.skip_ref
  18.9 0.2 broadcast_in_dim.12
  19.1 1.5 %pad.4 = bf16[16,24,16,128]{3,2,1,0:T(8,128)(2,1)} pad(bf16[16,16,16,128]{3,2,1,0:T(8,128)(2,1)S(1)} %broadcast_in_dim.12, bf16[]{:T(256)} %constant.114.clone.1), padding=0_0x0_8x0_0x0_0 | pad | bytes 2621442 | tf_op jit(solution)/shard_map/weight_load/jit(_pad)/pad | solution.py:367
  20.6 9.0 %all-to-all-done = bf16[128,5,4,128]{3,2,1,0:T(4,128)(2,1)S(1)} async-done(((bf16[128,5,4,128]{3,2,1,0:T(4,128)(2,1)}), bf16[128,5,4,128]{3,2,1,0:T(4,128)(2,1)S(1)}, u32[]{:S(2)}, u32[]{:S(2)}) %all-to-all-start) | async-done | bytes 655392 | tf_op jit(solution)/shard_map/signal_a2a/all_to_all | solution.py:348
  29.6 0.1 copy.27
  29.9 4.8 %conv.1 = bf16[16,128,128]{2,1,0:T(8,128)(2,1)S(1)} custom-call(f32[16]{0:T(128)S(1)} %dynamic_slice.22.skip_ref, bf16[16,128,128]{2,1,0:T(8,128)(2,1)S(1)} %slice_bitcast_fusion.x_ref, bf16[16,32,128]{2,1,0:T(8,128)(2,1)S(1)} %bitcast.80), custom_call_target="tpu_custom_call" | custom-call | flops 1048576 | bytes 65536 | tf_op jit(solution)/shard_map/conv/pallas_call | solution.py:162
  34.7 0.6 copy.29
  35.3 0.9 constant_dynamic-update-slice_fusion.2
  36.2 3.7 %all-to-all-start.1 = ((bf16[16,24,16,128]{3,2,1,0:T(8,128)(2,1)}), bf16[16,24,16,128]{3,2,1,0:T(8,128)(2,1)S(1)}, u32[]{:S(2)}, u32[]{:S(2)}) async-start(bf16[16,24,16,128]{3,2,1,0:T(8,128)(2,1)} %constant_dynamic-update-slice_fusion.2), calls=%async_computation.1 | async-start | bytes 3145728 | tf_op jit(solution)/shard_map/conv_a2a/all_to_all | solution.py:377
  39.9 0.0 collective-permute-done.refs_1_
  39.9 0.2 collective-permute-start.2
  40.1 0.0 collective-permute-done.1.refs_2_
  40.2 2.6 %collective-permute-start.3 = (bf16[64,2048]{1,0:T(8,128)(2,1)S(1)}, bf16[64,2048]{1,0:T(8,128)(2,1)S(1)}, u32[]{:S(2)}, u32[]{:S(2)}) collective-permute-start(bf16[64,2048]{1,0:T(8,128)(2,1)S(1)} %slice.19), channel_id=1, source_target_pairs={{0,80},{32,112},{64,0},{96,32},{16,64},{48,96},{80,16},{112,48},{1... | collective-permute-start | bytes 786440 | tf_op jit(solution)/shard_map/share_cotangent/ppermute | solution.py:327
  42.8 1.4 %collective-permute-start.4 = (bf16[128,2048]{1,0:T(8,128)(2,1)}, bf16[128,2048]{1,0:T(8,128)(2,1)}, u32[]{:S(2)}, u32[]{:S(2)}) collective-permute-start(bf16[128,2048]{1,0:T(8,128)(2,1)} %bitcast.22.refs_0_), channel_id=1, source_target_pairs={{0,32},{32,0},{64,96},{96,64},{16,48},{48,16},{80,112},{112,80},{1... | collective-permute-start | bytes 1572872 | tf_op jit(solution)/shard_map/share_cotangent/ppermute | solution.py:327
  44.2 0.0 collective-permute-start.5
  44.2 0.5 collective-permute-start.6
  44.7 3.4 %collective-permute-done.2 = bf16[64,2048]{1,0:T(8,128)(2,1)S(1)} collective-permute-done((bf16[64,2048]{1,0:T(8,128)(2,1)S(1)}, bf16[64,2048]{1,0:T(8,128)(2,1)S(1)}, u32[]{:S(2)}, u32[]{:S(2)}) %collective-permute-start.2) | collective-permute-done | bytes 262176 | tf_op jit(solution)/shard_map/share_cotangent/ppermute | solution.py:327
  48.1 0.7 constant_dynamic-update-slice_fusion.1
  48.9 0.7 constant_dynamic-update-slice_fusion.refs_3_
  49.6 1.8 %collective-permute-start.7 = (bf16[128,2048]{1,0:T(8,128)(2,1)}, bf16[128,2048]{1,0:T(8,128)(2,1)}, u32[]{:S(2)}, u32[]{:S(2)}) collective-permute-start(bf16[128,2048]{1,0:T(8,128)(2,1)} %constant_dynamic-update-slice_fusion.refs_3_), channel_id=1, source_target_pairs={{0,32},{32,0},{64,96},{96,64},{16,48},{48,16},{80,112},{112,80},{1... | collective-permute-start | bytes 1572872 | tf_op jit(solution)/shard_map/share_cotangent/ppermute | solution.py:327
  51.4 0.1 stack.48.place_ref
  51.5 1.8 %collective-permute-done.7.refs_7_ = bf16[128,2048]{1,0:T(8,128)(2,1)} collective-permute-done((bf16[128,2048]{1,0:T(8,128)(2,1)}, bf16[128,2048]{1,0:T(8,128)(2,1)}, u32[]{:S(2)}, u32[]{:S(2)}) %collective-permute-start.7) | collective-permute-done | bytes 524320 | tf_op jit(solution)/shard_map/share_cotangent/ppermute | solution.py:327
  53.2 7.4 %all-to-all-done.1.c_ref.w_ref = bf16[16,24,16,128]{3,2,1,0:T(8,128)(2,1)S(1)} async-done(((bf16[16,24,16,128]{3,2,1,0:T(8,128)(2,1)}), bf16[16,24,16,128]{3,2,1,0:T(8,128)(2,1)S(1)}, u32[]{:S(2)}, u32[]{:S(2)}) %all-to-all-start.1) | async-done | bytes 1572896 | tf_op jit(solution)/shard_map/conv_a2a/all_to_all | solution.py:377
  60.7 3.5 %dconv.1 = bf16[16,8,16,128]{3,2,1,0:T(8,128)(2,1)S(1)} custom-call(s32[8]{0:T(128)S(1)} %stack.48.place_ref, bf16[16,24,16,128]{3,2,1,0:T(8,128)(2,1)S(1)} %all-to-all-done.1.c_ref.w_ref, bf16[128,2048]{1,0:T(8,128)(2,1)} %bitcast.22.refs_0_, bf16[128,2048]{1,0:T(8,128)(2,1)S(1)} %collective-permute-done.refs_1_, ...), custom_call_target="tpu_custom_call" | custom-call | flops 1073741824 | bytes 6291456 | tf_op jit(solution)/shard_map/dconv/pallas_call | solution.py:261
  64.2 0.8 copy-done.1
  65.0 5.0 %all-to-all-start.3 = ((bf16[16,8,16,128]{3,2,1,0:T(8,128)(2,1)}), bf16[16,8,16,128]{3,2,1,0:T(8,128)(2,1)}, u32[]{:S(2)}, u32[]{:S(2)}) async-start(bf16[16,8,16,128]{3,2,1,0:T(8,128)(2,1)} %copy-done.1), calls=%async_computation.3 | async-start | bytes 1048576 | tf_op jit(solution)/shard_map/dconv_a2a/all_to_all | solution.py:381
  70.0 4.1 %grad_proj.1 = bf16[256,2048]{1,0:T(8,128)(2,1)} custom-call(s32[8]{0:T(128)S(1)} %stack.48.place_ref, bf16[16,24,16,128]{3,2,1,0:T(8,128)(2,1)S(1)} %all-to-all-done.1.c_ref.w_ref, bf16[128,2048]{1,0:T(8,128)(2,1)} %bitcast.22.refs_0_, bf16[128,2048]{1,0:T(8,128)(2,1)S(1)} %collective-permute-done.refs_1_, ...), custom_call_target="tpu_custom_call" | custom-call | flops 1073741824 | bytes 6291456 | tf_op jit(solution)/shard_map/grad_proj/pallas_call | solution.py:298
  74.2 5.2 %all-to-all-done.3 = bf16[16,8,16,128]{3,2,1,0:T(8,128)(2,1)} async-done(((bf16[16,8,16,128]{3,2,1,0:T(8,128)(2,1)}), bf16[16,8,16,128]{3,2,1,0:T(8,128)(2,1)}, u32[]{:S(2)}, u32[]{:S(2)}) %all-to-all-start.3) | async-done | bytes 524320 | tf_op jit(solution)/shard_map/dconv_a2a/all_to_all | solution.py:381
  79.4 3.8 %all-to-all-start.2 = ((bf16[16,16,2048]{2,1,0:T(8,128)(2,1)}), bf16[16,16,2048]{2,1,0:T(8,128)(2,1)S(1)}, u32[]{:S(2)}, u32[]{:S(2)}) async-start(bf16[16,16,2048]{2,1,0:T(8,128)(2,1)} %bitcast.23), calls=%async_computation.2 | async-start | bytes 2097152 | tf_op jit(solution)/shard_map/grad_proj_a2a/all_to_all | solution.py:402
  83.3 1.3 %copy.30 = bf16[2,2,2,2,2,4,16,128]{7,5,2,3,0,1,4,6:T(4,128)(2,1)S(1)} copy(bf16[2,2,2,2,2,4,16,128]{7,6,5,4,3,2,1,0:T(8,128)(2,1)} %bitcast.24) | data formatting | bytes 1048576 | tf_op jit(solution)/shard_map/dconv_a2a/reshape | solution.py:382
  84.6 6.4 %grad_taps.1 = bf16[512,128]{1,0:T(8,128)(2,1)S(1)} custom-call(f32[1]{0:T(128)} %constant.121.clone.1.scale_ref, bf16[16,128,128]{2,1,0:T(8,128)(2,1)S(1)} %slice_bitcast_fusion.x_ref, bf16[16,128,128]{2,1,0:T(8,128)(2,1)S(1)} %bitcast.76), custom_call_target="tpu_custom_call" | custom-call | flops 1048576 | bytes 65536 | tf_op jit(solution)/shard_map/grad_taps/pallas_call | solution.py:180
  91.0 7.7 %collective-permute-start.8 = (bf16[16,32,128]{2,1,0:T(8,128)(2,1)S(1)}, bf16[16,32,128]{2,1,0:T(8,128)(2,1)S(1)}, u32[]{:S(2)}, u32[]{:S(2)}) collective-permute-start(bf16[16,32,128]{2,1,0:T(8,128)(2,1)S(1)} %bitcast.82), channel_id=1, source_target_pairs={{0,0},{1,32},{2,64},{3,96},{4,1},{5,33},{6,65},{7,97},{8,2},{9,34}... | collective-permute-start | bytes 393224 | tf_op jit(solution)/shard_map/grad_taps/ppermute | solution.py:398
  98.7 4.8 %grad_in.1 = bf16[16,128,128]{2,1,0:T(8,128)(2,1)S(1)} custom-call(f32[16]{0:T(128)S(1)} %dynamic_slice.22.skip_ref, bf16[16,128,128]{2,1,0:T(8,128)(2,1)S(1)} %bitcast.77, bf16[16,32,128]{2,1,0:T(8,128)(2,1)S(1)} %bitcast.81), custom_call_target="tpu_custom_call" | custom-call | flops 1048576 | bytes 65536 | tf_op jit(solution)/shard_map/grad_in/pallas_call | solution.py:162
  103.5 1.1 copy.31
  104.7 7.0 %all-to-all-start.4 = ((bf16[128,16,128]{2,1,0:T(8,128)(2,1)}), bf16[128,16,128]{2,1,0:T(8,128)(2,1)S(1)}, u32[]{:S(2)}, u32[]{:S(2)}) async-start(bf16[128,16,128]{2,1,0:T(8,128)(2,1)} %copy.31), calls=%async_computation.4 | async-start | bytes 1048576 | tf_op jit(solution)/shard_map/grad_in_a2a/all_to_all | solution.py:406
  111.7 1.1 collective-permute-start.9
  112.8 0.8 collective-permute-start.10
  113.6 0.9 collective-permute-start.11
  114.6 0.1 convert_reduce_fusion
  114.7 0.7 broadcast_multiply_fusion
  115.4 9.8 %all-to-all-done.4 = bf16[128,16,128]{2,1,0:T(8,128)(2,1)S(1)} async-done(((bf16[128,16,128]{2,1,0:T(8,128)(2,1)}), bf16[128,16,128]{2,1,0:T(8,128)(2,1)S(1)}, u32[]{:S(2)}, u32[]{:S(2)}) %all-to-all-start.4) | async-done | bytes 524320 | tf_op jit(solution)/shard_map/grad_in_a2a/all_to_all | solution.py:406
  125.3 0.7 maximum_convert_fusion
  126.1 1.1 fusion
  (24 shorter events, 0.3 us)
Async XLA Ops:
  0.6 18.3 %copy-start = (bf16[16,2048]{1,0:T(8,128)(2,1)S(1)}, bf16[16,2048]{1,0:T(8,128)(2,1)}, u32[]{:S(2)}) copy-start(bf16[16,2048]{1,0:T(8,128)(2,1)} %param.11) | copy-start | bytes 196612
  3.2 26.4 %all-to-all-start = ((bf16[128,5,4,128]{3,2,1,0:T(4,128)(2,1)}), bf16[128,5,4,128]{3,2,1,0:T(4,128)(2,1)S(1)}, u32[]{:S(2)}, u32[]{:S(2)}) async-start(bf16[128,5,4,128]{3,2,1,0:T(4,128)(2,1)} %bitcast.83), calls=%async_computation | async-start | bytes 1310720 | tf_op jit(solution)/shard_map/signal_a2a/all_to_all | solution.py:348
  14.7 25.1 %collective-permute-start = (bf16[128,2048]{1,0:T(8,128)(2,1)}, bf16[128,2048]{1,0:T(8,128)(2,1)S(1)}, u32[]{:S(2)}, u32[]{:S(2)}) collective-permute-start(bf16[128,2048]{1,0:T(8,128)(2,1)} %bitcast.22.refs_0_), channel_id=1, source_target_pairs={{0,64},{32,96},{64,16},{96,48},{16,80},{48,112},{80,0},{112,32},{1... | collective-permute-start | bytes 1572872 | tf_op jit(solution)/shard_map/share_cotangent/ppermute | solution.py:327
  16.3 23.8 %collective-permute-start.1 = (bf16[128,2048]{1,0:T(8,128)(2,1)}, bf16[128,2048]{1,0:T(8,128)(2,1)S(1)}, u32[]{:S(2)}, u32[]{:S(2)}) collective-permute-start(bf16[128,2048]{1,0:T(8,128)(2,1)} %bitcast.22.refs_0_), channel_id=1, source_target_pairs={{0,80},{32,112},{64,0},{96,32},{16,64},{48,96},{80,16},{112,48},{1... | collective-permute-start | bytes 1572872 | tf_op jit(solution)/shard_map/share_cotangent/ppermute | solution.py:327
  36.2 24.5 %all-to-all-start.1 = ((bf16[16,24,16,128]{3,2,1,0:T(8,128)(2,1)}), bf16[16,24,16,128]{3,2,1,0:T(8,128)(2,1)S(1)}, u32[]{:S(2)}, u32[]{:S(2)}) async-start(bf16[16,24,16,128]{3,2,1,0:T(8,128)(2,1)} %constant_dynamic-update-slice_fusion.2), calls=%async_computation.1 | async-start | bytes 3145728 | tf_op jit(solution)/shard_map/conv_a2a/all_to_all | solution.py:377
  39.9 8.2 %collective-permute-start.2 = (bf16[64,2048]{1,0:T(8,128)(2,1)S(1)}, bf16[64,2048]{1,0:T(8,128)(2,1)S(1)}, u32[]{:S(2)}, u32[]{:S(2)}) collective-permute-start(bf16[64,2048]{1,0:T(8,128)(2,1)S(1)} %slice.18), channel_id=1, source_target_pairs={{0,64},{32,96},{64,16},{96,48},{16,80},{48,112},{80,0},{112,32},{1... | collective-permute-start | bytes 786440 | tf_op jit(solution)/shard_map/share_cotangent/ppermute | solution.py:327
  40.2 8.7 %collective-permute-start.3 = (bf16[64,2048]{1,0:T(8,128)(2,1)S(1)}, bf16[64,2048]{1,0:T(8,128)(2,1)S(1)}, u32[]{:S(2)}, u32[]{:S(2)}) collective-permute-start(bf16[64,2048]{1,0:T(8,128)(2,1)S(1)} %slice.19), channel_id=1, source_target_pairs={{0,80},{32,112},{64,0},{96,32},{16,64},{48,96},{80,16},{112,48},{1... | collective-permute-start | bytes 786440 | tf_op jit(solution)/shard_map/share_cotangent/ppermute | solution.py:327
  42.8 8.7 %collective-permute-start.4 = (bf16[128,2048]{1,0:T(8,128)(2,1)}, bf16[128,2048]{1,0:T(8,128)(2,1)}, u32[]{:S(2)}, u32[]{:S(2)}) collective-permute-start(bf16[128,2048]{1,0:T(8,128)(2,1)} %bitcast.22.refs_0_), channel_id=1, source_target_pairs={{0,32},{32,0},{64,96},{96,64},{16,48},{48,16},{80,112},{112,80},{1... | collective-permute-start | bytes 1572872 | tf_op jit(solution)/shard_map/share_cotangent/ppermute | solution.py:327
  44.2 7.3 %collective-permute-start.5 = (bf16[128,2048]{1,0:T(8,128)(2,1)S(1)}, bf16[128,2048]{1,0:T(8,128)(2,1)}, u32[]{:S(2)}, u32[]{:S(2)}) collective-permute-start(bf16[128,2048]{1,0:T(8,128)(2,1)S(1)} %collective-permute-done.refs_1_), channel_id=1, source_target_pairs={{0,32},{32,0},{64,96},{96,64},{16,48},{48,16},{80,112},{112,80},{1... | collective-permute-start | bytes 1572872 | tf_op jit(solution)/shard_map/share_cotangent/ppermute | solution.py:327
  44.2 7.3 %collective-permute-start.6 = (bf16[128,2048]{1,0:T(8,128)(2,1)S(1)}, bf16[128,2048]{1,0:T(8,128)(2,1)}, u32[]{:S(2)}, u32[]{:S(2)}) collective-permute-start(bf16[128,2048]{1,0:T(8,128)(2,1)S(1)} %collective-permute-done.1.refs_2_), channel_id=1, source_target_pairs={{0,32},{32,0},{64,96},{96,64},{16,48},{48,16},{80,112},{112,80},{1... | collective-permute-start | bytes 1572872 | tf_op jit(solution)/shard_map/share_cotangent/ppermute | solution.py:327
  49.6 3.7 %collective-permute-start.7 = (bf16[128,2048]{1,0:T(8,128)(2,1)}, bf16[128,2048]{1,0:T(8,128)(2,1)}, u32[]{:S(2)}, u32[]{:S(2)}) collective-permute-start(bf16[128,2048]{1,0:T(8,128)(2,1)} %constant_dynamic-update-slice_fusion.refs_3_), channel_id=1, source_target_pairs={{0,32},{32,0},{64,96},{96,64},{16,48},{48,16},{80,112},{112,80},{1... | collective-permute-start | bytes 1572872 | tf_op jit(solution)/shard_map/share_cotangent/ppermute | solution.py:327
  64.2 0.8 copy-start.1
  65.0 14.4 %all-to-all-start.3 = ((bf16[16,8,16,128]{3,2,1,0:T(8,128)(2,1)}), bf16[16,8,16,128]{3,2,1,0:T(8,128)(2,1)}, u32[]{:S(2)}, u32[]{:S(2)}) async-start(bf16[16,8,16,128]{3,2,1,0:T(8,128)(2,1)} %copy-done.1), calls=%async_computation.3 | async-start | bytes 1048576 | tf_op jit(solution)/shard_map/dconv_a2a/all_to_all | solution.py:381
  79.4 25.3 %all-to-all-start.2 = ((bf16[16,16,2048]{2,1,0:T(8,128)(2,1)}), bf16[16,16,2048]{2,1,0:T(8,128)(2,1)S(1)}, u32[]{:S(2)}, u32[]{:S(2)}) async-start(bf16[16,16,2048]{2,1,0:T(8,128)(2,1)} %bitcast.23), calls=%async_computation.2 | async-start | bytes 2097152 | tf_op jit(solution)/shard_map/grad_proj_a2a/all_to_all | solution.py:402
  91.0 20.7 %collective-permute-start.8 = (bf16[16,32,128]{2,1,0:T(8,128)(2,1)S(1)}, bf16[16,32,128]{2,1,0:T(8,128)(2,1)S(1)}, u32[]{:S(2)}, u32[]{:S(2)}) collective-permute-start(bf16[16,32,128]{2,1,0:T(8,128)(2,1)S(1)} %bitcast.82), channel_id=1, source_target_pairs={{0,0},{1,32},{2,64},{3,96},{4,1},{5,33},{6,65},{7,97},{8,2},{9,34}... | collective-permute-start | bytes 393224 | tf_op jit(solution)/shard_map/grad_taps/ppermute | solution.py:398
  104.7 20.5 %all-to-all-start.4 = ((bf16[128,16,128]{2,1,0:T(8,128)(2,1)}), bf16[128,16,128]{2,1,0:T(8,128)(2,1)S(1)}, u32[]{:S(2)}, u32[]{:S(2)}) async-start(bf16[128,16,128]{2,1,0:T(8,128)(2,1)} %copy.31), calls=%async_computation.4 | async-start | bytes 1048576 | tf_op jit(solution)/shard_map/grad_in_a2a/all_to_all | solution.py:406
  111.7 13.5 %collective-permute-start.9 = (bf16[16,8,128]{2,1,0:T(8,128)(2,1)S(1)}, bf16[16,8,128]{2,1,0:T(8,128)(2,1)S(1)}, u32[]{:S(2)}, u32[]{:S(2)}) collective-permute-start(bf16[16,8,128]{2,1,0:T(8,128)(2,1)S(1)} %get-tuple-element.28), channel_id=1, source_target_pairs={{0,32},{32,0},{64,96},{96,64},{1,33},{33,1},{65,97},{97,65},{2,34}... | collective-permute-start | bytes 98312 | tf_op jit(solution)/shard_map/grad_filter/ppermute | solution.py:413
  112.8 12.4 %collective-permute-start.10 = (bf16[16,8,128]{2,1,0:T(8,128)(2,1)S(1)}, bf16[16,8,128]{2,1,0:T(8,128)(2,1)S(1)}, u32[]{:S(2)}, u32[]{:S(2)}) collective-permute-start(bf16[16,8,128]{2,1,0:T(8,128)(2,1)S(1)} %get-tuple-element.27), channel_id=1, source_target_pairs={{0,64},{32,96},{64,0},{96,32},{1,65},{33,97},{65,1},{97,33},{2,66}... | collective-permute-start | bytes 98312 | tf_op jit(solution)/shard_map/grad_filter/ppermute | solution.py:413
  113.6 11.6 %collective-permute-start.11 = (bf16[16,8,128]{2,1,0:T(8,128)(2,1)S(1)}, bf16[16,8,128]{2,1,0:T(8,128)(2,1)S(1)}, u32[]{:S(2)}, u32[]{:S(2)}) collective-permute-start(bf16[16,8,128]{2,1,0:T(8,128)(2,1)S(1)} %get-tuple-element.26), channel_id=1, source_target_pairs={{0,96},{32,64},{64,32},{96,0},{1,97},{33,65},{65,33},{97,1},{2,98}... | collective-permute-start | bytes 98312 | tf_op jit(solution)/shard_map/grad_filter/ppermute | solution.py:413

commit v7 on v6

--- a/solution.py
+++ b/solution.py
@@ -169,7 +169,7 @@
         ],
         out_specs=per_channel(MANY, field.shape),
         out_shape=jax.ShapeDtypeStruct((chans, rows, LANES), bf16),
-        compiler_params=pltpu.CompilerParams(vmem_limit_bytes=24 << 20),
+        compiler_params=pltpu.CompilerParams(vmem_limit_bytes=16 << 20),
         cost_estimate=estimate(1 << 20),
     )(skip, field, taps)
 
@@ -191,7 +191,7 @@
             pltpu.VMEM((MANY, 2, 2 * rows, LANES), bf16),
             pltpu.VMEM(out.shape, f32),
         ],
-        compiler_params=pltpu.CompilerParams(vmem_limit_bytes=24 << 20),
+        compiler_params=pltpu.CompilerParams(vmem_limit_bytes=16 << 20),
         cost_estimate=estimate(1 << 20),
     )(scale, x, d).reshape(chans, rows // seqs, LANES)
 
@@ -264,7 +264,7 @@
         out_specs=whole(1)[0],
         out_shape=jax.ShapeDtypeStruct((plane, len(pieces), chans, LANES), bf16),
         scratch_shapes=[pltpu.VMEM((plane * chans, pieces[0].shape[1]), bf16)],
-        compiler_params=pltpu.CompilerParams(vmem_limit_bytes=32 << 20),
+        compiler_params=pltpu.CompilerParams(vmem_limit_bytes=16 << 20),
         cost_estimate=pl.CostEstimate(flops=1 << 30, bytes_accessed=6 << 20, transcendentals=0),
     )(place, load, *pieces)
 
@@ -301,7 +301,7 @@
         out_specs=whole(1)[0],
         out_shape=jax.ShapeDtypeStruct((rows, width), jnp.bfloat16),
         scratch_shapes=[pltpu.VMEM((rows, len(pieces) * LANES), jnp.bfloat16)],
-        compiler_params=pltpu.CompilerParams(vmem_limit_bytes=32 << 20),
+        compiler_params=pltpu.CompilerParams(vmem_limit_bytes=16 << 20),
         cost_estimate=pl.CostEstimate(flops=1 << 30, bytes_accessed=6 << 20, transcendentals=0),
     )(place, conv, *pieces)
 

time: 128 us -> 128 us (level)
  no operation moved by 1% of the time
where the time goes in v7:
time: 128 us; the launch traced here: 127 us
  starting transfers between devices  51.5 us (40%)
  waiting for transfers between devices  36.8 us (29%)
  Pallas kernels  26.2 us (20%)
  local copies, waits for them, and re-layouts  9.04 us (7%)
  other arithmetic  1.57 us (1%)
    all_to_all x1, starting transfers between devices, on_device(): load = lax.all_to_all(load, POS + SEQ, 0, 0)  11.5 us
    ppermute x8, starting transfers between devices, move(): return lax.ppermute(a, COLUMN, column_pairs(step, other))  9.95 us
    all_to_all x1, waiting for transfers between devices, on_device(): grad_in = lax.all_to_all(grad_in, POS + SEQ, 0, 0)  9.79 us
    pallas_call x2, Pallas kernels, conv_call(): pl.pallas_call(functools.partial(kernel, seqs), grid=(chans // MANY,), in...  9.61 us
    all_to_all x1, waiting for transfers between devices, on_device(): load = lax.all_to_all(load, POS + SEQ, 0, 0)  9.04 us
    ppermute x1, starting transfers between devices, on_device(): held = lax.ppermute(grad_taps, SEQ + POS, pairs)  7.68 us
    all_to_all x1, waiting for transfers between devices, on_device(): load = lax.all_to_all(load, PLANE, 0, 0)  7.44 us
    all_to_all x1, starting transfers between devices, on_device(): grad_in = lax.all_to_all(grad_in, POS + SEQ, 0, 0)  6.95 us
  transfers between devices with their start and end apart: 17, of which 6 were waited for; matrix products, arithmetic and copies ran while one was open for 7% of the time, Pallas kernels for 16%

profile of v7, /device:TPU:1, one launch (start us, length us, event | category | flops | bytes accessed | tf_op | source)
XLA Modules:
  0.0 127.2 jit_solution(6603448309728977075)
XLA Ops:
  0.6 0.0 copy-start
  0.7 2.6 %signal.1 = bf16[32,4,5,4,128]{4,3,2,1,0:T(4,128)(2,1)} custom-call(s32[1]{0:T(128)} %bitcast.9.me_ref, bf16[128,2048]{1,0:T(8,128)(2,1)} %bitcast.89, f32[16,128]{1,0:T(8,128)} %bitcast.99, bf16[2048,128]{1,0:T(8,128)(2,1)} %taps_ref.1), custom_call_target="tpu_custom_call" | custom-call | flops 1048576 | bytes 65536 | tf_op jit(solution)/shard_map/signal/pallas_call | solution.py:278
  3.2 11.5 %all-to-all-start = ((bf16[128,5,4,128]{3,2,1,0:T(4,128)(2,1)}), bf16[128,5,4,128]{3,2,1,0:T(4,128)(2,1)S(1)}, u32[]{:S(2)}, u32[]{:S(2)}) async-start(bf16[128,5,4,128]{3,2,1,0:T(4,128)(2,1)} %bitcast.83), calls=%async_computation | async-start | bytes 1310720 | tf_op jit(solution)/shard_map/signal_a2a/all_to_all | solution.py:348
  14.7 1.6 %collective-permute-start = (bf16[128,2048]{1,0:T(8,128)(2,1)}, bf16[128,2048]{1,0:T(8,128)(2,1)S(1)}, u32[]{:S(2)}, u32[]{:S(2)}) collective-permute-start(bf16[128,2048]{1,0:T(8,128)(2,1)} %bitcast.22.refs_0_), channel_id=1, source_target_pairs={{0,64},{32,96},{64,16},{96,48},{16,80},{48,112},{80,0},{112,32},{1... | collective-permute-start | bytes 1572872 | tf_op jit(solution)/shard_map/share_cotangent/ppermute | solution.py:327
  16.3 1.8 %collective-permute-start.1 = (bf16[128,2048]{1,0:T(8,128)(2,1)}, bf16[128,2048]{1,0:T(8,128)(2,1)S(1)}, u32[]{:S(2)}, u32[]{:S(2)}) collective-permute-start(bf16[128,2048]{1,0:T(8,128)(2,1)} %bitcast.22.refs_0_), channel_id=1, source_target_pairs={{0,80},{32,112},{64,0},{96,32},{16,64},{48,96},{80,16},{112,48},{1... | collective-permute-start | bytes 1572872 | tf_op jit(solution)/shard_map/share_cotangent/ppermute | solution.py:327
  18.2 0.8 dynamic_slice.22.skip_ref
  18.9 0.2 broadcast_in_dim.12
  19.1 1.5 %pad.4 = bf16[16,24,16,128]{3,2,1,0:T(8,128)(2,1)} pad(bf16[16,16,16,128]{3,2,1,0:T(8,128)(2,1)S(1)} %broadcast_in_dim.12, bf16[]{:T(256)} %constant.114.clone.1), padding=0_0x0_8x0_0x0_0 | pad | bytes 2621442 | tf_op jit(solution)/shard_map/weight_load/jit(_pad)/pad | solution.py:367
  20.6 9.0 %all-to-all-done = bf16[128,5,4,128]{3,2,1,0:T(4,128)(2,1)S(1)} async-done(((bf16[128,5,4,128]{3,2,1,0:T(4,128)(2,1)}), bf16[128,5,4,128]{3,2,1,0:T(4,128)(2,1)S(1)}, u32[]{:S(2)}, u32[]{:S(2)}) %all-to-all-start) | async-done | bytes 655392 | tf_op jit(solution)/shard_map/signal_a2a/all_to_all | solution.py:348
  29.6 0.1 copy.27
  29.9 4.8 %conv.1 = bf16[16,128,128]{2,1,0:T(8,128)(2,1)S(1)} custom-call(f32[16]{0:T(128)S(1)} %dynamic_slice.22.skip_ref, bf16[16,128,128]{2,1,0:T(8,128)(2,1)S(1)} %slice_bitcast_fusion.x_ref, bf16[16,32,128]{2,1,0:T(8,128)(2,1)S(1)} %bitcast.80), custom_call_target="tpu_custom_call" | custom-call | flops 1048576 | bytes 65536 | tf_op jit(solution)/shard_map/conv/pallas_call | solution.py:162
  34.7 0.6 copy.29
  35.3 0.9 constant_dynamic-update-slice_fusion.2
  36.2 3.7 %all-to-all-start.1 = ((bf16[16,24,16,128]{3,2,1,0:T(8,128)(2,1)}), bf16[16,24,16,128]{3,2,1,0:T(8,128)(2,1)S(1)}, u32[]{:S(2)}, u32[]{:S(2)}) async-start(bf16[16,24,16,128]{3,2,1,0:T(8,128)(2,1)} %constant_dynamic-update-slice_fusion.2), calls=%async_computation.1 | async-start | bytes 3145728 | tf_op jit(solution)/shard_map/conv_a2a/all_to_all | solution.py:377
  39.9 0.0 collective-permute-done.refs_1_
  39.9 0.2 collective-permute-start.2
  40.1 0.0 collective-permute-done.1.refs_2_
  40.2 2.6 %collective-permute-start.3 = (bf16[64,2048]{1,0:T(8,128)(2,1)S(1)}, bf16[64,2048]{1,0:T(8,128)(2,1)S(1)}, u32[]{:S(2)}, u32[]{:S(2)}) collective-permute-start(bf16[64,2048]{1,0:T(8,128)(2,1)S(1)} %slice.19), channel_id=1, source_target_pairs={{0,80},{32,112},{64,0},{96,32},{16,64},{48,96},{80,16},{112,48},{1... | collective-permute-start | bytes 786440 | tf_op jit(solution)/shard_map/share_cotangent/ppermute | solution.py:327
  42.8 1.4 %collective-permute-start.4 = (bf16[128,2048]{1,0:T(8,128)(2,1)}, bf16[128,2048]{1,0:T(8,128)(2,1)}, u32[]{:S(2)}, u32[]{:S(2)}) collective-permute-start(bf16[128,2048]{1,0:T(8,128)(2,1)} %bitcast.22.refs_0_), channel_id=1, source_target_pairs={{0,32},{32,0},{64,96},{96,64},{16,48},{48,16},{80,112},{112,80},{1... | collective-permute-start | bytes 1572872 | tf_op jit(solution)/shard_map/share_cotangent/ppermute | solution.py:327
  44.2 0.0 collective-permute-start.5
  44.2 0.5 collective-permute-start.6
  44.7 3.4 %collective-permute-done.2 = bf16[64,2048]{1,0:T(8,128)(2,1)S(1)} collective-permute-done((bf16[64,2048]{1,0:T(8,128)(2,1)S(1)}, bf16[64,2048]{1,0:T(8,128)(2,1)S(1)}, u32[]{:S(2)}, u32[]{:S(2)}) %collective-permute-start.2) | collective-permute-done | bytes 262176 | tf_op jit(solution)/shard_map/share_cotangent/ppermute | solution.py:327
  48.1 0.7 constant_dynamic-update-slice_fusion.1
  48.9 0.7 constant_dynamic-update-slice_fusion.refs_3_
  49.6 1.8 %collective-permute-start.7 = (bf16[128,2048]{1,0:T(8,128)(2,1)}, bf16[128,2048]{1,0:T(8,128)(2,1)}, u32[]{:S(2)}, u32[]{:S(2)}) collective-permute-start(bf16[128,2048]{1,0:T(8,128)(2,1)} %constant_dynamic-update-slice_fusion.refs_3_), channel_id=1, source_target_pairs={{0,32},{32,0},{64,96},{96,64},{16,48},{48,16},{80,112},{112,80},{1... | collective-permute-start | bytes 1572872 | tf_op jit(solution)/shard_map/share_cotangent/ppermute | solution.py:327
  51.4 0.1 stack.48.place_ref
  51.5 1.8 %collective-permute-done.7.refs_7_ = bf16[128,2048]{1,0:T(8,128)(2,1)} collective-permute-done((bf16[128,2048]{1,0:T(8,128)(2,1)}, bf16[128,2048]{1,0:T(8,128)(2,1)}, u32[]{:S(2)}, u32[]{:S(2)}) %collective-permute-start.7) | collective-permute-done | bytes 524320 | tf_op jit(solution)/shard_map/share_cotangent/ppermute | solution.py:327
  53.2 7.4 %all-to-all-done.1.c_ref.w_ref = bf16[16,24,16,128]{3,2,1,0:T(8,128)(2,1)S(1)} async-done(((bf16[16,24,16,128]{3,2,1,0:T(8,128)(2,1)}), bf16[16,24,16,128]{3,2,1,0:T(8,128)(2,1)S(1)}, u32[]{:S(2)}, u32[]{:S(2)}) %all-to-all-start.1) | async-done | bytes 1572896 | tf_op jit(solution)/shard_map/conv_a2a/all_to_all | solution.py:377
  60.7 3.5 %dconv.1 = bf16[16,8,16,128]{3,2,1,0:T(8,128)(2,1)S(1)} custom-call(s32[8]{0:T(128)S(1)} %stack.48.place_ref, bf16[16,24,16,128]{3,2,1,0:T(8,128)(2,1)S(1)} %all-to-all-done.1.c_ref.w_ref, bf16[128,2048]{1,0:T(8,128)(2,1)} %bitcast.22.refs_0_, bf16[128,2048]{1,0:T(8,128)(2,1)S(1)} %collective-permute-done.refs_1_, ...), custom_call_target="tpu_custom_call" | custom-call | flops 1073741824 | bytes 6291456 | tf_op jit(solution)/shard_map/dconv/pallas_call | solution.py:261
  64.2 0.8 copy-done.1
  65.0 5.0 %all-to-all-start.3 = ((bf16[16,8,16,128]{3,2,1,0:T(8,128)(2,1)}), bf16[16,8,16,128]{3,2,1,0:T(8,128)(2,1)}, u32[]{:S(2)}, u32[]{:S(2)}) async-start(bf16[16,8,16,128]{3,2,1,0:T(8,128)(2,1)} %copy-done.1), calls=%async_computation.3 | async-start | bytes 1048576 | tf_op jit(solution)/shard_map/dconv_a2a/all_to_all | solution.py:381
  70.0 4.1 %grad_proj.1 = bf16[256,2048]{1,0:T(8,128)(2,1)} custom-call(s32[8]{0:T(128)S(1)} %stack.48.place_ref, bf16[16,24,16,128]{3,2,1,0:T(8,128)(2,1)S(1)} %all-to-all-done.1.c_ref.w_ref, bf16[128,2048]{1,0:T(8,128)(2,1)} %bitcast.22.refs_0_, bf16[128,2048]{1,0:T(8,128)(2,1)S(1)} %collective-permute-done.refs_1_, ...), custom_call_target="tpu_custom_call" | custom-call | flops 1073741824 | bytes 6291456 | tf_op jit(solution)/shard_map/grad_proj/pallas_call | solution.py:298
  74.2 5.2 %all-to-all-done.3 = bf16[16,8,16,128]{3,2,1,0:T(8,128)(2,1)} async-done(((bf16[16,8,16,128]{3,2,1,0:T(8,128)(2,1)}), bf16[16,8,16,128]{3,2,1,0:T(8,128)(2,1)}, u32[]{:S(2)}, u32[]{:S(2)}) %all-to-all-start.3) | async-done | bytes 524320 | tf_op jit(solution)/shard_map/dconv_a2a/all_to_all | solution.py:381
  79.4 3.8 %all-to-all-start.2 = ((bf16[16,16,2048]{2,1,0:T(8,128)(2,1)}), bf16[16,16,2048]{2,1,0:T(8,128)(2,1)S(1)}, u32[]{:S(2)}, u32[]{:S(2)}) async-start(bf16[16,16,2048]{2,1,0:T(8,128)(2,1)} %bitcast.23), calls=%async_computation.2 | async-start | bytes 2097152 | tf_op jit(solution)/shard_map/grad_proj_a2a/all_to_all | solution.py:402
  83.3 1.3 %copy.30 = bf16[2,2,2,2,2,4,16,128]{7,5,2,3,0,1,4,6:T(4,128)(2,1)S(1)} copy(bf16[2,2,2,2,2,4,16,128]{7,6,5,4,3,2,1,0:T(8,128)(2,1)} %bitcast.24) | data formatting | bytes 1048576 | tf_op jit(solution)/shard_map/dconv_a2a/reshape | solution.py:382
  84.6 6.4 %grad_taps.1 = bf16[512,128]{1,0:T(8,128)(2,1)S(1)} custom-call(f32[1]{0:T(128)} %constant.121.clone.1.scale_ref, bf16[16,128,128]{2,1,0:T(8,128)(2,1)S(1)} %slice_bitcast_fusion.x_ref, bf16[16,128,128]{2,1,0:T(8,128)(2,1)S(1)} %bitcast.76), custom_call_target="tpu_custom_call" | custom-call | flops 1048576 | bytes 65536 | tf_op jit(solution)/shard_map/grad_taps/pallas_call | solution.py:180
  91.0 7.7 %collective-permute-start.8 = (bf16[16,32,128]{2,1,0:T(8,128)(2,1)S(1)}, bf16[16,32,128]{2,1,0:T(8,128)(2,1)S(1)}, u32[]{:S(2)}, u32[]{:S(2)}) collective-permute-start(bf16[16,32,128]{2,1,0:T(8,128)(2,1)S(1)} %bitcast.82), channel_id=1, source_target_pairs={{0,0},{1,32},{2,64},{3,96},{4,1},{5,33},{6,65},{7,97},{8,2},{9,34}... | collective-permute-start | bytes 393224 | tf_op jit(solution)/shard_map/grad_taps/ppermute | solution.py:398
  98.7 4.8 %grad_in.1 = bf16[16,128,128]{2,1,0:T(8,128)(2,1)S(1)} custom-call(f32[16]{0:T(128)S(1)} %dynamic_slice.22.skip_ref, bf16[16,128,128]{2,1,0:T(8,128)(2,1)S(1)} %bitcast.77, bf16[16,32,128]{2,1,0:T(8,128)(2,1)S(1)} %bitcast.81), custom_call_target="tpu_custom_call" | custom-call | flops 1048576 | bytes 65536 | tf_op jit(solution)/shard_map/grad_in/pallas_call | solution.py:162
  103.5 1.1 copy.31
  104.7 7.0 %all-to-all-start.4 = ((bf16[128,16,128]{2,1,0:T(8,128)(2,1)}), bf16[128,16,128]{2,1,0:T(8,128)(2,1)S(1)}, u32[]{:S(2)}, u32[]{:S(2)}) async-start(bf16[128,16,128]{2,1,0:T(8,128)(2,1)} %copy.31), calls=%async_computation.4 | async-start | bytes 1048576 | tf_op jit(solution)/shard_map/grad_in_a2a/all_to_all | solution.py:406
  111.7 1.1 collective-permute-start.9
  112.8 0.8 collective-permute-start.10
  113.6 0.9 collective-permute-start.11
  114.6 0.1 convert_reduce_fusion
  114.7 0.7 broadcast_multiply_fusion
  115.4 9.8 %all-to-all-done.4 = bf16[128,16,128]{2,1,0:T(8,128)(2,1)S(1)} async-done(((bf16[128,16,128]{2,1,0:T(8,128)(2,1)}), bf16[128,16,128]{2,1,0:T(8,128)(2,1)S(1)}, u32[]{:S(2)}, u32[]{:S(2)}) %all-to-all-start.4) | async-done | bytes 524320 | tf_op jit(solution)/shard_map/grad_in_a2a/all_to_all | solution.py:406
  125.3 0.7 maximum_convert_fusion
  126.1 1.1 fusion
  (24 shorter events, 0.3 us)
Async XLA Ops:
  0.6 18.3 %copy-start = (bf16[16,2048]{1,0:T(8,128)(2,1)S(1)}, bf16[16,2048]{1,0:T(8,128)(2,1)}, u32[]{:S(2)}) copy-start(bf16[16,2048]{1,0:T(8,128)(2,1)} %param.11) | copy-start | bytes 196612
  3.2 26.4 %all-to-all-start = ((bf16[128,5,4,128]{3,2,1,0:T(4,128)(2,1)}), bf16[128,5,4,128]{3,2,1,0:T(4,128)(2,1)S(1)}, u32[]{:S(2)}, u32[]{:S(2)}) async-start(bf16[128,5,4,128]{3,2,1,0:T(4,128)(2,1)} %bitcast.83), calls=%async_computation | async-start | bytes 1310720 | tf_op jit(solution)/shard_map/signal_a2a/all_to_all | solution.py:348
  14.7 25.1 %collective-permute-start = (bf16[128,2048]{1,0:T(8,128)(2,1)}, bf16[128,2048]{1,0:T(8,128)(2,1)S(1)}, u32[]{:S(2)}, u32[]{:S(2)}) collective-permute-start(bf16[128,2048]{1,0:T(8,128)(2,1)} %bitcast.22.refs_0_), channel_id=1, source_target_pairs={{0,64},{32,96},{64,16},{96,48},{16,80},{48,112},{80,0},{112,32},{1... | collective-permute-start | bytes 1572872 | tf_op jit(solution)/shard_map/share_cotangent/ppermute | solution.py:327
  16.3 23.8 %collective-permute-start.1 = (bf16[128,2048]{1,0:T(8,128)(2,1)}, bf16[128,2048]{1,0:T(8,128)(2,1)S(1)}, u32[]{:S(2)}, u32[]{:S(2)}) collective-permute-start(bf16[128,2048]{1,0:T(8,128)(2,1)} %bitcast.22.refs_0_), channel_id=1, source_target_pairs={{0,80},{32,112},{64,0},{96,32},{16,64},{48,96},{80,16},{112,48},{1... | collective-permute-start | bytes 1572872 | tf_op jit(solution)/shard_map/share_cotangent/ppermute | solution.py:327
  36.2 24.5 %all-to-all-start.1 = ((bf16[16,24,16,128]{3,2,1,0:T(8,128)(2,1)}), bf16[16,24,16,128]{3,2,1,0:T(8,128)(2,1)S(1)}, u32[]{:S(2)}, u32[]{:S(2)}) async-start(bf16[16,24,16,128]{3,2,1,0:T(8,128)(2,1)} %constant_dynamic-update-slice_fusion.2), calls=%async_computation.1 | async-start | bytes 3145728 | tf_op jit(solution)/shard_map/conv_a2a/all_to_all | solution.py:377
  39.9 8.2 %collective-permute-start.2 = (bf16[64,2048]{1,0:T(8,128)(2,1)S(1)}, bf16[64,2048]{1,0:T(8,128)(2,1)S(1)}, u32[]{:S(2)}, u32[]{:S(2)}) collective-permute-start(bf16[64,2048]{1,0:T(8,128)(2,1)S(1)} %slice.18), channel_id=1, source_target_pairs={{0,64},{32,96},{64,16},{96,48},{16,80},{48,112},{80,0},{112,32},{1... | collective-permute-start | bytes 786440 | tf_op jit(solution)/shard_map/share_cotangent/ppermute | solution.py:327
  40.2 8.7 %collective-permute-start.3 = (bf16[64,2048]{1,0:T(8,128)(2,1)S(1)}, bf16[64,2048]{1,0:T(8,128)(2,1)S(1)}, u32[]{:S(2)}, u32[]{:S(2)}) collective-permute-start(bf16[64,2048]{1,0:T(8,128)(2,1)S(1)} %slice.19), channel_id=1, source_target_pairs={{0,80},{32,112},{64,0},{96,32},{16,64},{48,96},{80,16},{112,48},{1... | collective-permute-start | bytes 786440 | tf_op jit(solution)/shard_map/share_cotangent/ppermute | solution.py:327
  42.8 8.7 %collective-permute-start.4 = (bf16[128,2048]{1,0:T(8,128)(2,1)}, bf16[128,2048]{1,0:T(8,128)(2,1)}, u32[]{:S(2)}, u32[]{:S(2)}) collective-permute-start(bf16[128,2048]{1,0:T(8,128)(2,1)} %bitcast.22.refs_0_), channel_id=1, source_target_pairs={{0,32},{32,0},{64,96},{96,64},{16,48},{48,16},{80,112},{112,80},{1... | collective-permute-start | bytes 1572872 | tf_op jit(solution)/shard_map/share_cotangent/ppermute | solution.py:327
  44.2 7.3 %collective-permute-start.5 = (bf16[128,2048]{1,0:T(8,128)(2,1)S(1)}, bf16[128,2048]{1,0:T(8,128)(2,1)}, u32[]{:S(2)}, u32[]{:S(2)}) collective-permute-start(bf16[128,2048]{1,0:T(8,128)(2,1)S(1)} %collective-permute-done.refs_1_), channel_id=1, source_target_pairs={{0,32},{32,0},{64,96},{96,64},{16,48},{48,16},{80,112},{112,80},{1... | collective-permute-start | bytes 1572872 | tf_op jit(solution)/shard_map/share_cotangent/ppermute | solution.py:327
  44.2 7.3 %collective-permute-start.6 = (bf16[128,2048]{1,0:T(8,128)(2,1)S(1)}, bf16[128,2048]{1,0:T(8,128)(2,1)}, u32[]{:S(2)}, u32[]{:S(2)}) collective-permute-start(bf16[128,2048]{1,0:T(8,128)(2,1)S(1)} %collective-permute-done.1.refs_2_), channel_id=1, source_target_pairs={{0,32},{32,0},{64,96},{96,64},{16,48},{48,16},{80,112},{112,80},{1... | collective-permute-start | bytes 1572872 | tf_op jit(solution)/shard_map/share_cotangent/ppermute | solution.py:327
  49.6 3.7 %collective-permute-start.7 = (bf16[128,2048]{1,0:T(8,128)(2,1)}, bf16[128,2048]{1,0:T(8,128)(2,1)}, u32[]{:S(2)}, u32[]{:S(2)}) collective-permute-start(bf16[128,2048]{1,0:T(8,128)(2,1)} %constant_dynamic-update-slice_fusion.refs_3_), channel_id=1, source_target_pairs={{0,32},{32,0},{64,96},{96,64},{16,48},{48,16},{80,112},{112,80},{1... | collective-permute-start | bytes 1572872 | tf_op jit(solution)/shard_map/share_cotangent/ppermute | solution.py:327
  64.2 0.8 copy-start.1
  65.0 14.4 %all-to-all-start.3 = ((bf16[16,8,16,128]{3,2,1,0:T(8,128)(2,1)}), bf16[16,8,16,128]{3,2,1,0:T(8,128)(2,1)}, u32[]{:S(2)}, u32[]{:S(2)}) async-start(bf16[16,8,16,128]{3,2,1,0:T(8,128)(2,1)} %copy-done.1), calls=%async_computation.3 | async-start | bytes 1048576 | tf_op jit(solution)/shard_map/dconv_a2a/all_to_all | solution.py:381
  79.4 25.3 %all-to-all-start.2 = ((bf16[16,16,2048]{2,1,0:T(8,128)(2,1)}), bf16[16,16,2048]{2,1,0:T(8,128)(2,1)S(1)}, u32[]{:S(2)}, u32[]{:S(2)}) async-start(bf16[16,16,2048]{2,1,0:T(8,128)(2,1)} %bitcast.23), calls=%async_computation.2 | async-start | bytes 2097152 | tf_op jit(solution)/shard_map/grad_proj_a2a/all_to_all | solution.py:402
  91.0 20.7 %collective-permute-start.8 = (bf16[16,32,128]{2,1,0:T(8,128)(2,1)S(1)}, bf16[16,32,128]{2,1,0:T(8,128)(2,1)S(1)}, u32[]{:S(2)}, u32[]{:S(2)}) collective-permute-start(bf16[16,32,128]{2,1,0:T(8,128)(2,1)S(1)} %bitcast.82), channel_id=1, source_target_pairs={{0,0},{1,32},{2,64},{3,96},{4,1},{5,33},{6,65},{7,97},{8,2},{9,34}... | collective-permute-start | bytes 393224 | tf_op jit(solution)/shard_map/grad_taps/ppermute | solution.py:398
  104.7 20.5 %all-to-all-start.4 = ((bf16[128,16,128]{2,1,0:T(8,128)(2,1)}), bf16[128,16,128]{2,1,0:T(8,128)(2,1)S(1)}, u32[]{:S(2)}, u32[]{:S(2)}) async-start(bf16[128,16,128]{2,1,0:T(8,128)(2,1)} %copy.31), calls=%async_computation.4 | async-start | bytes 1048576 | tf_op jit(solution)/shard_map/grad_in_a2a/all_to_all | solution.py:406
  111.7 13.5 %collective-permute-start.9 = (bf16[16,8,128]{2,1,0:T(8,128)(2,1)S(1)}, bf16[16,8,128]{2,1,0:T(8,128)(2,1)S(1)}, u32[]{:S(2)}, u32[]{:S(2)}) collective-permute-start(bf16[16,8,128]{2,1,0:T(8,128)(2,1)S(1)} %get-tuple-element.28), channel_id=1, source_target_pairs={{0,32},{32,0},{64,96},{96,64},{1,33},{33,1},{65,97},{97,65},{2,34}... | collective-permute-start | bytes 98312 | tf_op jit(solution)/shard_map/grad_filter/ppermute | solution.py:413
  112.8 12.4 %collective-permute-start.10 = (bf16[16,8,128]{2,1,0:T(8,128)(2,1)S(1)}, bf16[16,8,128]{2,1,0:T(8,128)(2,1)S(1)}, u32[]{:S(2)}, u32[]{:S(2)}) collective-permute-start(bf16[16,8,128]{2,1,0:T(8,128)(2,1)S(1)} %get-tuple-element.27), channel_id=1, source_target_pairs={{0,64},{32,96},{64,0},{96,32},{1,65},{33,97},{65,1},{97,33},{2,66}... | collective-permute-start | bytes 98312 | tf_op jit(solution)/shard_map/grad_filter/ppermute | solution.py:413
  113.6 11.6 %collective-permute-start.11 = (bf16[16,8,128]{2,1,0:T(8,128)(2,1)S(1)}, bf16[16,8,128]{2,1,0:T(8,128)(2,1)S(1)}, u32[]{:S(2)}, u32[]{:S(2)}) collective-permute-start(bf16[16,8,128]{2,1,0:T(8,128)(2,1)S(1)} %get-tuple-element.26), channel_id=1, source_target_pairs={{0,96},{32,64},{64,32},{96,0},{1,97},{33,65},{65,33},{97,1},{2,98}... | collective-permute-start | bytes 98312 | tf_op jit(solution)/shard_map/grad_filter/ppermute | solution.py:413
